TPU v7x, 32 devices: a whole 2x2x4 slice. The times are simulated.
32 devices in a mesh: seq: 8 (over z, x), chan: 4 (over y, core).
Axes of the slice: x: 2, y: 2, z: 4, core: 2. Of those that a mesh axis runs over, the one named last changes fastest.
Arguments:
- query_rows: bfloat16 [2048, 2048], P('seq', 'chan'), may hold values from -6 to 6
- key_rows: bfloat16 [2048, 2048], P('seq', 'chan'), may hold values from -6 to 6
- value_rows: bfloat16 [2048, 2048], P('seq', 'chan'), may hold values from -6 to 6
- long_filter: float32 [2048, 2048], P('seq', 'chan'), may hold values from -2 to 2
- short_taps: float32 [3, 3, 2048], P(None, None, ('seq', 'chan')), may hold values from -3 to 3
- skip_gain: float32 [2048], P(('seq', 'chan')), may hold values from -3 to 3
- cotangent: bfloat16 [2048, 2048], P('seq', 'chan'), may hold values from -6 to 6
Outputs:
- gated_out: bfloat16 [2048, 2048], P('seq', 'chan')
- query_grad: bfloat16 [2048, 2048], P('seq', 'chan')
- key_grad: bfloat16 [2048, 2048], P('seq', 'chan')
- value_grad: bfloat16 [2048, 2048], P('seq', 'chan')
- filter_grad: float32 [2048, 2048], P('seq', 'chan')
- taps_grad: float32 [3, 3, 2048], P(None, None, 'chan')
- skip_grad: float32 [2048], P('chan')
All inputs are finite; a program needn't handle non-finite values.
Results may differ from a plain program's by a relative error of at most 0.00135.
Values may be sent and summed in bfloat16 or wider, within the bound.
No kernel may reach another device: no remote copies, remote signals or barrier semaphores. Data moves between devices by JAX's collectives and lax.ppermute only.
A program may use at most 64 MiB of HBM per device.

v0:
```python
import math

import jax
import jax.numpy as jnp
from jax import lax
from jax.sharding import PartitionSpec as P

exact_dot = lax.Precision.HIGHEST


def from_behind(value, axis, by):
    length = lax.axis_size(axis)
    pairs = [(i, i + by) for i in range(length) if 0 <= i + by < length]
    return lax.ppermute(value, axis, pairs)


def angles(left_index, right_index, period):
    product = left_index[:, None] * right_index[None, :] % period
    return 2.0 * math.pi / period * product.astype(jnp.float32)


def source_transform(pieces, row_start, total):
    sources = pieces.shape[1]
    row_count = pieces.shape[2]
    source_index = jnp.arange(sources, dtype=jnp.int32)
    freq_index = jnp.arange(2 * sources, dtype=jnp.int32)
    theta = angles(source_index, freq_index, 2 * sources)
    real_part = jnp.einsum("fqrc,qk->fkrc", pieces, jnp.cos(theta), precision=exact_dot)
    imag_part = -jnp.einsum("fqrc,qk->fkrc", pieces, jnp.sin(theta), precision=exact_dot)
    row_index = row_start + jnp.arange(row_count, dtype=jnp.int32)
    twist = angles(freq_index, row_index, total)
    cosine = jnp.cos(twist)[None, :, :, None]
    sine = jnp.sin(twist)[None, :, :, None]
    return jnp.stack([real_part * cosine + imag_part * sine, imag_part * cosine - real_part * sine])


def row_transform(spectra, direction):
    length = spectra.shape[3]
    positions = jnp.arange(length, dtype=jnp.int32)
    theta = angles(positions, positions, length)
    cosine = jnp.cos(theta)
    sine = jnp.sin(theta)
    real_cos = jnp.einsum("femc,mk->fekc", spectra[0], cosine, precision=exact_dot)
    real_sin = jnp.einsum("femc,mk->fekc", spectra[0], sine, precision=exact_dot)
    imag_cos = jnp.einsum("femc,mk->fekc", spectra[1], cosine, precision=exact_dot)
    imag_sin = jnp.einsum("femc,mk->fekc", spectra[1], sine, precision=exact_dot)
    return jnp.stack([real_cos - direction * imag_sin, imag_cos + direction * real_sin])


def untwist(spectra, freq_start, total):
    freq_index = freq_start + jnp.arange(spectra.shape[2], dtype=jnp.int32)
    row_index = jnp.arange(spectra.shape[3], dtype=jnp.int32)
    twist = angles(freq_index, row_index, total)
    cosine = jnp.cos(twist)[None, :, :, None]
    sine = jnp.sin(twist)[None, :, :, None]
    return jnp.stack(
        [spectra[0] * cosine - spectra[1] * sine, spectra[1] * cosine + spectra[0] * sine]
    )


def source_sum(spectra, total):
    freqs = spectra.shape[2]
    theta = angles(
        jnp.arange(freqs // 2, dtype=jnp.int32), jnp.arange(freqs, dtype=jnp.int32), freqs
    )
    summed = jnp.einsum("fkrc,qk->fqrc", spectra[0], jnp.cos(theta), precision=exact_dot)
    summed = summed - jnp.einsum("fkrc,qk->fqrc", spectra[1], jnp.sin(theta), precision=exact_dot)
    return summed / total


def spectrum_split(fields):
    devices = lax.axis_size("seq")
    place = lax.axis_index("seq")
    nfields, row_count, channels = fields.shape
    share = row_count // devices
    total = 2 * devices * row_count
    mixed = source_transform(
        lax.all_to_all(
            fields.reshape(nfields, 1, row_count, channels),
            "seq",
            split_axis=2,
            concat_axis=1,
            tiled=True,
        ),
        place * share,
        total,
    )
    mixed = mixed.reshape(2, nfields, devices, 2, share, channels)
    return row_transform(
        lax.all_to_all(mixed, "seq", split_axis=2, concat_axis=4, tiled=True)[:, :, 0], -1.0
    )


def signal_split(spectra):
    devices = lax.axis_size("seq")
    place = lax.axis_index("seq")
    nfields = spectra.shape[1]
    row_count = spectra.shape[3]
    channels = spectra.shape[4]
    share = row_count // devices
    total = 2 * devices * row_count
    turned = untwist(row_transform(spectra, 1.0), 2 * place, total)
    turned = turned.reshape(2, nfields, 1, 2, devices, share, channels)
    pieces = lax.all_to_all(turned, "seq", split_axis=4, concat_axis=2, tiled=True)
    gathered = source_sum(pieces.reshape(2, nfields, 2 * devices, share, pieces.shape[6]), total)
    return lax.all_to_all(gathered, "seq", split_axis=1, concat_axis=2, tiled=True).reshape(
        nfields, row_count, channels
    )


def complex_product(left, right, conjugate):
    right_imag = -right[1] if conjugate else right[1]
    return jnp.stack(
        [left[0] * right[0] - left[1] * right_imag, left[0] * right_imag + left[1] * right[0]]
    )


def per_device(query_rows, key_rows, value_rows, long_filter, short_taps, skip_gain, cotangent):
    row_count, channels = query_rows.shape
    devices = lax.axis_size("seq")
    grad_scale = 1.0 / math.sqrt(row_count * devices)
    all_taps, all_gain = (
        lax.all_gather(short_taps, ("seq", "chan"), axis=2, tiled=True),
        lax.all_gather(skip_gain, ("seq", "chan"), axis=0, tiled=True),
    )
    start = lax.axis_index("chan") * channels
    tap_block = lax.dynamic_slice_in_dim(all_taps, start, channels, 2)
    skip_block = lax.dynamic_slice_in_dim(all_gain, start, channels, 0)
    streams = jnp.stack([query_rows, key_rows, value_rows])
    lower = from_behind(streams[:, row_count - 2 :, :], "seq", 1)
    extended = jnp.concatenate([lower, streams], axis=1).astype(jnp.float32)
    shorted = sum(
        (
            tap_block[:, offset, None, :] * extended[:, 2 - offset : 2 - offset + row_count]
            for offset in range(3)
        )
    )
    query_conv = shorted[0]
    key_conv = shorted[1]
    value_conv = shorted[2]
    product = key_conv * value_conv
    upstream = cotangent.astype(jnp.float32)
    gated_grad = upstream * query_conv
    spectra = spectrum_split(jnp.stack([product, long_filter]))
    prod_spec = spectra[:, 0]
    filt_spec = spectra[:, 1]
    conv_part = signal_split(complex_product(prod_spec, filt_spec, False)[:, None])[0]
    grad_spec = spectrum_split(gated_grad[None])[:, 0]
    back = signal_split(
        jnp.stack(
            [
                complex_product(grad_spec, filt_spec, True),
                complex_product(grad_spec, prod_spec, True),
            ],
            axis=1,
        )
    )
    corr_product = back[0]
    corr_filter = back[1]
    mixed_conv = conv_part + skip_block * product
    gated_out = (query_conv * mixed_conv).astype(jnp.bfloat16)
    query_conv_grad = upstream * mixed_conv
    product_grad = corr_product + skip_block * gated_grad
    filter_grad = grad_scale * corr_filter
    key_conv_grad = product_grad * value_conv
    value_conv_grad = product_grad * key_conv
    conv_grads = jnp.stack([query_conv_grad, key_conv_grad, value_conv_grad])
    upper = from_behind(conv_grads[:, :2, :], "seq", -1)
    ext_grads = jnp.concatenate([conv_grads, upper], axis=1)
    input_grads = sum(
        (
            tap_block[:, offset, None, :] * ext_grads[:, offset : offset + row_count]
            for offset in range(3)
        )
    ).astype(jnp.bfloat16)
    tap_terms = jnp.stack(
        [
            jnp.sum(conv_grads * extended[:, 2 - offset : 2 - offset + row_count], axis=1)
            for offset in range(3)
        ],
        axis=1,
    )
    skip_terms = jnp.sum(gated_grad * product, axis=0)
    tap_total, skip_total = lax.psum((tap_terms, skip_terms), "seq")
    return (
        gated_out,
        input_grads[0],
        input_grads[1],
        input_grads[2],
        filter_grad,
        grad_scale * tap_total,
        grad_scale * skip_total,
    )


def solution(mesh):
    in_specs = (
        P("seq", "chan"),
        P("seq", "chan"),
        P("seq", "chan"),
        P("seq", "chan"),
        P(None, None, ("seq", "chan")),
        P(("seq", "chan")),
        P("seq", "chan"),
    )
    out_specs = (
        P("seq", "chan"),
        P("seq", "chan"),
        P("seq", "chan"),
        P("seq", "chan"),
        P("seq", "chan"),
        P(None, None, "chan"),
        P("chan"),
    )
    return jax.shard_map(
        per_device, mesh=mesh, in_specs=in_specs, out_specs=out_specs, check_vma=False
    )
```

profile of v0, /device:TPU:0, one launch (start us, length us, event | category | flops | bytes accessed | tf_op | source)
XLA Modules:
  0.0 584.0 jit_solution(4823256226947450307)
XLA Ops:
  1.4 4.8 collective-permute-start
  7.1 59.3 %all_gather.6 = f32[3,3,2048]{1,0,2:T(4,128)} all-gather(f32[3,3,64]{1,0,2:T(4,128)S(1)} %copy.38), channel_id=1, replica_groups=mesh['seq'=8,'chan'=4] {'seq','chan'}, dimensions={2}, use_global_device_ids=true | all-gather | bytes 76032 | tf_op jit(solution)/shard_map/all_gather | solution.py:123
  66.4 3.3 constant_dynamic-slice_fusion.1
  73.7 4.8 all-to-all-start.4
  81.6 12.4 %all-to-all-done.4 = f32[1,1,256,512]{3,1,0,2:T(1,128)} async-done(((f32[1,1,256,512]{3,1,0,2:T(1,128)}), f32[1,1,256,512]{3,1,0,2:T(1,128)}, u32[]{:S(2)}, u32[]{:S(2)}) %all-to-all-start.4) | async-done | bytes 524320 | tf_op jit(solution)/shard_map/all_to_all | solution.py:78
  94.0 4.3 all-to-all-start
  100.7 2.8 multiply_add_fusion.1
  103.4 2.8 stack.127
  106.3 2.8 stack.126
  114.2 9.8 %all-to-all-done = f32[2,1,256,512]{3,0,1,2:T(2,128)} async-done(((f32[2,1,256,512]{3,0,1,2:T(2,128)}), f32[2,1,256,512]{3,0,1,2:T(2,128)}, u32[]{:S(2)}, u32[]{:S(2)}) %all-to-all-start) | async-done | bytes 1048608 | tf_op jit(solution)/shard_map/all_to_all | solution.py:78
  124.0 4.8 all-to-all-start.5
  132.5 4.4 add_bitcast_fusion.1
  136.9 3.4 stack.118
  140.3 3.4 stack.117
  143.8 4.4 pad_maximum_fusion
  148.1 4.3 copy.74
  152.4 24.1 %all-to-all-done.5 = f32[2,1,8,2,32,512]{5,3,4,1,0,2:T(2,128)} async-done(((f32[2,1,8,2,32,512]{5,3,4,1,0,2:T(2,128)}), f32[2,1,8,2,32,512]{5,3,4,1,0,2:T(2,128)}, u32[]{:S(2)}, u32[]{:S(2)}) %all-to-all-start.5) | async-done | bytes 2097184 | tf_op jit(solution)/shard_map/all_to_all | solution.py:90
  176.6 4.8 all-to-all-start.1
  186.2 3.0 fusion.13
  189.3 3.0 fusion.63
  192.3 81.4 %all-to-all-done.1 = f32[2,2,8,2,32,512]{5,3,4,1,0,2:T(2,128)} async-done(((f32[2,2,8,2,32,512]{5,3,4,1,0,2:T(2,128)}), f32[2,2,8,2,32,512]{5,3,4,1,0,2:T(2,128)}, u32[]{:S(2)}, u32[]{:S(2)}) %all-to-all-start.1) | async-done | bytes 4194336 | tf_op jit(solution)/shard_map/all_to_all | solution.py:90
  273.7 3.7 fusion.232
  277.8 2.9 fusion.59
  281.3 2.9 fusion.61
  284.2 3.1 add_bitcast_fusion
  287.3 3.1 subtract_bitcast_fusion
  290.4 2.6 fusion.20
  294.0 2.9 fusion.57
  296.9 2.9 fusion.35
  299.8 2.9 convolution_subtract_fusion
  302.7 3.4 fusion.3
  309.6 4.6 all-to-all-start.6
  314.2 2.7 multiply_add_fusion.3
  327.2 79.5 %all-to-all-done.6 = f32[2,2,1,2,8,32,512]{6,5,3,1,2,0,4:T(8,128)} async-done(((f32[2,2,1,2,8,32,512]{6,5,3,1,2,0,4:T(8,128)}), f32[2,2,1,2,8,32,512]{6,5,3,1,2,0,4:T(8,128)}, u32[]{:S(2)}, u32[]{:S(2)}) %all-to-all-start.6) | async-done | bytes 4194336 | tf_op jit(solution)/shard_map/all_to_all | solution.py:104
  406.7 4.6 all-to-all-start.2
  411.3 4.3 fusion.231
  415.6 2.9 copy.64
  418.5 3.6 squeeze.39
  422.2 4.5 copy.65
  426.7 3.8 squeeze.40
  430.4 2.9 fusion.105
  436.0 23.1 %all-to-all-done.2 = f32[2,1,1,2,8,32,512]{6,5,3,2,1,0,4:T(8,128)} async-done(((f32[2,1,1,2,8,32,512]{6,5,3,2,1,0,4:T(8,128)}), f32[2,1,1,2,8,32,512]{6,5,3,2,1,0,4:T(8,128)}, u32[]{:S(2)}, u32[]{:S(2)}) %all-to-all-start.2) | async-done | bytes 2097184 | tf_op jit(solution)/shard_map/all_to_all | solution.py:104
  459.1 4.2 all-to-all-start.7
  468.6 20.4 %all-to-all-done.7 = f32[2,8,32,512]{3,2,0,1:T(8,128)} async-done(((f32[2,8,32,512]{3,2,0,1:T(8,128)}), f32[2,8,32,512]{3,2,0,1:T(8,128)}, u32[]{:S(2)}, u32[]{:S(2)}) %all-to-all-start.7) | async-done | bytes 1048608 | tf_op jit(solution)/shard_map/all_to_all | solution.py:106
  489.0 4.4 all-to-all-start.3
  493.7 40.7 %all-reduce = f32[2048]{0:T(1024)S(1)} all-reduce(f32[2048]{0:T(1024)S(1)} %dynamic-update-slice), channel_id=1, replica_groups=mesh['seq'=8,'chan'=4] {'seq','chan'}, use_global_device_ids=true, to_apply=%add | all-reduce | flops 2048 | bytes 16384
  541.8 2.6 collective-permute-done.1
  546.6 35.8 %all-reduce.1 = (f32[3,3,512]{2,0,1:T(4,128)S(1)}, f32[512]{0:T(512)S(1)}) all-reduce(f32[3,3,512]{2,0,1:T(4,128)S(1)} %pad_maximum_fusion.7, f32[512]{0:T(512)S(1)} %get-tuple-element.57), channel_id=1, replica_groups=mesh['seq'=8,'chan'=4] {'seq'}, use_global_device_ids=true, to_apply=%region_3.4 | all-reduce | flops 5120 | bytes 40960 | tf_op jit(solution)/shard_map/psum | solution.py:184
  (85 shorter events, 59.2 us)
Async XLA Ops:
  1.4 69.4 %collective-permute-start = (bf16[3,2,512]{2,1,0:T(2,128)(2,1)S(1)}, bf16[3,2,512]{2,1,0:T(2,128)(2,1)S(1)}, u32[]{:S(2)}, u32[]{:S(2)}) collective-permute-start(bf16[3,2,512]{2,1,0:T(2,128)(2,1)S(1)} %pad_maximum_fusion.8), channel_id=1, source_target_pairs={{0,4},{4,8},{8,12},{12,16},{16,20},{20,24},{24,28},{1,5},{5,9},{9,... | collective-permute-start | bytes 18440 | tf_op jit(solution)/shard_map/ppermute | solution.py:14
  69.7 1.1 copy-start.7
  70.1 1.0 copy-start.8
  70.1 1.1 copy-start.9
  71.4 1.0 copy-start.10
  73.7 20.2 %all-to-all-start.4 = ((f32[1,1,256,512]{3,1,0,2:T(1,128)}), f32[1,1,256,512]{3,1,0,2:T(1,128)}, u32[]{:S(2)}, u32[]{:S(2)}) async-start(f32[1,1,256,512]{3,1,0,2:T(1,128)} %copy.55), calls=%async_computation.4 | async-start | bytes 1048576 | tf_op jit(solution)/shard_map/all_to_all | solution.py:78
  94.0 30.0 %all-to-all-start = ((f32[2,1,256,512]{3,0,1,2:T(2,128)}), f32[2,1,256,512]{3,0,1,2:T(2,128)}, u32[]{:S(2)}, u32[]{:S(2)}) async-start(f32[2,1,256,512]{3,0,1,2:T(2,128)} %copy.42), calls=%async_computation | async-start | bytes 2097152 | tf_op jit(solution)/shard_map/all_to_all | solution.py:78
  124.0 52.6 %all-to-all-start.5 = ((f32[2,1,8,2,32,512]{5,3,4,1,0,2:T(2,128)}), f32[2,1,8,2,32,512]{5,3,4,1,0,2:T(2,128)}, u32[]{:S(2)}, u32[]{:S(2)}) async-start(f32[2,1,8,2,32,512]{5,3,4,1,0,2:T(2,128)} %copy.78), calls=%async_computation.5 | async-start | bytes 4194304 | tf_op jit(solution)/shard_map/all_to_all | solution.py:90
  176.6 97.1 %all-to-all-start.1 = ((f32[2,2,8,2,32,512]{5,3,4,1,0,2:T(2,128)}), f32[2,2,8,2,32,512]{5,3,4,1,0,2:T(2,128)}, u32[]{:S(2)}, u32[]{:S(2)}) async-start(f32[2,2,8,2,32,512]{5,3,4,1,0,2:T(2,128)} %copy.74), calls=%async_computation.1 | async-start | bytes 8388608 | tf_op jit(solution)/shard_map/all_to_all | solution.py:90
  184.0 2.3 copy-start.2
  287.2 3.1 copy-start
  287.3 3.1 copy-start.3
  287.3 3.1 copy-start.5
  287.3 3.1 copy-start.6
  290.4 2.7 copy-start.1
  309.6 97.1 %all-to-all-start.6 = ((f32[2,2,1,2,8,32,512]{6,5,3,1,2,0,4:T(8,128)}), f32[2,2,1,2,8,32,512]{6,5,3,1,2,0,4:T(8,128)}, u32[]{:S(2)}, u32[]{:S(2)}) async-start(f32[2,2,1,2,8,32,512]{6,5,3,1,2,0,4:T(8,128)} %copy.79), calls=%async_computation.6 | async-start | bytes 8388608 | tf_op jit(solution)/shard_map/all_to_all | solution.py:104
  406.7 52.4 %all-to-all-start.2 = ((f32[2,1,1,2,8,32,512]{6,5,3,2,1,0,4:T(8,128)}), f32[2,1,1,2,8,32,512]{6,5,3,2,1,0,4:T(8,128)}, u32[]{:S(2)}, u32[]{:S(2)}) async-start(f32[2,1,1,2,8,32,512]{6,5,3,2,1,0,4:T(8,128)} %copy.75), calls=%async_computation.2 | async-start | bytes 4194304 | tf_op jit(solution)/shard_map/all_to_all | solution.py:104
  430.4 2.9 copy-start.4
  459.1 29.9 %all-to-all-start.7 = ((f32[2,8,32,512]{3,2,0,1:T(8,128)}), f32[2,8,32,512]{3,2,0,1:T(8,128)}, u32[]{:S(2)}, u32[]{:S(2)}) async-start(f32[2,8,32,512]{3,2,0,1:T(8,128)} %copy.66), calls=%async_computation.7 | async-start | bytes 2097152 | tf_op jit(solution)/shard_map/all_to_all | solution.py:106
  466.3 27.1 %copy-start.11 = (f32[64]{0:T(128)S(1)}, f32[64]{0:T(128)}, u32[]{:S(2)}) copy-start(f32[64]{0:T(128)} %param.12) | copy-start | bytes 772
  489.0 47.3 %all-to-all-start.3 = ((f32[1,8,32,512]{3,2,0,1:T(8,128)}), f32[1,8,32,512]{3,2,0,1:T(8,128)}, u32[]{:S(2)}, u32[]{:S(2)}) async-start(f32[1,8,32,512]{3,2,0,1:T(8,128)} %copy.54), calls=%async_computation.3 | async-start | bytes 1048576 | tf_op jit(solution)/shard_map/all_to_all | solution.py:106
  538.6 5.9 %collective-permute-start.1 = (f32[3,2,512]{2,1,0:T(2,128)S(1)}, f32[3,2,512]{2,1,0:T(2,128)S(1)}, u32[]{:S(2)}, u32[]{:S(2)}) collective-permute-start(f32[3,2,512]{2,1,0:T(2,128)S(1)} %slice.211), channel_id=1, source_target_pairs={{4,0},{8,4},{12,8},{16,12},{20,16},{24,20},{28,24},{5,1},{9,5},{13... | collective-permute-start | bytes 36872 | tf_op jit(solution)/shard_map/ppermute | solution.py:14
where the time goes:
time: 593 us; the launch traced here: 584 us
  waiting for transfers between devices  253 us (43%)
  blocking collectives  136 us (23%)
  local copies, waits for them, and re-layouts  69.7 us (12%)
  matrix products  60.2 us (10%)
  starting transfers between devices  42.6 us (7%)
  other arithmetic  20.8 us (4%)
    all_to_all x2, waiting for transfers between devices, spectrum_split(): lax.all_to_all(mixed, 'seq', split_axis=2, concat_axis=4, tiled=True)  105 us
    all_to_all x2, waiting for transfers between devices, signal_split(): lax.all_to_all(turned, 'seq', split_axis=4, concat_axis=2, tiled=True)  103 us
    all_gather x1, blocking collectives, per_device(): lax.all_gather(short_taps, ('seq', 'chan'), axis=2, tiled=True)  59.3 us
    unnamed x1, blocking collectives  40.7 us
    psum x1, blocking collectives, per_device(): tap_total, skip_total = lax.psum((tap_terms, skip_terms), 'seq')  35.8 us
    all_to_all x2, waiting for transfers between devices, spectrum_split(): lax.all_to_all(fields.reshape(nfields, 1, row_count, channels), 'seq', sp...  22.3 us
    all_to_all x2, waiting for transfers between devices, signal_split(): lax.all_to_all(gathered, 'seq', split_axis=1, concat_axis=2, tiled=True)  20.4 us
    another operation x6, local copies, waits for them, and re-layouts, source_transform(): jnp.stack([real_part * cosine + imag_part * sine, imag_part * cosine - re...  19.3 us
  transfers between devices with their start and end apart: 10, of which 8 were waited for; matrix products, arithmetic and copies ran while one was open for 18% of the time, Pallas kernels for 0%

commit v1 on v0

v1 whole, which is shorter than its diff:
```python
import math

import jax
import jax.numpy as jnp
import numpy as np
from jax import lax
from jax.experimental import pallas as pl
from jax.experimental.pallas import tpu as pltpu
from jax.sharding import PartitionSpec as P

HALF = 64
LANES = 2 * HALF
SUMS = 16
VMEM_BYTES = 62 * 1024 * 1024


def swap(value):
    return pltpu.roll(value, HALF, 1)


def left_lanes(shape):
    return lax.broadcasted_iota(jnp.int32, shape, 1) < HALF


def head_tail(value):
    head = value.astype(jnp.bfloat16)
    tail = (value - head.astype(jnp.float32)).astype(jnp.bfloat16)
    return head, tail


def transform_matrices(rows):
    freq = np.concatenate([np.arange(0, rows, 2), np.arange(1, rows, 2)])
    turn = (2 * freq[:, None] + 1) * np.arange(rows)[None, :] % (4 * rows)
    theta = turn * (math.pi / (2 * rows))
    forward = np.concatenate([np.cos(theta), -np.sin(theta)])
    inverse = forward.T / rows

    def split(matrix):
        single = matrix.astype(np.float32)
        head = single.astype(jnp.bfloat16)
        tail = (single - head.astype(np.float32)).astype(jnp.bfloat16)
        return np.concatenate([head, head, tail], axis=1)

    return split(forward), split(inverse)


def pack_kernel(query_ref, key_ref, value_ref, cot_ref, filter_ref, out_ref):
    rows, channels = query_ref.shape
    left = left_lanes((rows, LANES))
    for tile in range(channels // LANES):
        at = pl.ds(tile * LANES, LANES)
        for first, second, place in ((query_ref, key_ref, 0), (cot_ref, value_ref, 1)):
            one = first[:, at].astype(jnp.float32)
            two = second[:, at].astype(jnp.float32)
            here = pl.ds(place * rows, rows)
            out_ref[2 * tile, here, :] = jnp.where(left, one, swap(two)).astype(jnp.bfloat16)
            out_ref[2 * tile + 1, here, :] = jnp.where(left, swap(one), two).astype(jnp.bfloat16)
        head, tail = head_tail(filter_ref[:, at])
        head, tail = head.astype(jnp.float32), tail.astype(jnp.float32)
        here = pl.ds(2 * rows, rows)
        out_ref[2 * tile, here, :] = jnp.where(left, head, swap(tail)).astype(jnp.bfloat16)
        out_ref[2 * tile + 1, here, :] = jnp.where(left, swap(head), tail).astype(jnp.bfloat16)


def pack(query_rows, key_rows, value_rows, cotangent, long_filter, devices):
    rows, channels = query_rows.shape
    if channels == devices * HALF:
        return pl.pallas_call(
            pack_kernel,
            out_shape=jax.ShapeDtypeStruct((devices, 3 * rows, LANES), jnp.bfloat16),
            compiler_params=pltpu.CompilerParams(vmem_limit_bytes=VMEM_BYTES),
        )(query_rows, key_rows, value_rows, cotangent, long_filter)
    head, tail = head_tail(long_filter)
    share = channels // devices

    def lay(value):
        pieces = value.reshape(rows, devices, share).transpose(1, 0, 2)
        return jnp.pad(pieces, ((0, 0), (0, 0), (0, HALF - share)))

    pairs = ((query_rows, key_rows), (cotangent, value_rows), (head, tail))
    return jnp.concatenate([jnp.concatenate([lay(a), lay(b)], axis=2) for a, b in pairs], axis=1)


def unpack_kernel(in_ref, gated_ref, query_ref, key_ref, value_ref, filter_ref, sums_ref):
    rows, channels = gated_ref.shape
    left = left_lanes((rows, LANES))
    left_sums = left_lanes((SUMS // 2, LANES))
    for tile in range(channels // LANES):
        at = pl.ds(tile * LANES, LANES)
        for first, second, place in ((query_ref, key_ref, 0), (gated_ref, value_ref, 1)):
            here = pl.ds(place * rows, rows)
            one = in_ref[2 * tile, here, :].astype(jnp.float32)
            two = in_ref[2 * tile + 1, here, :].astype(jnp.float32)
            first[:, at] = jnp.where(left, one, swap(two)).astype(jnp.bfloat16)
            second[:, at] = jnp.where(left, swap(one), two).astype(jnp.bfloat16)
        here = pl.ds(2 * rows, rows)
        one = in_ref[2 * tile, here, :].astype(jnp.float32)
        two = in_ref[2 * tile + 1, here, :].astype(jnp.float32)
        filter_ref[:, at] = jnp.where(left, one + swap(one), two + swap(two))
        sums = []
        for source in (2 * tile, 2 * tile + 1):
            pair = in_ref[source, pl.ds(3 * rows, SUMS), :].astype(jnp.float32)
            sums.append(pair[: SUMS // 2] + pair[SUMS // 2 :])
        sums_ref[0, :, at] = jnp.where(left_sums, sums[0], swap(sums[1]))
        sums_ref[1, :, at] = jnp.where(left_sums, swap(sums[0]), sums[1])


def unpack(received, rows, channels):
    devices = received.shape[0]
    low = jax.ShapeDtypeStruct((rows, channels), jnp.bfloat16)
    if channels == devices * HALF:
        return pl.pallas_call(
            unpack_kernel,
            out_shape=(
                low,
                low,
                low,
                low,
                jax.ShapeDtypeStruct((rows, channels), jnp.float32),
                jax.ShapeDtypeStruct((2, SUMS // 2, channels), jnp.float32),
            ),
            compiler_params=pltpu.CompilerParams(vmem_limit_bytes=VMEM_BYTES),
        )(received)
    share = channels // devices

    def lay(start, count, side):
        piece = received[:, start : start + count, side * HALF : side * HALF + share]
        return piece.transpose(1, 0, 2).reshape(count, channels)

    def whole(start, count, side):
        return lay(start, count, side).astype(jnp.float32)

    sums = [
        whole(3 * rows, SUMS // 2, side) + whole(3 * rows + SUMS // 2, SUMS // 2, side)
        for side in (0, 1)
    ]
    return (
        lay(rows, rows, 0),
        lay(0, rows, 0),
        lay(0, rows, 1),
        lay(rows, rows, 1),
        whole(2 * rows, rows, 0) + whole(2 * rows, rows, 1),
        jnp.stack(sums),
    )


def operator_kernel(
    forward_ref, inverse_ref, taps_ref, in_ref, out_ref,
    behind, ahead, first_ref, second_ref, fields, spectra, filters, rhs, rhs_back, sums_ref,
):
    blocks = in_ref.shape[0]
    rows = in_ref.shape[1] // 3
    half = blocks // 2
    grad_scale = 1.0 / math.sqrt(blocks * rows)
    left = left_lanes((rows, LANES))
    taps = taps_ref[...]
    query_taps = [taps[i : i + 1] for i in range(3)]
    value_taps = [taps[3 + i : 4 + i] for i in range(3)]
    gain = taps[6:7]

    def short(block, carry):
        outs, ends = [], []
        for place, weights, before in ((0, query_taps, carry[0]), (1, value_taps, carry[1])):
            now = in_ref[block, pl.ds(place * rows, rows), :].astype(jnp.float32)
            behind[place, pl.ds(0, 8), :] = before
            behind[place, pl.ds(8, rows), :] = now
            total = weights[0] * now
            for offset in (1, 2):
                total = total + weights[offset] * behind[place, pl.ds(8 - offset, rows), :]
            outs.append(total)
            ends.append(now[rows - 8 :])
        first_ref[block] = outs[0]
        second_ref[block] = outs[1]
        fields[block] = outs[0] * outs[1]
        return tuple(ends)

    nothing = jnp.zeros((8, LANES), jnp.float32)
    lax.fori_loop(0, blocks, short, (nothing, nothing))

    def transform(pair, _):
        for side in range(2):
            block = 2 * pair + side
            field = jnp.where(left, fields[blocks - 1 - block], fields[block])
            head, tail = head_tail(field)
            at = pl.ds(side * LANES, LANES)
            rhs[pl.ds(0, rows), at] = head
            rhs[pl.ds(rows, rows), at] = tail
            rhs[pl.ds(2 * rows, rows), at] = head
        result = jnp.dot(forward_ref[...], rhs[...], preferred_element_type=jnp.float32)
        for side in range(2):
            spectra[2 * pair + side] = result[:, side * LANES : (side + 1) * LANES]
        for side in range(2):
            both = in_ref[2 * pair + side, pl.ds(2 * rows, rows), :]
            wide = both.astype(jnp.float32)
            turned = swap(wide)
            at = pl.ds(side * LANES, LANES)
            rhs[pl.ds(0, rows), at] = both
            rhs[pl.ds(rows, rows), at] = turned.astype(jnp.bfloat16)
            rhs[pl.ds(2 * rows, rows), at] = jnp.where(left, wide, turned).astype(jnp.bfloat16)
        result = jnp.dot(forward_ref[...], rhs[...], preferred_element_type=jnp.float32)
        for side in range(2):
            filters[2 * pair + side] = result[:, side * LANES : (side + 1) * LANES]
        return 0

    lax.fori_loop(0, half, transform, 0)

    chunk = 8
    left_chunk = left_lanes((chunk, LANES))
    conjugate = jnp.where(left_chunk, -1.0, 1.0)

    def spectral(step, sign):
        real_at = pl.ds(pl.multiple_of(step * chunk, chunk), chunk)
        imag_at = pl.ds(pl.multiple_of(rows + step * chunk, chunk), chunk)
        field_re = [spectra[block, real_at, :] for block in range(blocks)]
        field_im = [spectra[block, imag_at, :] for block in range(blocks)]

        def joined(re, im, block):
            if block == 0:
                return re[0], im[0]
            if sign > 0:
                return re[block] - im[block - 1], im[block] + re[block - 1]
            return re[block] + im[block - 1], im[block] - re[block - 1]

        filt_re = [filters[block, real_at, :] for block in range(blocks)]
        filt_im = [filters[block, imag_at, :] for block in range(blocks)]
        joins = [joined(filt_re, filt_im, block) for block in range(blocks)]
        joins = [(re, im * conjugate) for re, im in joins]
        for block in range(blocks):
            out_re = out_im = None
            for lag in range(block + 1):
                re, im = field_re[block - lag], field_im[block - lag]
                join_re, join_im = joins[lag]
                term_re = re * join_re - im * join_im
                term_im = re * join_im + im * join_re
                out_re = term_re if out_re is None else out_re + term_re
                out_im = term_im if out_im is None else out_im + term_im
            spectra[block, real_at, :] = out_re
            spectra[block, imag_at, :] = out_im
        grads = []
        for block in range(blocks):
            re, im = field_re[blocks - 1 - block], field_im[blocks - 1 - block]
            grads.append(
                (jnp.where(left_chunk, re, swap(re)), jnp.where(left_chunk, im, swap(im)))
            )
        joins = [joined(field_re, field_im, block) for block in range(blocks)]
        products = []
        for block in range(blocks):
            parts = []
            for part in range(2):
                far = joins[block - half][part] if block >= half else 0.0
                parts.append(jnp.where(left_chunk, swap(joins[block][part]), far))
            products.append(parts)
        for lag in range(half):
            out_re = out_im = None
            for block in range(lag, blocks):
                re, im = grads[block]
                join_re, join_im = products[block - lag]
                term_re = re * join_re + im * join_im
                term_im = im * join_re - re * join_im
                out_re = term_re if out_re is None else out_re + term_re
                out_im = term_im if out_im is None else out_im + term_im
            filters[lag, real_at, :] = out_re
            filters[lag, imag_at, :] = out_im

    def even(step, _):
        spectral(step, 1)
        return 0

    def odd(step, _):
        spectral(step, -1)
        return 0

    steps = rows // chunk
    lax.fori_loop(0, steps // 2, even, 0)
    lax.fori_loop(steps // 2, steps, odd, 0)

    def back(source, pair):
        for side in range(2):
            head, tail = head_tail(source[2 * pair + side])
            at = pl.ds(side * LANES, LANES)
            rhs_back[pl.ds(0, 2 * rows), at] = head
            rhs_back[pl.ds(2 * rows, 2 * rows), at] = tail
            rhs_back[pl.ds(4 * rows, 2 * rows), at] = head
        return jnp.dot(inverse_ref[...], rhs_back[...], preferred_element_type=jnp.float32)

    def mixed(pair, _):
        result = back(spectra, pair)
        for side in range(2):
            spectra[2 * pair + side, pl.ds(0, rows), :] = result[
                :, side * LANES : (side + 1) * LANES
            ]
        return 0

    lax.fori_loop(0, half, mixed, 0)

    def filter_grads(pair, _):
        result = back(filters, pair) * grad_scale
        for side in range(2):
            value = result[:, side * LANES : (side + 1) * LANES]
            head, tail = head_tail(value)
            head, tail = head.astype(jnp.float32), tail.astype(jnp.float32)
            near = 2 * pair + side
            here = pl.ds(2 * rows, rows)
            out_ref[near, here, :] = jnp.where(left, head, swap(tail)).astype(jnp.bfloat16)
            out_ref[near + half, here, :] = jnp.where(left, swap(head), tail).astype(jnp.bfloat16)
        return 0

    lax.fori_loop(0, half // 2, filter_grads, 0)

    def fold(value):
        return jnp.sum(value.reshape(rows // 8, 8, LANES), axis=0)

    def outputs(step, carry):
        block = blocks - 1 - step
        starts, totals = carry[:2], carry[2:]
        field = fields[block]
        result = jnp.where(
            left,
            spectra[blocks - 1 - block, pl.ds(0, rows), :],
            spectra[block, pl.ds(0, rows), :],
        )
        turned = swap(result + gain * field)
        grads = (second_ref[block] * turned, first_ref[block] * turned)
        new_totals = []
        for place, weights in ((0, query_taps), (1, value_taps)):
            grad = grads[place]
            ahead[place, pl.ds(0, rows), :] = grad
            ahead[place, pl.ds(rows, 8), :] = starts[place]
            here = pl.ds(place * rows, rows)
            stream = in_ref[block, here, :].astype(jnp.float32)
            total = weights[0] * grad
            new_totals.append(totals[3 * place] + fold(grad * stream))
            for offset in (1, 2):
                later = ahead[place, pl.ds(offset, rows), :]
                total = total + weights[offset] * later
                new_totals.append(totals[3 * place + offset] + fold(later * stream))
            out_ref[block, here, :] = total.astype(jnp.bfloat16)
        new_totals.append(totals[6] + fold(field * swap(field)))
        return (grads[0][:8], grads[1][:8], *new_totals)

    totals = lax.fori_loop(0, blocks, outputs, (nothing,) * 9)[2:]
    sums_ref[...] = jnp.zeros((8, LANES), jnp.float32)
    for row, total in enumerate(totals):
        sums_ref[row : row + 1, :] = grad_scale * jnp.sum(total, axis=0, keepdims=True)
    head, tail = head_tail(sums_ref[...])
    both = jnp.concatenate([head.astype(jnp.float32), tail.astype(jnp.float32)], axis=0)
    for block in range(blocks):
        out_ref[block, pl.ds(3 * rows, SUMS), :] = both.astype(jnp.bfloat16)


def operator(taps, streams):
    blocks = streams.shape[0]
    rows = streams.shape[1] // 3
    forward, inverse = transform_matrices(rows)
    wide = (blocks, rows, LANES)
    return pl.pallas_call(
        operator_kernel,
        out_shape=jax.ShapeDtypeStruct((blocks, 3 * rows + SUMS, LANES), jnp.bfloat16),
        scratch_shapes=[
            pltpu.VMEM((2, rows + 8, LANES), jnp.float32),
            pltpu.VMEM((2, rows + 8, LANES), jnp.float32),
            pltpu.VMEM(wide, jnp.float32),
            pltpu.VMEM(wide, jnp.float32),
            pltpu.VMEM(wide, jnp.float32),
            pltpu.VMEM((blocks, 2 * rows, LANES), jnp.float32),
            pltpu.VMEM((blocks, 2 * rows, LANES), jnp.float32),
            pltpu.VMEM((3 * rows, 2 * LANES), jnp.bfloat16),
            pltpu.VMEM((6 * rows, 2 * LANES), jnp.bfloat16),
            pltpu.VMEM((8, LANES), jnp.float32),
        ],
        compiler_params=pltpu.CompilerParams(vmem_limit_bytes=VMEM_BYTES),
    )(jnp.asarray(forward), jnp.asarray(inverse), taps, streams)


def own_taps(short_taps, skip_gain):
    places = lax.axis_size("seq")
    columns = lax.axis_size("chan")
    share = skip_gain.shape[0]

    def pair(one, two):
        fill = ((0, 0), (0, HALF - share))
        return jnp.concatenate([jnp.pad(one, fill), jnp.pad(two, fill)], axis=1)

    straight = jnp.concatenate([jnp.ones((1, share)), jnp.zeros((2, share))]).astype(jnp.float32)
    rows = jnp.concatenate(
        [
            pair(short_taps[0], short_taps[1]),
            pair(straight, short_taps[2]),
            pair(skip_gain[None], skip_gain[None]),
            jnp.zeros((1, LANES), jnp.float32),
        ]
    )
    route = [
        (flat, (flat % places) * columns + flat // places) for flat in range(places * columns)
    ]
    return lax.ppermute(rows, ("seq", "chan"), route)


def per_device(query_rows, key_rows, value_rows, long_filter, short_taps, skip_gain, cotangent):
    rows, channels = query_rows.shape
    devices = lax.axis_size("seq")
    taps = own_taps(short_taps, skip_gain)
    sent = pack(query_rows, key_rows, value_rows, cotangent, long_filter, devices)
    streams = lax.all_to_all(sent, "seq", 0, 0, tiled=True)
    results = lax.all_to_all(operator(taps, streams), "seq", 0, 0, tiled=True)
    gated, query_grad, key_grad, value_grad, filter_grad, sums = unpack(results, rows, channels)
    taps_grad = jnp.stack([sums[0, 0:3], sums[1, 0:3], sums[1, 3:6]])
    return gated, query_grad, key_grad, value_grad, filter_grad, taps_grad, sums[0, 6]


def solution(mesh):
    in_specs = (
        P("seq", "chan"),
        P("seq", "chan"),
        P("seq", "chan"),
        P("seq", "chan"),
        P(None, None, ("seq", "chan")),
        P(("seq", "chan")),
        P("seq", "chan"),
    )
    out_specs = (
        P("seq", "chan"),
        P("seq", "chan"),
        P("seq", "chan"),
        P("seq", "chan"),
        P("seq", "chan"),
        P(None, None, "chan"),
        P("chan"),
    )
    return jax.shard_map(
        per_device, mesh=mesh, in_specs=in_specs, out_specs=out_specs, check_vma=False
    )
```

time: 593 us -> 115 us (0.19); the launches traced: 584 us -> 114 us
  waiting for transfers between devices: 253 us -> 36.3 us
  blocking collectives: 136 us -> 43.8 us
  local copies, waits for them, and re-layouts: 69.7 us -> 4.02 us
  matrix products: 60.2 us -> 0 us
  starting transfers between devices: 42.6 us -> 8.04 us
  Pallas kernels: 0 us -> 20.9 us
  other arithmetic: 20.8 us -> 0.7 us
    all_to_all x8 -> x1, waiting for transfers between devices: 251 us -> 36.3 us  [per_device(): streams = lax.all_to_all(sent, 'seq', 0, 0, tiled=True)]
    dot_general x24 -> x0, matrix products: 60.2 us -> none  [the longest x4 11.5 us: row_transform(): jnp.einsum('femc,mk->fekc', spectra[0], sine, precision=exact_dot)]
    all_gather x1 -> x0, blocking collectives: 59.3 us -> none  [per_device(): lax.all_gather(short_taps, ('seq', 'chan'), axis=2, tiled=True)]
    all_to_all x0 -> x1, blocking collectives: none -> 43.8 us  [per_device(): results = lax.all_to_all(operator(taps, streams), 'seq', 0, 0, tiled=True)]
    unnamed x1 -> x0, blocking collectives: 40.7 us -> none
    psum x1 -> x0, blocking collectives: 35.8 us -> none  [per_device(): tap_total, skip_total = lax.psum((tap_terms, skip_terms), 'seq')]
    all_to_all x8 -> x1, starting transfers between devices: 36.5 us -> 7.39 us  [per_device(): streams = lax.all_to_all(sent, 'seq', 0, 0, tiled=True)]
    another operation x9 -> x0, local copies, waits for them, and re-layouts: 24.7 us -> none  [the longest x6 19.3 us: source_transform(): jnp.stack([real_part * cosine + imag_part * sine, imag_part * cosine - re...]
  transfers between devices with their start and end apart: 10 -> 2, of which waited for: 8 -> 1; matrix products, arithmetic and copies ran while one was open for 18% -> 0% of each run, Pallas kernels for 0% -> 0%
where the time goes in v1:
time: 115 us; the launch traced here: 114 us
  blocking collectives  43.8 us (38%)
  waiting for transfers between devices  36.3 us (32%)
  Pallas kernels  20.9 us (18%)
  starting transfers between devices  8.04 us (7%)
  local copies, waits for them, and re-layouts  4.02 us (3%)
    all_to_all x1, blocking collectives, per_device(): results = lax.all_to_all(operator(taps, streams), 'seq', 0, 0, tiled=True)  43.8 us
    all_to_all x1, waiting for transfers between devices, per_device(): streams = lax.all_to_all(sent, 'seq', 0, 0, tiled=True)  36.3 us
    pallas_call x1, Pallas kernels, operator(): pl.pallas_call(operator_kernel, out_shape=jax.ShapeDtypeStruct((blocks, 3...  14.7 us
    all_to_all x1, starting transfers between devices, per_device(): streams = lax.all_to_all(sent, 'seq', 0, 0, tiled=True)  7.39 us
    pallas_call x1, Pallas kernels, pack(): pl.pallas_call(pack_kernel, out_shape=jax.ShapeDtypeStruct((devices, 3 *...  3.09 us
    pallas_call x1, Pallas kernels, unpack(): pl.pallas_call(unpack_kernel, out_shape=(low, low, low, low, jax.ShapeDty...  3.07 us
  transfers between devices with their start and end apart: 2, of which 1 were waited for; matrix products, arithmetic and copies ran while one was open for 0% of the time, Pallas kernels for 0%

profile of v1, /device:TPU:0, one launch (start us, length us, event | category | flops | bytes accessed | tf_op | source)
XLA Modules:
  0.0 114.4 jit_solution(13384639235249508737)
XLA Ops:
  0.6 3.1 %shard_map.144 = bf16[8,768,128]{2,1,0:T(8,128)(2,1)} custom-call(bf16[256,512]{1,0:T(8,128)(2,1)} %query_ref.1, bf16[256,512]{1,0:T(8,128)(2,1)} %key_ref.1, bf16[256,512]{1,0:T(8,128)(2,1)} %value_ref.1, bf16[256,512]{1,0:T(8,128)(2,1)} %cot_ref.1, f32[256,512]{1,0:T(8,128)} %filter_ref.1), custom_call_target="tpu_custom_call" | custom-call | tf_op jit(solution)/shard_map/pallas_call | solution.py:68
  3.7 0.0 copy-start.1
  3.7 0.0 copy-start.3
  3.7 0.0 copy-start.4
  3.7 7.4 %all-to-all-start = ((bf16[8,768,128]{2,1,0:T(8,128)(2,1)}), bf16[8,768,128]{2,1,0:T(8,128)(2,1)S(1)}, u32[]{:S(2)}, u32[]{:S(2)}) async-start(bf16[8,768,128]{2,1,0:T(8,128)(2,1)} %shard_map.144), calls=%async_computation | async-start | bytes 3145728 | tf_op jit(solution)/shard_map/all_to_all | solution.py:404
  11.1 0.1 pad.8.clone
  11.2 0.0 copy-done.1
  11.2 0.0 copy-done.3
  11.2 0.0 copy-done.4
  11.2 0.1 maximum_maximum_fusion
  11.3 0.7 collective-permute-start
  12.0 0.0 collective-permute-done.taps_ref
  12.0 0.0 copy-start.2
  12.0 36.3 %all-to-all-done.in_ref = bf16[8,768,128]{2,1,0:T(8,128)(2,1)S(1)} async-done(((bf16[8,768,128]{2,1,0:T(8,128)(2,1)}), bf16[8,768,128]{2,1,0:T(8,128)(2,1)S(1)}, u32[]{:S(2)}, u32[]{:S(2)}) %all-to-all-start) | async-done | bytes 1572896 | tf_op jit(solution)/shard_map/all_to_all | solution.py:404
  48.3 0.0 copy-done.2
  48.3 0.0 copy-start
  48.3 1.2 %copy-done = bf16[8,768,128]{2,1,0:T(8,128)(2,1)} copy-done((bf16[8,768,128]{2,1,0:T(8,128)(2,1)}, bf16[8,768,128]{2,1,0:T(8,128)(2,1)S(1)}, u32[]{:S(2)}) %copy-start) | copy-done | bytes 1572888
  49.4 14.7 %shard_map.145 = bf16[8,784,128]{2,1,0:T(8,128)(2,1)} custom-call(bf16[512,768]{1,0:T(8,128)(2,1)} %constant.3.clone.forward_ref, bf16[256,1536]{1,0:T(8,128)(2,1)} %constant.10.clone.inverse_ref, f32[8,128]{1,0:T(8,128)} %copy-done.2, bf16[8,768,128]{2,1,0:T(8,128)(2,1)} %copy-done), custom_call_target="tpu_custom_call" | custom-call | tf_op jit(solution)/shard_map/pallas_call | solution.py:356
  64.1 43.8 %all_to_all.10.in_ref = bf16[8,784,128]{2,1,0:T(8,128)(2,1)} all-to-all(bf16[8,784,128]{2,1,0:T(8,128)(2,1)} %shard_map.145), channel_id=1, replica_groups=mesh['seq'=8,'chan'=4] {'seq'}, dimensions={0} | all-to-all | bytes 3211264 | tf_op jit(solution)/shard_map/all_to_all | solution.py:405
  107.9 3.1 %shard_map.146 = (bf16[256,512]{1,0:T(8,128)(2,1)}, bf16[256,512]{1,0:T(8,128)(2,1)}, bf16[256,512]{1,0:T(8,128)(2,1)}, bf16[256,512]{1,0:T(8,128)(2,1)}, f32[256,512]{1,0:T(8,128)}, /*index=5*/f32[2,8,512]{2,1,0:T(8,128)}) custom-call(bf16[8,784,128]{2,1,0:T(8,128)(2,1)} %all_to_all.10.in_ref), custom_call_target="tpu_custom_call" | custom-call | tf_op jit(solution)/shard_map/pallas_call | solution.py:112
  111.0 1.3 %slice.25 = f32[1,1,512]{2,1,0:T(1,128)} slice(f32[2,8,512]{2,1,0:T(8,128)} %get-tuple-element.18), slice={[0:1], [6:7], [0:512]} | slice | bytes 4096 | tf_op jit(solution)/shard_map/slice | solution.py:408
  112.3 0.7 slice.24
  113.0 0.8 slice.23
  113.8 0.6 pad_maximum_fusion
  (1 shorter events, 0.0 us)
Async XLA Ops:
  3.7 7.5 %copy-start.1 = (f32[3,3,64]{2,1,0:T(4,128)S(1)}, f32[3,3,64]{2,1,0:T(4,128)}, u32[]{:S(2)}) copy-start(f32[3,3,64]{2,1,0:T(4,128)} %param.13) | copy-start | bytes 6916
  3.7 7.5 %copy-start.3 = (f32[3,64]{1,0:T(4,128)S(1)}, f32[3,64]{1,0:T(4,128)}, u32[]{:S(2)}) copy-start(f32[3,64]{1,0:T(4,128)} %constant.4.clone.1) | copy-start | bytes 2308
  3.7 7.5 %copy-start.4 = (f32[64]{0:T(128)S(1)}, f32[64]{0:T(128)}, u32[]{:S(2)}) copy-start(f32[64]{0:T(128)} %param.14) | copy-start | bytes 772
  3.7 44.5 %all-to-all-start = ((bf16[8,768,128]{2,1,0:T(8,128)(2,1)}), bf16[8,768,128]{2,1,0:T(8,128)(2,1)S(1)}, u32[]{:S(2)}, u32[]{:S(2)}) async-start(bf16[8,768,128]{2,1,0:T(8,128)(2,1)} %shard_map.144), calls=%async_computation | async-start | bytes 3145728 | tf_op jit(solution)/shard_map/all_to_all | solution.py:404
  11.3 0.7 collective-permute-start
  12.0 36.3 %copy-start.2 = (f32[8,128]{1,0:T(8,128)}, f32[8,128]{1,0:T(8,128)S(1)}, u32[]{:S(2)}) copy-start(f32[8,128]{1,0:T(8,128)S(1)} %collective-permute-done.taps_ref) | copy-start | bytes 12292
  48.3 1.2 %copy-start = (bf16[8,768,128]{2,1,0:T(8,128)(2,1)}, bf16[8,768,128]{2,1,0:T(8,128)(2,1)S(1)}, u32[]{:S(2)}) copy-start(bf16[8,768,128]{2,1,0:T(8,128)(2,1)S(1)} %all-to-all-done.in_ref) | copy-start | bytes 4718596

commit v2 on v1

--- a/solution.py
+++ b/solution.py
@@ -10,7 +10,10 @@
 
 HALF = 64
 LANES = 2 * HALF
-SUMS = 16
+EDGE = 16
+MISC = 24
+SPAN = 252.0
+FLOOR = 125.0
 VMEM_BYTES = 62 * 1024 * 1024
 
 
@@ -44,9 +47,28 @@
     return split(forward), split(inverse)
 
 
-def pack_kernel(query_ref, key_ref, value_ref, cot_ref, filter_ref, out_ref):
+def encode(value, scale):
+    code = jnp.exp2(jnp.abs(value) * (SPAN / scale) - FLOOR)
+    return jnp.where(value < 0.0, -code, code)
+
+
+def decode(code, scale):
+    size = (jnp.log2(jnp.abs(code)) + FLOOR) * (scale * (1.0 / SPAN))
+    return jnp.where(code < 0.0, -size, size)
+
+
+def scale_of(value):
+    peak = jnp.max(jnp.abs(value), axis=0, keepdims=True)
+    return jnp.maximum(peak * 1.0001, 1e-30)
+
+
+def pack_kernel(
+    query_ref, key_ref, value_ref, cot_ref, filter_ref, out_ref, last_ref, first_ref
+):
     rows, channels = query_ref.shape
+    half = rows // 2
     left = left_lanes((rows, LANES))
+    left_half = left_lanes((half, LANES))
     for tile in range(channels // LANES):
         at = pl.ds(tile * LANES, LANES)
         for first, second, place in ((query_ref, key_ref, 0), (cot_ref, value_ref, 1)):
@@ -55,104 +77,139 @@
             here = pl.ds(place * rows, rows)
             out_ref[2 * tile, here, :] = jnp.where(left, one, swap(two)).astype(jnp.bfloat16)
             out_ref[2 * tile + 1, here, :] = jnp.where(left, swap(one), two).astype(jnp.bfloat16)
-        head, tail = head_tail(filter_ref[:, at])
-        head, tail = head.astype(jnp.float32), tail.astype(jnp.float32)
-        here = pl.ds(2 * rows, rows)
-        out_ref[2 * tile, here, :] = jnp.where(left, head, swap(tail)).astype(jnp.bfloat16)
-        out_ref[2 * tile + 1, here, :] = jnp.where(left, swap(head), tail).astype(jnp.bfloat16)
-
-
-def pack(query_rows, key_rows, value_rows, cotangent, long_filter, devices):
-    rows, channels = query_rows.shape
-    if channels == devices * HALF:
-        return pl.pallas_call(
-            pack_kernel,
-            out_shape=jax.ShapeDtypeStruct((devices, 3 * rows, LANES), jnp.bfloat16),
-            compiler_params=pltpu.CompilerParams(vmem_limit_bytes=VMEM_BYTES),
-        )(query_rows, key_rows, value_rows, cotangent, long_filter)
-    head, tail = head_tail(long_filter)
-    share = channels // devices
-
-    def lay(value):
-        pieces = value.reshape(rows, devices, share).transpose(1, 0, 2)
-        return jnp.pad(pieces, ((0, 0), (0, 0), (0, HALF - share)))
-
-    pairs = ((query_rows, key_rows), (cotangent, value_rows), (head, tail))
-    return jnp.concatenate([jnp.concatenate([lay(a), lay(b)], axis=2) for a, b in pairs], axis=1)
-
-
-def unpack_kernel(in_ref, gated_ref, query_ref, key_ref, value_ref, filter_ref, sums_ref):
-    rows, channels = gated_ref.shape
+        upper = filter_ref[pl.ds(0, half), at]
+        lower = filter_ref[pl.ds(half, half), at]
+        for dest, pair in (
+            (2 * tile, jnp.where(left_half, upper, swap(lower))),
+            (2 * tile + 1, jnp.where(left_half, swap(upper), lower)),
+        ):
+            scale = scale_of(pair)
+            out_ref[dest, pl.ds(2 * rows, half), :] = encode(pair, scale).astype(jnp.bfloat16)
+            head, tail = head_tail(jnp.broadcast_to(scale, (8, LANES)))
+            both = jnp.concatenate([head.astype(jnp.float32), tail.astype(jnp.float32)], axis=0)
+            out_ref[dest, pl.ds(2 * rows + half, 16), :] = both.astype(jnp.bfloat16)
+    for stream, source in enumerate((query_ref, key_ref, value_ref, cot_ref)):
+        first_ref[stream] = source[pl.ds(0, EDGE), :]
+        if stream < 3:
+            last_ref[stream] = source[pl.ds(rows - EDGE, EDGE), :]
+
+
+def pack(streams, cotangent, long_filter, devices):
+    rows, channels = cotangent.shape
+    return pl.pallas_call(
+        pack_kernel,
+        out_shape=(
+            jax.ShapeDtypeStruct((devices, 2 * rows + rows // 2 + 16, LANES), jnp.bfloat16),
+            jax.ShapeDtypeStruct((3, EDGE, channels), jnp.bfloat16),
+            jax.ShapeDtypeStruct((4, EDGE, channels), jnp.bfloat16),
+        ),
+        compiler_params=pltpu.CompilerParams(vmem_limit_bytes=VMEM_BYTES),
+    )(*streams, cotangent, long_filter)
+
+
+def finish_kernel(
+    in_ref, query_ref, key_ref, value_ref, cot_ref, last_ref, first_ref,
+    gated_out, query_out, key_out, value_out, filter_out, taps_out, skip_out,
+    before, after,
+):
+    rows, channels = query_ref.shape
+    half = rows // 2
     left = left_lanes((rows, LANES))
-    left_sums = left_lanes((SUMS // 2, LANES))
+    left_half = left_lanes((half, LANES))
+    left_misc = left_lanes((MISC, LANES))
     for tile in range(channels // LANES):
         at = pl.ds(tile * LANES, LANES)
-        for first, second, place in ((query_ref, key_ref, 0), (gated_ref, value_ref, 1)):
-            here = pl.ds(place * rows, rows)
-            one = in_ref[2 * tile, here, :].astype(jnp.float32)
-            two = in_ref[2 * tile + 1, here, :].astype(jnp.float32)
-            first[:, at] = jnp.where(left, one, swap(two)).astype(jnp.bfloat16)
-            second[:, at] = jnp.where(left, swap(one), two).astype(jnp.bfloat16)
-        here = pl.ds(2 * rows, rows)
-        one = in_ref[2 * tile, here, :].astype(jnp.float32)
-        two = in_ref[2 * tile + 1, here, :].astype(jnp.float32)
-        filter_ref[:, at] = jnp.where(left, one + swap(one), two + swap(two))
-        sums = []
+        miscs, results, grads = [], [], []
         for source in (2 * tile, 2 * tile + 1):
-            pair = in_ref[source, pl.ds(3 * rows, SUMS), :].astype(jnp.float32)
-            sums.append(pair[: SUMS // 2] + pair[SUMS // 2 :])
-        sums_ref[0, :, at] = jnp.where(left_sums, sums[0], swap(sums[1]))
-        sums_ref[1, :, at] = jnp.where(left_sums, swap(sums[0]), sums[1])
-
-
-def unpack(received, rows, channels):
-    devices = received.shape[0]
+            pair = in_ref[source, pl.ds(rows + half, 2 * MISC), :].astype(jnp.float32)
+            misc = pair[:MISC] + pair[MISC:]
+            miscs.append(misc)
+            code = in_ref[source, pl.ds(0, rows), :].astype(jnp.float32)
+            results.append(decode(code, misc[0:1]))
+            code = in_ref[source, pl.ds(rows, half), :].astype(jnp.float32)
+            grads.append(decode(code, misc[1:2]))
+        one, two = grads
+        filter_out[pl.ds(0, half), at] = jnp.where(left_half, one, swap(two))
+        filter_out[pl.ds(half, half), at] = jnp.where(left_half, swap(one), two)
+        one, two = results
+        back = jnp.where(left, one, swap(two))
+        mixed = jnp.where(left, swap(one), two)
+        one, two = miscs
+        lefts = jnp.where(left_misc, one, swap(two))
+        rights = jnp.where(left_misc, swap(one), two)
+        taps = (lefts[4:7], rights[4:7], rights[7:10])
+        for offset in range(3):
+            taps_out[0, offset : offset + 1, at] = lefts[10 + offset : 11 + offset]
+            taps_out[1, offset : offset + 1, at] = rights[10 + offset : 11 + offset]
+            taps_out[2, offset : offset + 1, at] = rights[13 + offset : 14 + offset]
+        skip_out[0:1, at] = lefts[16:17]
+        back_edge, mixed_edge = lefts[2:4], rights[2:4]
+        convs, edges = [], []
+        for stream, source in enumerate((query_ref, key_ref, value_ref)):
+            now = source[:, at].astype(jnp.float32)
+            before[pl.ds(0, 8), :] = last_ref[stream, :, at].astype(jnp.float32)[EDGE - 8 :]
+            before[pl.ds(8, rows), :] = now
+            before[pl.ds(8 + rows, 8), :] = first_ref[stream, :, at].astype(jnp.float32)[:8]
+            conv = taps[stream][0:1] * now
+            edge = taps[stream][0:1] * before[pl.ds(8 + rows, 2), :]
+            for offset in (1, 2):
+                weight = taps[stream][offset : offset + 1]
+                conv = conv + weight * before[pl.ds(8 - offset, rows), :]
+                edge = edge + weight * before[pl.ds(8 + rows - offset, 2), :]
+            convs.append(conv)
+            edges.append(edge)
+        cotangent = cot_ref[:, at].astype(jnp.float32)
+        cot_edge = first_ref[3, :, at].astype(jnp.float32)[0:2]
+        gated_out[:, at] = (convs[0] * mixed).astype(jnp.bfloat16)
+        for stream, (out, grad, edge) in enumerate(
+            (
+                (query_out, cotangent * mixed, cot_edge * mixed_edge),
+                (key_out, back * convs[2], back_edge * edges[2]),
+                (value_out, back * convs[1], back_edge * edges[1]),
+            )
+        ):
+            after[pl.ds(0, rows), :] = grad
+            after[pl.ds(rows, 2), :] = edge
+            total = taps[stream][0:1] * grad
+            for offset in (1, 2):
+                weight = taps[stream][offset : offset + 1]
+                total = total + weight * after[pl.ds(offset, rows), :]
+            out[:, at] = total.astype(jnp.bfloat16)
+
+
+def finish(received, streams, cotangent, last_rows, next_rows):
+    rows, channels = cotangent.shape
     low = jax.ShapeDtypeStruct((rows, channels), jnp.bfloat16)
-    if channels == devices * HALF:
-        return pl.pallas_call(
-            unpack_kernel,
-            out_shape=(
-                low,
-                low,
-                low,
-                low,
-                jax.ShapeDtypeStruct((rows, channels), jnp.float32),
-                jax.ShapeDtypeStruct((2, SUMS // 2, channels), jnp.float32),
-            ),
-            compiler_params=pltpu.CompilerParams(vmem_limit_bytes=VMEM_BYTES),
-        )(received)
-    share = channels // devices
-
-    def lay(start, count, side):
-        piece = received[:, start : start + count, side * HALF : side * HALF + share]
-        return piece.transpose(1, 0, 2).reshape(count, channels)
-
-    def whole(start, count, side):
-        return lay(start, count, side).astype(jnp.float32)
-
-    sums = [
-        whole(3 * rows, SUMS // 2, side) + whole(3 * rows + SUMS // 2, SUMS // 2, side)
-        for side in (0, 1)
-    ]
-    return (
-        lay(rows, rows, 0),
-        lay(0, rows, 0),
-        lay(0, rows, 1),
-        lay(rows, rows, 1),
-        whole(2 * rows, rows, 0) + whole(2 * rows, rows, 1),
-        jnp.stack(sums),
-    )
+    return pl.pallas_call(
+        finish_kernel,
+        out_shape=(
+            low,
+            low,
+            low,
+            low,
+            jax.ShapeDtypeStruct((rows, channels), jnp.float32),
+            jax.ShapeDtypeStruct((3, 3, channels), jnp.float32),
+            jax.ShapeDtypeStruct((1, channels), jnp.float32),
+        ),
+        scratch_shapes=[
+            pltpu.VMEM((rows + 16, LANES), jnp.float32),
+            pltpu.VMEM((rows + 8, LANES), jnp.float32),
+        ],
+        compiler_params=pltpu.CompilerParams(vmem_limit_bytes=VMEM_BYTES),
+    )(received, *streams, cotangent, last_rows, next_rows)
 
 
 def operator_kernel(
     forward_ref, inverse_ref, taps_ref, in_ref, out_ref,
-    behind, ahead, first_ref, second_ref, fields, spectra, filters, rhs, rhs_back, sums_ref,
+    behind, ahead, first_ref, second_ref, fields, spectra, filters, rhs, rhs_back, sums_ref, misc,
 ):
     blocks = in_ref.shape[0]
-    rows = in_ref.shape[1] // 3
+    rows = forward_ref.shape[0] // 2
     half = blocks // 2
+    half_rows = rows // 2
     grad_scale = 1.0 / math.sqrt(blocks * rows)
     left = left_lanes((rows, LANES))
+    left_half = left_lanes((half_rows, LANES))
     taps = taps_ref[...]
     query_taps = [taps[i : i + 1] for i in range(3)]
     value_taps = [taps[3 + i : 4 + i] for i in range(3)]
@@ -190,13 +247,20 @@
         for side in range(2):
             spectra[2 * pair + side] = result[:, side * LANES : (side + 1) * LANES]
         for side in range(2):
-            both = in_ref[2 * pair + side, pl.ds(2 * rows, rows), :]
-            wide = both.astype(jnp.float32)
-            turned = swap(wide)
+            block = 2 * pair + side
+            ends = in_ref[block, pl.ds(2 * rows + half_rows, 16), :].astype(jnp.float32)
+            code = in_ref[block, pl.ds(2 * rows, half_rows), :].astype(jnp.float32)
+            taken = decode(code, ends[0:1] + ends[8:9])
+            turned = swap(taken)
             at = pl.ds(side * LANES, LANES)
-            rhs[pl.ds(0, rows), at] = both
-            rhs[pl.ds(rows, rows), at] = turned.astype(jnp.bfloat16)
-            rhs[pl.ds(2 * rows, rows), at] = jnp.where(left, wide, turned).astype(jnp.bfloat16)
+            for place, value in (
+                (0, jnp.where(left_half, taken, turned)),
+                (half_rows, jnp.where(left_half, turned, taken)),
+            ):
+                head, tail = head_tail(value)
+                rhs[pl.ds(place, half_rows), at] = head
+                rhs[pl.ds(rows + place, half_rows), at] = tail
+                rhs[pl.ds(2 * rows + place, half_rows), at] = head
         result = jnp.dot(forward_ref[...], rhs[...], preferred_element_type=jnp.float32)
         for side in range(2):
             filters[2 * pair + side] = result[:, side * LANES : (side + 1) * LANES]
@@ -297,12 +361,16 @@
         result = back(filters, pair) * grad_scale
         for side in range(2):
             value = result[:, side * LANES : (side + 1) * LANES]
-            head, tail = head_tail(value)
-            head, tail = head.astype(jnp.float32), tail.astype(jnp.float32)
+            upper, lower = value[:half_rows], value[half_rows:]
             near = 2 * pair + side
-            here = pl.ds(2 * rows, rows)
-            out_ref[near, here, :] = jnp.where(left, head, swap(tail)).astype(jnp.bfloat16)
-            out_ref[near + half, here, :] = jnp.where(left, swap(head), tail).astype(jnp.bfloat16)
+            for dest, halves in (
+                (near, jnp.where(left_half, upper, swap(lower))),
+                (near + half, jnp.where(left_half, swap(upper), lower)),
+            ):
+                scale = scale_of(halves)
+                code = encode(halves, scale).astype(jnp.bfloat16)
+                out_ref[dest, pl.ds(rows, half_rows), :] = code
+                misc[dest, 1:2, :] = scale
         return 0
 
     lax.fori_loop(0, half // 2, filter_grads, 0)
@@ -312,50 +380,57 @@
 
     def outputs(step, carry):
         block = blocks - 1 - step
-        starts, totals = carry[:2], carry[2:]
+        starts, totals = carry[:3], carry[3:]
         field = fields[block]
         result = jnp.where(
             left,
             spectra[blocks - 1 - block, pl.ds(0, rows), :],
             spectra[block, pl.ds(0, rows), :],
         )
-        turned = swap(result + gain * field)
+        result = result + gain * field
+        scale = scale_of(result)
+        out_ref[block, pl.ds(0, rows), :] = encode(result, scale).astype(jnp.bfloat16)
+        misc[block, 0:1, :] = scale
+        misc[block, 2:4, :] = starts[2][0:2]
+        turned = swap(result)
         grads = (second_ref[block] * turned, first_ref[block] * turned)
         new_totals = []
-        for place, weights in ((0, query_taps), (1, value_taps)):
+        for place in (0, 1):
             grad = grads[place]
             ahead[place, pl.ds(0, rows), :] = grad
             ahead[place, pl.ds(rows, 8), :] = starts[place]
-            here = pl.ds(place * rows, rows)
-            stream = in_ref[block, here, :].astype(jnp.float32)
-            total = weights[0] * grad
+            stream = in_ref[block, pl.ds(place * rows, rows), :].astype(jnp.float32)
             new_totals.append(totals[3 * place] + fold(grad * stream))
             for offset in (1, 2):
                 later = ahead[place, pl.ds(offset, rows), :]
-                total = total + weights[offset] * later
                 new_totals.append(totals[3 * place + offset] + fold(later * stream))
-            out_ref[block, here, :] = total.astype(jnp.bfloat16)
         new_totals.append(totals[6] + fold(field * swap(field)))
-        return (grads[0][:8], grads[1][:8], *new_totals)
-
-    totals = lax.fori_loop(0, blocks, outputs, (nothing,) * 9)[2:]
-    sums_ref[...] = jnp.zeros((8, LANES), jnp.float32)
+        return (grads[0][:8], grads[1][:8], result[:8], *new_totals)
+
+    totals = lax.fori_loop(0, blocks, outputs, (nothing,) * 10)[3:]
+    sums_ref[pl.ds(0, 6), :] = taps[0:6]
     for row, total in enumerate(totals):
-        sums_ref[row : row + 1, :] = grad_scale * jnp.sum(total, axis=0, keepdims=True)
-    head, tail = head_tail(sums_ref[...])
-    both = jnp.concatenate([head.astype(jnp.float32), tail.astype(jnp.float32)], axis=0)
-    for block in range(blocks):
-        out_ref[block, pl.ds(3 * rows, SUMS), :] = both.astype(jnp.bfloat16)
+        sums_ref[6 + row : 7 + row, :] = grad_scale * jnp.sum(total, axis=0, keepdims=True)
+
+    def close(block, _):
+        misc[block, pl.ds(4, 13), :] = sums_ref[pl.ds(0, 13), :]
+        misc[block, pl.ds(17, 7), :] = jnp.zeros((7, LANES), jnp.float32)
+        head, tail = head_tail(misc[block])
+        both = jnp.concatenate([head.astype(jnp.float32), tail.astype(jnp.float32)], axis=0)
+        out_ref[block, pl.ds(rows + half_rows, 2 * MISC), :] = both.astype(jnp.bfloat16)
+        return 0
+
+    lax.fori_loop(0, blocks, close, 0)
 
 
 def operator(taps, streams):
     blocks = streams.shape[0]
-    rows = streams.shape[1] // 3
+    rows = (streams.shape[1] - 16) * 2 // 5
     forward, inverse = transform_matrices(rows)
     wide = (blocks, rows, LANES)
     return pl.pallas_call(
         operator_kernel,
-        out_shape=jax.ShapeDtypeStruct((blocks, 3 * rows + SUMS, LANES), jnp.bfloat16),
+        out_shape=jax.ShapeDtypeStruct((blocks, rows + rows // 2 + 2 * MISC, LANES), jnp.bfloat16),
         scratch_shapes=[
             pltpu.VMEM((2, rows + 8, LANES), jnp.float32),
             pltpu.VMEM((2, rows + 8, LANES), jnp.float32),
@@ -366,7 +441,8 @@
             pltpu.VMEM((blocks, 2 * rows, LANES), jnp.float32),
             pltpu.VMEM((3 * rows, 2 * LANES), jnp.bfloat16),
             pltpu.VMEM((6 * rows, 2 * LANES), jnp.bfloat16),
-            pltpu.VMEM((8, LANES), jnp.float32),
+            pltpu.VMEM((16, LANES), jnp.float32),
+            pltpu.VMEM((blocks, MISC, LANES), jnp.float32),
         ],
         compiler_params=pltpu.CompilerParams(vmem_limit_bytes=VMEM_BYTES),
     )(jnp.asarray(forward), jnp.asarray(inverse), taps, streams)
@@ -396,16 +472,42 @@
     return lax.ppermute(rows, ("seq", "chan"), route)
 
 
+def spread(value, devices):
+    rows, channels = value.shape
+    share = channels // devices
+    if share == HALF:
+        return value
+    wide = jnp.pad(value.reshape(rows, devices, share), ((0, 0), (0, 0), (0, HALF - share)))
+    return wide.reshape(rows, devices * HALF)
+
+
+def gathered(value, share):
+    if share == HALF:
+        return value
+    groups = value.reshape(*value.shape[:-1], value.shape[-1] // HALF, HALF)[..., :share]
+    return groups.reshape(*value.shape[:-1], -1)
+
+
+def shift(value, by):
+    length = lax.axis_size("seq")
+    pairs = [(i, i + by) for i in range(length) if 0 <= i + by < length]
+    return lax.ppermute(value, "seq", pairs)
+
+
 def per_device(query_rows, key_rows, value_rows, long_filter, short_taps, skip_gain, cotangent):
-    rows, channels = query_rows.shape
     devices = lax.axis_size("seq")
+    share = query_rows.shape[1] // devices
     taps = own_taps(short_taps, skip_gain)
-    sent = pack(query_rows, key_rows, value_rows, cotangent, long_filter, devices)
-    streams = lax.all_to_all(sent, "seq", 0, 0, tiled=True)
-    results = lax.all_to_all(operator(taps, streams), "seq", 0, 0, tiled=True)
-    gated, query_grad, key_grad, value_grad, filter_grad, sums = unpack(results, rows, channels)
-    taps_grad = jnp.stack([sums[0, 0:3], sums[1, 0:3], sums[1, 3:6]])
-    return gated, query_grad, key_grad, value_grad, filter_grad, taps_grad, sums[0, 6]
+    streams = [spread(value, devices) for value in (query_rows, key_rows, value_rows)]
+    upstream = spread(cotangent, devices)
+    sent, last_rows, first_rows = pack(streams, upstream, spread(long_filter, devices), devices)
+    received = lax.all_to_all(sent, "seq", 0, 0, tiled=True)
+    last_rows = shift(last_rows, 1)
+    next_rows = shift(first_rows, -1)
+    results = lax.all_to_all(operator(taps, received), "seq", 0, 0, tiled=True)
+    outs = finish(results, streams, upstream, last_rows, next_rows)
+    *outs, skip_grad = (gathered(value, share) for value in outs)
+    return (*outs, skip_grad[0])
 
 
 def solution(mesh):

time: 115 us -> 92.6 us (0.81)
  blocking collectives: 43.8 us -> 0 us
  waiting for transfers between devices: 36.3 us -> 49.4 us
  starting transfers between devices: 8.04 us -> 17.7 us
  local copies, waits for them, and re-layouts: 4.02 us -> 2.1 us
  Pallas kernels: 20.9 us -> 22.2 us
    all_to_all x1 -> x0, blocking collectives: 43.8 us -> none  [per_device(): results = lax.all_to_all(operator(taps, streams), 'seq', 0, 0, tiled=True)]
    ppermute x0 -> x2, waiting for transfers between devices: none -> 6.66 us  [shift(): return lax.ppermute(value, 'seq', pairs)]
    all_to_all x1 -> x2, waiting for transfers between devices: 36.3 us -> 42.8 us  [the longest x1 31.4 us: per_device(): received = lax.all_to_all(sent, 'seq', 0, 0, tiled=True)]
    ppermute x0 -> x2, starting transfers between devices: none -> 5.84 us  [shift(): return lax.ppermute(value, 'seq', pairs)]
    all_to_all x1 -> x2, starting transfers between devices: 7.39 us -> 11.2 us  [the longest x1 7.4 us: per_device(): received = lax.all_to_all(sent, 'seq', 0, 0, tiled=True)]
    slice x3 -> x0, local copies, waits for them, and re-layouts: 2.78 us -> none  [the longest x2 1.48 us: per_device(): taps_grad = jnp.stack([sums[0, 0:3], sums[1, 0:3], sums[1, 3:6]])]
    pallas_call x3, Pallas kernels: 20.9 us -> 22.2 us  [the longest x1 14.6 us: operator(): pl.pallas_call(operator_kernel, out_shape=jax.ShapeDtypeStruct((blocks, r...]
  transfers between devices with their start and end apart: 2 -> 5, of which waited for: 1 -> 3; matrix products, arithmetic and copies ran while one was open for 0% -> 0% of each run, Pallas kernels for 0% -> 0%
where the time goes in v2:
time: 92.6 us; the launch traced here: 92.1 us
  waiting for transfers between devices  49.4 us (53%)
  Pallas kernels  22.2 us (24%)
  starting transfers between devices  17.7 us (19%)
  local copies, waits for them, and re-layouts  2.1 us (2%)
    all_to_all x1, waiting for transfers between devices, per_device(): received = lax.all_to_all(sent, 'seq', 0, 0, tiled=True)  31.4 us
    pallas_call x1, Pallas kernels, operator(): pl.pallas_call(operator_kernel, out_shape=jax.ShapeDtypeStruct((blocks, r...  14.6 us
    all_to_all x1, waiting for transfers between devices, per_device(): results = lax.all_to_all(operator(taps, received), 'seq', 0, 0, tiled=True)  11.4 us
    all_to_all x1, starting transfers between devices, per_device(): received = lax.all_to_all(sent, 'seq', 0, 0, tiled=True)  7.4 us
    ppermute x2, waiting for transfers between devices, shift(): return lax.ppermute(value, 'seq', pairs)  6.66 us
    ppermute x2, starting transfers between devices, shift(): return lax.ppermute(value, 'seq', pairs)  5.84 us
    pallas_call x1, Pallas kernels, finish(): pl.pallas_call(finish_kernel, out_shape=(low, low, low, low, jax.ShapeDty...  4.53 us
    all_to_all x1, starting transfers between devices, per_device(): results = lax.all_to_all(operator(taps, received), 'seq', 0, 0, tiled=True)  3.77 us
  transfers between devices with their start and end apart: 5, of which 3 were waited for; matrix products, arithmetic and copies ran while one was open for 0% of the time, Pallas kernels for 0%

profile of v2, /device:TPU:0, one launch (start us, length us, event | category | flops | bytes accessed | tf_op | source)
XLA Modules:
  0.0 92.1 jit_solution(2272874708111182895)
XLA Ops:
  0.6 3.1 %shard_map.144 = (bf16[8,656,128]{2,1,0:T(8,128)(2,1)}, bf16[3,16,512]{2,1,0:T(8,128)(2,1)}, bf16[4,16,512]{2,1,0:T(8,128)(2,1)}) custom-call(bf16[256,512]{1,0:T(8,128)(2,1)} %query_ref.3, bf16[256,512]{1,0:T(8,128)(2,1)} %key_ref.3, bf16[256,512]{1,0:T(8,128)(2,1)} %value_ref.3, bf16[256,512]{1,0:T(8,128)(2,1)} %cot_ref.3, f32[256,512]{1,0:T(8,128)} %filter_ref.1), custom_call_target="tpu_custom_call" | custom-call | tf_op jit(solution)/shard_map/pallas_call | solution.py:99
  3.7 0.0 copy-start.4
  3.7 0.0 copy-start.6
  3.7 0.0 copy-start.7
  3.7 7.4 %all-to-all-start = ((bf16[8,656,128]{2,1,0:T(8,128)(2,1)}), bf16[8,656,128]{2,1,0:T(8,128)(2,1)S(1)}, u32[]{:S(2)}, u32[]{:S(2)}) async-start(bf16[8,656,128]{2,1,0:T(8,128)(2,1)} %get-tuple-element.17), calls=%async_computation | async-start | bytes 2686976 | tf_op jit(solution)/shard_map/all_to_all | solution.py:504
  11.1 0.1 pad.6.clone
  11.2 0.0 copy-done.4
  11.2 0.0 copy-done.6
  11.2 0.0 copy-done.7
  11.2 0.1 maximum_maximum_fusion
  11.3 0.7 collective-permute-start
  11.9 0.0 collective-permute-done.taps_ref
  11.9 0.0 copy-start.5
  12.0 31.4 %all-to-all-done.in_ref = bf16[8,656,128]{2,1,0:T(8,128)(2,1)S(1)} async-done(((bf16[8,656,128]{2,1,0:T(8,128)(2,1)}), bf16[8,656,128]{2,1,0:T(8,128)(2,1)S(1)}, u32[]{:S(2)}, u32[]{:S(2)}) %all-to-all-start) | async-done | bytes 1343520 | tf_op jit(solution)/shard_map/all_to_all | solution.py:504
  43.3 0.0 copy-done.5
  43.3 0.0 copy-start
  43.3 1.1 %copy-done = bf16[8,656,128]{2,1,0:T(8,128)(2,1)} copy-done((bf16[8,656,128]{2,1,0:T(8,128)(2,1)}, bf16[8,656,128]{2,1,0:T(8,128)(2,1)S(1)}, u32[]{:S(2)}) %copy-start) | copy-done | bytes 1343512
  44.4 14.6 %shard_map.145 = bf16[8,432,128]{2,1,0:T(8,128)(2,1)} custom-call(bf16[512,768]{1,0:T(8,128)(2,1)} %constant.3.clone.forward_ref, bf16[256,1536]{1,0:T(8,128)(2,1)} %constant.10.clone.inverse_ref, f32[8,128]{1,0:T(8,128)} %copy-done.5, bf16[8,656,128]{2,1,0:T(8,128)(2,1)} %copy-done), custom_call_target="tpu_custom_call" | custom-call | tf_op jit(solution)/shard_map/pallas_call | solution.py:431
  59.0 0.0 copy-start.8
  59.0 0.0 copy-start.9
  59.0 3.8 %all-to-all-start.1 = ((bf16[8,432,128]{2,1,0:T(8,128)(2,1)}), bf16[8,432,128]{2,1,0:T(8,128)(2,1)S(1)}, u32[]{:S(2)}, u32[]{:S(2)}) async-start(bf16[8,432,128]{2,1,0:T(8,128)(2,1)} %shard_map.145), calls=%async_computation.1 | async-start | bytes 1769472 | tf_op jit(solution)/shard_map/all_to_all | solution.py:507
  62.7 0.0 copy-done.8
  62.8 1.3 %collective-permute-start.2 = (bf16[4,16,512]{2,1,0:T(8,128)(2,1)S(1)}, bf16[4,16,512]{2,1,0:T(8,128)(2,1)S(1)}, u32[]{:S(2)}, u32[]{:S(2)}) collective-permute-start(bf16[4,16,512]{2,1,0:T(8,128)(2,1)S(1)} %copy-done.8), channel_id=1, source_target_pairs={{4,0},{8,4},{12,8},{16,12},{20,16},{24,20},{28,24},{5,1},{9,5},{13... | collective-permute-start | bytes 196616 | tf_op jit(solution)/shard_map/ppermute | solution.py:494
  64.1 0.0 copy-done.9
  64.1 4.5 %collective-permute-start.1 = (bf16[3,16,512]{2,1,0:T(8,128)(2,1)S(1)}, bf16[3,16,512]{2,1,0:T(8,128)(2,1)S(1)}, u32[]{:S(2)}, u32[]{:S(2)}) collective-permute-start(bf16[3,16,512]{2,1,0:T(8,128)(2,1)S(1)} %copy-done.9), channel_id=1, source_target_pairs={{0,4},{4,8},{8,12},{12,16},{16,20},{20,24},{24,28},{1,5},{5,9},{9,... | collective-permute-start | bytes 147464 | tf_op jit(solution)/shard_map/ppermute | solution.py:494
  68.6 6.7 %collective-permute-done.1.last_ref = bf16[3,16,512]{2,1,0:T(8,128)(2,1)S(1)} collective-permute-done((bf16[3,16,512]{2,1,0:T(8,128)(2,1)S(1)}, bf16[3,16,512]{2,1,0:T(8,128)(2,1)S(1)}, u32[]{:S(2)}, u32[]{:S(2)}) %collective-permute-start.1) | collective-permute-done | bytes 49184 | tf_op jit(solution)/shard_map/ppermute | solution.py:494
  75.3 0.0 copy-start.3
  75.3 0.0 collective-permute-done.2.first_ref
  75.3 0.0 copy-start.2
  75.3 11.4 %all-to-all-done.1.in_ref = bf16[8,432,128]{2,1,0:T(8,128)(2,1)S(1)} async-done(((bf16[8,432,128]{2,1,0:T(8,128)(2,1)}), bf16[8,432,128]{2,1,0:T(8,128)(2,1)S(1)}, u32[]{:S(2)}, u32[]{:S(2)}) %all-to-all-start.1) | async-done | bytes 884768 | tf_op jit(solution)/shard_map/all_to_all | solution.py:507
  86.7 0.0 copy-done.3
  86.7 0.0 copy-done.2
  86.7 0.0 copy-start.1
  86.7 0.9 copy-done.1
  87.6 4.5 %shard_map.146 = (bf16[256,512]{1,0:T(8,128)(2,1)}, bf16[256,512]{1,0:T(8,128)(2,1)}, bf16[256,512]{1,0:T(8,128)(2,1)}, bf16[256,512]{1,0:T(8,128)(2,1)}, f32[25...) custom-call(bf16[8,432,128]{2,1,0:T(8,128)(2,1)} %copy-done.1, bf16[256,512]{1,0:T(8,128)(2,1)} %query_ref.3, ...), custom_call_target="tpu_custom_call" | custom-call | tf_op jit(solution)/shard_map/pallas_call | solution.py:183
  (1 shorter events, 0.0 us)
Async XLA Ops:
  3.7 7.5 %copy-start.4 = (f32[3,3,64]{2,1,0:T(4,128)S(1)}, f32[3,3,64]{2,1,0:T(4,128)}, u32[]{:S(2)}) copy-start(f32[3,3,64]{2,1,0:T(4,128)} %param.13) | copy-start | bytes 6916
  3.7 7.5 %copy-start.6 = (f32[3,64]{1,0:T(4,128)S(1)}, f32[3,64]{1,0:T(4,128)}, u32[]{:S(2)}) copy-start(f32[3,64]{1,0:T(4,128)} %constant.4.clone.1) | copy-start | bytes 2308
  3.7 7.5 %copy-start.7 = (f32[64]{0:T(128)S(1)}, f32[64]{0:T(128)}, u32[]{:S(2)}) copy-start(f32[64]{0:T(128)} %param.14) | copy-start | bytes 772
  3.7 39.6 %all-to-all-start = ((bf16[8,656,128]{2,1,0:T(8,128)(2,1)}), bf16[8,656,128]{2,1,0:T(8,128)(2,1)S(1)}, u32[]{:S(2)}, u32[]{:S(2)}) async-start(bf16[8,656,128]{2,1,0:T(8,128)(2,1)} %get-tuple-element.17), calls=%async_computation | async-start | bytes 2686976 | tf_op jit(solution)/shard_map/all_to_all | solution.py:504
  11.3 0.7 collective-permute-start
  11.9 31.4 %copy-start.5 = (f32[8,128]{1,0:T(8,128)}, f32[8,128]{1,0:T(8,128)S(1)}, u32[]{:S(2)}) copy-start(f32[8,128]{1,0:T(8,128)S(1)} %collective-permute-done.taps_ref) | copy-start | bytes 12292
  43.3 1.1 %copy-start = (bf16[8,656,128]{2,1,0:T(8,128)(2,1)}, bf16[8,656,128]{2,1,0:T(8,128)(2,1)S(1)}, u32[]{:S(2)}) copy-start(bf16[8,656,128]{2,1,0:T(8,128)(2,1)S(1)} %all-to-all-done.in_ref) | copy-start | bytes 4030468
  59.0 3.8 %copy-start.8 = (bf16[4,16,512]{2,1,0:T(8,128)(2,1)S(1)}, bf16[4,16,512]{2,1,0:T(8,128)(2,1)}, u32[]{:S(2)}) copy-start(bf16[4,16,512]{2,1,0:T(8,128)(2,1)} %get-tuple-element.19) | copy-start | bytes 196612
  59.0 5.1 %copy-start.9 = (bf16[3,16,512]{2,1,0:T(8,128)(2,1)S(1)}, bf16[3,16,512]{2,1,0:T(8,128)(2,1)}, u32[]{:S(2)}) copy-start(bf16[3,16,512]{2,1,0:T(8,128)(2,1)} %get-tuple-element.18) | copy-start | bytes 147460
  59.0 27.7 %all-to-all-start.1 = ((bf16[8,432,128]{2,1,0:T(8,128)(2,1)}), bf16[8,432,128]{2,1,0:T(8,128)(2,1)S(1)}, u32[]{:S(2)}, u32[]{:S(2)}) async-start(bf16[8,432,128]{2,1,0:T(8,128)(2,1)} %shard_map.145), calls=%async_computation.1 | async-start | bytes 1769472 | tf_op jit(solution)/shard_map/all_to_all | solution.py:507
  62.8 12.5 %collective-permute-start.2 = (bf16[4,16,512]{2,1,0:T(8,128)(2,1)S(1)}, bf16[4,16,512]{2,1,0:T(8,128)(2,1)S(1)}, u32[]{:S(2)}, u32[]{:S(2)}) collective-permute-start(bf16[4,16,512]{2,1,0:T(8,128)(2,1)S(1)} %copy-done.8), channel_id=1, source_target_pairs={{4,0},{8,4},{12,8},{16,12},{20,16},{24,20},{28,24},{5,1},{9,5},{13... | collective-permute-start | bytes 196616 | tf_op jit(solution)/shard_map/ppermute | solution.py:494
  64.1 11.2 %collective-permute-start.1 = (bf16[3,16,512]{2,1,0:T(8,128)(2,1)S(1)}, bf16[3,16,512]{2,1,0:T(8,128)(2,1)S(1)}, u32[]{:S(2)}, u32[]{:S(2)}) collective-permute-start(bf16[3,16,512]{2,1,0:T(8,128)(2,1)S(1)} %copy-done.9), channel_id=1, source_target_pairs={{0,4},{4,8},{8,12},{12,16},{16,20},{20,24},{24,28},{1,5},{5,9},{9,... | collective-permute-start | bytes 147464 | tf_op jit(solution)/shard_map/ppermute | solution.py:494
  75.3 11.4 %copy-start.3 = (bf16[3,16,512]{2,1,0:T(8,128)(2,1)}, bf16[3,16,512]{2,1,0:T(8,128)(2,1)S(1)}, u32[]{:S(2)}) copy-start(bf16[3,16,512]{2,1,0:T(8,128)(2,1)S(1)} %collective-permute-done.1.last_ref) | copy-start | bytes 147460
  75.3 11.4 %copy-start.2 = (bf16[4,16,512]{2,1,0:T(8,128)(2,1)}, bf16[4,16,512]{2,1,0:T(8,128)(2,1)S(1)}, u32[]{:S(2)}) copy-start(bf16[4,16,512]{2,1,0:T(8,128)(2,1)S(1)} %collective-permute-done.2.first_ref) | copy-start | bytes 196612
  86.7 0.9 copy-start.1

commit v3 on v2

--- a/solution.py
+++ b/solution.py
@@ -11,10 +11,12 @@
 HALF = 64
 LANES = 2 * HALF
 EDGE = 16
-MISC = 24
+MISC = 16
 SPAN = 252.0
 FLOOR = 125.0
-VMEM_BYTES = 62 * 1024 * 1024
+MEBIBYTE = 1024 * 1024
+VMEM_BYTES = 62 * MEBIBYTE
+UNROLLED = 8
 
 
 def swap(value):
@@ -65,29 +67,26 @@
 def pack_kernel(
     query_ref, key_ref, value_ref, cot_ref, filter_ref, out_ref, last_ref, first_ref
 ):
-    rows, channels = query_ref.shape
+    rows = query_ref.shape[0]
     half = rows // 2
     left = left_lanes((rows, LANES))
     left_half = left_lanes((half, LANES))
-    for tile in range(channels // LANES):
-        at = pl.ds(tile * LANES, LANES)
-        for first, second, place in ((query_ref, key_ref, 0), (cot_ref, value_ref, 1)):
-            one = first[:, at].astype(jnp.float32)
-            two = second[:, at].astype(jnp.float32)
-            here = pl.ds(place * rows, rows)
-            out_ref[2 * tile, here, :] = jnp.where(left, one, swap(two)).astype(jnp.bfloat16)
-            out_ref[2 * tile + 1, here, :] = jnp.where(left, swap(one), two).astype(jnp.bfloat16)
-        upper = filter_ref[pl.ds(0, half), at]
-        lower = filter_ref[pl.ds(half, half), at]
-        for dest, pair in (
-            (2 * tile, jnp.where(left_half, upper, swap(lower))),
-            (2 * tile + 1, jnp.where(left_half, swap(upper), lower)),
-        ):
-            scale = scale_of(pair)
-            out_ref[dest, pl.ds(2 * rows, half), :] = encode(pair, scale).astype(jnp.bfloat16)
-            head, tail = head_tail(jnp.broadcast_to(scale, (8, LANES)))
-            both = jnp.concatenate([head.astype(jnp.float32), tail.astype(jnp.float32)], axis=0)
-            out_ref[dest, pl.ds(2 * rows + half, 16), :] = both.astype(jnp.bfloat16)
+    for first, second, place in ((query_ref, key_ref, 0), (cot_ref, value_ref, 1)):
+        one = first[...].astype(jnp.float32)
+        two = second[...].astype(jnp.float32)
+        here = pl.ds(place * rows, rows)
+        out_ref[0, here, :] = jnp.where(left, one, swap(two)).astype(jnp.bfloat16)
+        out_ref[1, here, :] = jnp.where(left, swap(one), two).astype(jnp.bfloat16)
+    upper = filter_ref[pl.ds(0, half), :]
+    lower = filter_ref[pl.ds(half, half), :]
+    for dest, pair in enumerate(
+        (jnp.where(left_half, upper, swap(lower)), jnp.where(left_half, swap(upper), lower))
+    ):
+        scale = scale_of(pair)
+        out_ref[dest, pl.ds(2 * rows, half), :] = encode(pair, scale).astype(jnp.bfloat16)
+        head, tail = head_tail(jnp.broadcast_to(scale, (8, LANES)))
+        both = jnp.concatenate([head.astype(jnp.float32), tail.astype(jnp.float32)], axis=0)
+        out_ref[dest, pl.ds(2 * rows + half, 16), :] = both.astype(jnp.bfloat16)
     for stream, source in enumerate((query_ref, key_ref, value_ref, cot_ref)):
         first_ref[stream] = source[pl.ds(0, EDGE), :]
         if stream < 3:
@@ -96,10 +95,19 @@
 
 def pack(streams, cotangent, long_filter, devices):
     rows, channels = cotangent.shape
+    sent_rows = 2 * rows + rows // 2 + 16
+    whole = pl.BlockSpec((rows, LANES), lambda tile: (0, tile))
     return pl.pallas_call(
         pack_kernel,
+        grid=(channels // LANES,),
+        in_specs=[whole] * 5,
+        out_specs=(
+            pl.BlockSpec((2, sent_rows, LANES), lambda tile: (tile, 0, 0)),
+            pl.BlockSpec((3, EDGE, LANES), lambda tile: (0, 0, tile)),
+            pl.BlockSpec((4, EDGE, LANES), lambda tile: (0, 0, tile)),
+        ),
         out_shape=(
-            jax.ShapeDtypeStruct((devices, 2 * rows + rows // 2 + 16, LANES), jnp.bfloat16),
+            jax.ShapeDtypeStruct((devices, sent_rows, LANES), jnp.bfloat16),
             jax.ShapeDtypeStruct((3, EDGE, channels), jnp.bfloat16),
             jax.ShapeDtypeStruct((4, EDGE, channels), jnp.bfloat16),
         ),
@@ -142,7 +150,7 @@
             taps_out[0, offset : offset + 1, at] = lefts[10 + offset : 11 + offset]
             taps_out[1, offset : offset + 1, at] = rights[10 + offset : 11 + offset]
             taps_out[2, offset : offset + 1, at] = rights[13 + offset : 14 + offset]
-        skip_out[0:1, at] = lefts[16:17]
+        skip_out[0:1, at] = lefts[13:14]
         back_edge, mixed_edge = lefts[2:4], rights[2:4]
         convs, edges = [], []
         for stream, source in enumerate((query_ref, key_ref, value_ref)):
@@ -195,18 +203,27 @@
             pltpu.VMEM((rows + 16, LANES), jnp.float32),
             pltpu.VMEM((rows + 8, LANES), jnp.float32),
         ],
-        compiler_params=pltpu.CompilerParams(vmem_limit_bytes=VMEM_BYTES),
+        compiler_params=pltpu.CompilerParams(vmem_limit_bytes=3 * received.shape[0] * MEBIBYTE // 2),
     )(received, *streams, cotangent, last_rows, next_rows)
+
+
+def loop(count, body, carry, unrolled):
+    if unrolled:
+        for index in range(count):
+            carry = body(index, carry)
+        return carry
+    return lax.fori_loop(0, count, body, carry)
 
 
 def operator_kernel(
     forward_ref, inverse_ref, taps_ref, in_ref, out_ref,
-    behind, ahead, first_ref, second_ref, fields, spectra, filters, rhs, rhs_back, sums_ref, misc,
+    edged, first_ref, second_ref, fields, spectra, filters, rhs, rhs_back, shared, misc,
 ):
     blocks = in_ref.shape[0]
     rows = forward_ref.shape[0] // 2
     half = blocks // 2
     half_rows = rows // 2
+    unrolled = blocks <= UNROLLED
     grad_scale = 1.0 / math.sqrt(blocks * rows)
     left = left_lanes((rows, LANES))
     left_half = left_lanes((half_rows, LANES))
@@ -214,63 +231,71 @@
     query_taps = [taps[i : i + 1] for i in range(3)]
     value_taps = [taps[3 + i : 4 + i] for i in range(3)]
     gain = taps[6:7]
-
-    def short(block, carry):
-        outs, ends = [], []
-        for place, weights, before in ((0, query_taps, carry[0]), (1, value_taps, carry[1])):
-            now = in_ref[block, pl.ds(place * rows, rows), :].astype(jnp.float32)
-            behind[place, pl.ds(0, 8), :] = before
-            behind[place, pl.ds(8, rows), :] = now
-            total = weights[0] * now
-            for offset in (1, 2):
-                total = total + weights[offset] * behind[place, pl.ds(8 - offset, rows), :]
-            outs.append(total)
-            ends.append(now[rows - 8 :])
-        first_ref[block] = outs[0]
-        second_ref[block] = outs[1]
-        fields[block] = outs[0] * outs[1]
-        return tuple(ends)
-
     nothing = jnp.zeros((8, LANES), jnp.float32)
-    lax.fori_loop(0, blocks, short, (nothing, nothing))
-
-    def transform(pair, _):
-        for side in range(2):
-            block = 2 * pair + side
-            field = jnp.where(left, fields[blocks - 1 - block], fields[block])
-            head, tail = head_tail(field)
-            at = pl.ds(side * LANES, LANES)
-            rhs[pl.ds(0, rows), at] = head
-            rhs[pl.ds(rows, rows), at] = tail
-            rhs[pl.ds(2 * rows, rows), at] = head
-        result = jnp.dot(forward_ref[...], rhs[...], preferred_element_type=jnp.float32)
-        for side in range(2):
-            spectra[2 * pair + side] = result[:, side * LANES : (side + 1) * LANES]
+
+    def lay(buffer, side, place, value):
+        head, tail = head_tail(value)
+        count = value.shape[0]
+        at = pl.ds(side * LANES, LANES)
+        rhs[buffer, pl.ds(place, count), at] = head
+        rhs[buffer, pl.ds(rows + place, count), at] = tail
+        rhs[buffer, pl.ds(2 * rows + place, count), at] = head
+
+    def transformed(buffer):
+        return jnp.dot(forward_ref[...], rhs[buffer], preferred_element_type=jnp.float32)
+
+    def transform(pair, carry):
+        spot = 2 * pair if unrolled else 0
         for side in range(2):
             block = 2 * pair + side
             ends = in_ref[block, pl.ds(2 * rows + half_rows, 16), :].astype(jnp.float32)
             code = in_ref[block, pl.ds(2 * rows, half_rows), :].astype(jnp.float32)
             taken = decode(code, ends[0:1] + ends[8:9])
             turned = swap(taken)
-            at = pl.ds(side * LANES, LANES)
-            for place, value in (
-                (0, jnp.where(left_half, taken, turned)),
-                (half_rows, jnp.where(left_half, turned, taken)),
-            ):
-                head, tail = head_tail(value)
-                rhs[pl.ds(place, half_rows), at] = head
-                rhs[pl.ds(rows + place, half_rows), at] = tail
-                rhs[pl.ds(2 * rows + place, half_rows), at] = head
-        result = jnp.dot(forward_ref[...], rhs[...], preferred_element_type=jnp.float32)
+            lay(spot, side, 0, jnp.where(left_half, taken, turned))
+            lay(spot, side, half_rows, jnp.where(left_half, turned, taken))
+        result = transformed(spot)
         for side in range(2):
             filters[2 * pair + side] = result[:, side * LANES : (side + 1) * LANES]
-        return 0
-
-    lax.fori_loop(0, half, transform, 0)
+        for side in range(2):
+            block = 2 * pair + side
+            outs, ends = [], []
+            for place, weights in ((0, query_taps), (1, value_taps)):
+                now = in_ref[block, pl.ds(place * rows, rows), :].astype(jnp.float32)
+                edged[block, place, pl.ds(0, 8), :] = carry[place]
+                edged[block, place, pl.ds(8, rows), :] = now
+                total = weights[0] * now
+                for offset in (1, 2):
+                    shifted = edged[block, place, pl.ds(8 - offset, rows), :]
+                    total = total + weights[offset] * shifted
+                outs.append(total)
+                ends.append(now[rows - 8 :])
+            carry = tuple(ends)
+            first_ref[block] = outs[0]
+            second_ref[block] = outs[1]
+            field = outs[0] * outs[1]
+            fields[block] = field
+            lay(spot + 1, side, 0, field)
+        result = transformed(spot + 1)
+        for side in range(2):
+            spectra[2 * pair + side] = result[:, side * LANES : (side + 1) * LANES]
+        return carry
+
+    loop(half, transform, (nothing, nothing), unrolled)
 
     chunk = 8
     left_chunk = left_lanes((chunk, LANES))
     conjugate = jnp.where(left_chunk, -1.0, 1.0)
+
+    def products(pairs):
+        one = two = three = None
+        for (re, im, both), (join_re, join_less, join_more) in pairs:
+            terms = join_re * both, re * join_less, im * join_more
+            if one is None:
+                one, two, three = terms
+            else:
+                one, two, three = one + terms[0], two + terms[1], three + terms[2]
+        return one - three, one + two
 
     def spectral(step, sign):
         real_at = pl.ds(pl.multiple_of(step * chunk, chunk), chunk)
@@ -285,46 +310,45 @@
                 return re[block] - im[block - 1], im[block] + re[block - 1]
             return re[block] + im[block - 1], im[block] - re[block - 1]
 
+        turned = []
+        for block in range(blocks):
+            re = jnp.where(left_chunk, field_re[blocks - 1 - block], field_re[block])
+            im = jnp.where(left_chunk, field_im[blocks - 1 - block], field_im[block])
+            turned.append((re, im, re + im))
         filt_re = [filters[block, real_at, :] for block in range(blocks)]
         filt_im = [filters[block, imag_at, :] for block in range(blocks)]
-        joins = [joined(filt_re, filt_im, block) for block in range(blocks)]
-        joins = [(re, im * conjugate) for re, im in joins]
+        joins = []
         for block in range(blocks):
-            out_re = out_im = None
-            for lag in range(block + 1):
-                re, im = field_re[block - lag], field_im[block - lag]
-                join_re, join_im = joins[lag]
-                term_re = re * join_re - im * join_im
-                term_im = re * join_im + im * join_re
-                out_re = term_re if out_re is None else out_re + term_re
-                out_im = term_im if out_im is None else out_im + term_im
-            spectra[block, real_at, :] = out_re
-            spectra[block, imag_at, :] = out_im
+            re, im = joined(filt_re, filt_im, block)
+            im = im * conjugate
+            joins.append((re, im - re, re + im))
+        outs = [
+            products([(turned[block - lag], joins[lag]) for lag in range(block + 1)])
+            for block in range(blocks)
+        ]
         grads = []
         for block in range(blocks):
-            re, im = field_re[blocks - 1 - block], field_im[blocks - 1 - block]
-            grads.append(
-                (jnp.where(left_chunk, re, swap(re)), jnp.where(left_chunk, im, swap(im)))
-            )
-        joins = [joined(field_re, field_im, block) for block in range(blocks)]
-        products = []
+            re = jnp.where(left_chunk, field_re[block], swap(field_re[block]))
+            im = jnp.where(left_chunk, field_im[block], swap(field_im[block]))
+            grads.append((re, im, re + im))
+        sums = [joined(field_re, field_im, block) for block in range(blocks)]
+        joins = []
         for block in range(blocks):
             parts = []
             for part in range(2):
-                far = joins[block - half][part] if block >= half else 0.0
-                parts.append(jnp.where(left_chunk, swap(joins[block][part]), far))
-            products.append(parts)
+                far = sums[block - half][part] if block >= half else 0.0
+                parts.append(jnp.where(left_chunk, swap(sums[block][part]), far))
+            re, im = parts
+            joins.append((re, -im - re, re - im))
+        for block in range(blocks):
+            for part, at in ((0, real_at), (1, imag_at)):
+                spectra[block, at, :] = jnp.where(
+                    left_chunk, outs[blocks - 1 - block][part], outs[block][part]
+                )
         for lag in range(half):
-            out_re = out_im = None
-            for block in range(lag, blocks):
-                re, im = grads[block]
-                join_re, join_im = products[block - lag]
-                term_re = re * join_re + im * join_im
-                term_im = im * join_re - re * join_im
-                out_re = term_re if out_re is None else out_re + term_re
-                out_im = term_im if out_im is None else out_im + term_im
-            filters[lag, real_at, :] = out_re
-            filters[lag, imag_at, :] = out_im
+            out = products([(grads[block], joins[block - lag]) for block in range(lag, blocks)])
+            filters[lag, real_at, :] = out[0]
+            filters[lag, imag_at, :] = out[1]
 
     def even(step, _):
         spectral(step, 1)
@@ -338,27 +362,17 @@
     lax.fori_loop(0, steps // 2, even, 0)
     lax.fori_loop(steps // 2, steps, odd, 0)
 
-    def back(source, pair):
+    def back(source, pair, buffer):
         for side in range(2):
             head, tail = head_tail(source[2 * pair + side])
             at = pl.ds(side * LANES, LANES)
-            rhs_back[pl.ds(0, 2 * rows), at] = head
-            rhs_back[pl.ds(2 * rows, 2 * rows), at] = tail
-            rhs_back[pl.ds(4 * rows, 2 * rows), at] = head
-        return jnp.dot(inverse_ref[...], rhs_back[...], preferred_element_type=jnp.float32)
-
-    def mixed(pair, _):
-        result = back(spectra, pair)
-        for side in range(2):
-            spectra[2 * pair + side, pl.ds(0, rows), :] = result[
-                :, side * LANES : (side + 1) * LANES
-            ]
-        return 0
-
-    lax.fori_loop(0, half, mixed, 0)
+            rhs_back[buffer, pl.ds(0, 2 * rows), at] = head
+            rhs_back[buffer, pl.ds(2 * rows, 2 * rows), at] = tail
+            rhs_back[buffer, pl.ds(4 * rows, 2 * rows), at] = head
+        return jnp.dot(inverse_ref[...], rhs_back[buffer], preferred_element_type=jnp.float32)
 
     def filter_grads(pair, _):
-        result = back(filters, pair) * grad_scale
+        result = back(filters, pair, pair if unrolled else 0) * grad_scale
         for side in range(2):
             value = result[:, side * LANES : (side + 1) * LANES]
             upper, lower = value[:half_rows], value[half_rows:]
@@ -373,54 +387,55 @@
                 misc[dest, 1:2, :] = scale
         return 0
 
-    lax.fori_loop(0, half // 2, filter_grads, 0)
+    loop(half // 2, filter_grads, 0, unrolled)
 
     def fold(value):
         return jnp.sum(value.reshape(rows // 8, 8, LANES), axis=0)
 
     def outputs(step, carry):
-        block = blocks - 1 - step
-        starts, totals = carry[:3], carry[3:]
-        field = fields[block]
-        result = jnp.where(
-            left,
-            spectra[blocks - 1 - block, pl.ds(0, rows), :],
-            spectra[block, pl.ds(0, rows), :],
-        )
-        result = result + gain * field
-        scale = scale_of(result)
-        out_ref[block, pl.ds(0, rows), :] = encode(result, scale).astype(jnp.bfloat16)
-        misc[block, 0:1, :] = scale
-        misc[block, 2:4, :] = starts[2][0:2]
-        turned = swap(result)
-        grads = (second_ref[block] * turned, first_ref[block] * turned)
-        new_totals = []
-        for place in (0, 1):
-            grad = grads[place]
-            ahead[place, pl.ds(0, rows), :] = grad
-            ahead[place, pl.ds(rows, 8), :] = starts[place]
-            stream = in_ref[block, pl.ds(place * rows, rows), :].astype(jnp.float32)
-            new_totals.append(totals[3 * place] + fold(grad * stream))
-            for offset in (1, 2):
-                later = ahead[place, pl.ds(offset, rows), :]
-                new_totals.append(totals[3 * place + offset] + fold(later * stream))
-        new_totals.append(totals[6] + fold(field * swap(field)))
-        return (grads[0][:8], grads[1][:8], result[:8], *new_totals)
-
-    totals = lax.fori_loop(0, blocks, outputs, (nothing,) * 10)[3:]
-    sums_ref[pl.ds(0, 6), :] = taps[0:6]
-    for row, total in enumerate(totals):
-        sums_ref[6 + row : 7 + row, :] = grad_scale * jnp.sum(total, axis=0, keepdims=True)
+        pair = half - 1 - step
+        results = back(spectra, pair, (half // 2 + step) if unrolled else 0)
+        for side in (1, 0):
+            block = 2 * pair + side
+            start, totals = carry[0], carry[1:]
+            field = fields[block]
+            result = results[:, side * LANES : (side + 1) * LANES] + gain * field
+            scale = scale_of(result)
+            out_ref[block, pl.ds(0, rows), :] = encode(result, scale).astype(jnp.bfloat16)
+            misc[block, 0:1, :] = scale
+            misc[block, 2:4, :] = start[0:2]
+            turned = swap(result)
+            grads = (second_ref[block] * turned, first_ref[block] * turned)
+            new_totals = []
+            for place in (0, 1):
+                grad = grads[place]
+                stream = edged[block, place, pl.ds(8, rows), :]
+                new_totals.append(totals[3 * place] + fold(grad * stream))
+                for offset in (1, 2):
+                    earlier = edged[block, place, pl.ds(8 - offset, rows), :]
+                    new_totals.append(totals[3 * place + offset] + fold(grad * earlier))
+            new_totals.append(totals[6] + fold(field * swap(field)))
+            carry = (result[:8], *new_totals)
+        return carry
+
+    totals = loop(half, outputs, (nothing,) * 8, unrolled)[1:]
+    sums = [grad_scale * jnp.sum(total, axis=0, keepdims=True) for total in totals]
+    shared[0:6, :] = taps[0:6]
+    for row in range(6):
+        value = sums[row]
+        if row == 3:
+            value = jnp.where(left_lanes((1, LANES)), sums[6], value)
+        shared[6 + row : 7 + row, :] = value
 
     def close(block, _):
-        misc[block, pl.ds(4, 13), :] = sums_ref[pl.ds(0, 13), :]
-        misc[block, pl.ds(17, 7), :] = jnp.zeros((7, LANES), jnp.float32)
+        misc[block, 4:16, :] = shared[0:12, :]
         head, tail = head_tail(misc[block])
-        both = jnp.concatenate([head.astype(jnp.float32), tail.astype(jnp.float32)], axis=0)
-        out_ref[block, pl.ds(rows + half_rows, 2 * MISC), :] = both.astype(jnp.bfloat16)
+        here = rows + half_rows
+        out_ref[block, pl.ds(here, MISC), :] = head
+        out_ref[block, pl.ds(here + MISC, MISC), :] = tail
         return 0
 
-    lax.fori_loop(0, blocks, close, 0)
+    loop(blocks, close, 0, unrolled)
 
 
 def operator(taps, streams):
@@ -428,23 +443,27 @@
     rows = (streams.shape[1] - 16) * 2 // 5
     forward, inverse = transform_matrices(rows)
     wide = (blocks, rows, LANES)
+    backs = 3 * blocks // 4 if blocks <= UNROLLED else 1
     return pl.pallas_call(
         operator_kernel,
-        out_shape=jax.ShapeDtypeStruct((blocks, rows + rows // 2 + 2 * MISC, LANES), jnp.bfloat16),
+        out_shape=jax.ShapeDtypeStruct(
+            (blocks, rows + rows // 2 + 2 * MISC, LANES), jnp.bfloat16
+        ),
         scratch_shapes=[
-            pltpu.VMEM((2, rows + 8, LANES), jnp.float32),
-            pltpu.VMEM((2, rows + 8, LANES), jnp.float32),
+            pltpu.VMEM((blocks, 2, rows + 8, LANES), jnp.float32),
             pltpu.VMEM(wide, jnp.float32),
             pltpu.VMEM(wide, jnp.float32),
             pltpu.VMEM(wide, jnp.float32),
             pltpu.VMEM((blocks, 2 * rows, LANES), jnp.float32),
             pltpu.VMEM((blocks, 2 * rows, LANES), jnp.float32),
-            pltpu.VMEM((3 * rows, 2 * LANES), jnp.bfloat16),
-            pltpu.VMEM((6 * rows, 2 * LANES), jnp.bfloat16),
+            pltpu.VMEM((blocks if blocks <= UNROLLED else 2, 3 * rows, 2 * LANES), jnp.bfloat16),
+            pltpu.VMEM((backs, 6 * rows, 2 * LANES), jnp.bfloat16),
             pltpu.VMEM((16, LANES), jnp.float32),
             pltpu.VMEM((blocks, MISC, LANES), jnp.float32),
         ],
-        compiler_params=pltpu.CompilerParams(vmem_limit_bytes=VMEM_BYTES),
+        compiler_params=pltpu.CompilerParams(
+            vmem_limit_bytes=min(4 * blocks * MEBIBYTE, VMEM_BYTES)
+        ),
     )(jnp.asarray(forward), jnp.asarray(inverse), taps, streams)
 
 

time: 92.6 us -> 84.4 us (0.911)
  Pallas kernels: 22.2 us -> 16.9 us
  local copies, waits for them, and re-layouts: 2.1 us -> 0.13 us
    pallas_call x1, Pallas kernels: 14.6 us -> 9.86 us  [operator(): pl.pallas_call(operator_kernel, out_shape=jax.ShapeDtypeStruct((blocks, r...]
    unnamed x20 -> x22, local copies, waits for them, and re-layouts: 2.03 us -> 0.06 us
    pallas_call x1, Pallas kernels: 4.53 us -> 3.02 us  [finish(): pl.pallas_call(finish_kernel, out_shape=(low, low, low, low, jax.ShapeDty...]
    ppermute x2, waiting for transfers between devices: 6.66 us -> 5.41 us  [shift(): return lax.ppermute(value, 'seq', pairs)]
    pallas_call x1, Pallas kernels: 3.07 us -> 4.02 us  [pack(): pl.pallas_call(pack_kernel, grid=(channels // LANES,), in_specs=[whole] *...]
where the time goes in v3:
time: 84.4 us; the launch traced here: 84 us
  waiting for transfers between devices  48.5 us (57%)
  starting transfers between devices  17.7 us (21%)
  Pallas kernels  16.9 us (20%)
    all_to_all x1, waiting for transfers between devices, per_device(): received = lax.all_to_all(sent, 'seq', 0, 0, tiled=True)  31.4 us
    all_to_all x1, waiting for transfers between devices, per_device(): results = lax.all_to_all(operator(taps, received), 'seq', 0, 0, tiled=True)  11.7 us
    pallas_call x1, Pallas kernels, operator(): pl.pallas_call(operator_kernel, out_shape=jax.ShapeDtypeStruct((blocks, r...  9.86 us
    all_to_all x1, starting transfers between devices, per_device(): received = lax.all_to_all(sent, 'seq', 0, 0, tiled=True)  7.4 us
    ppermute x2, starting transfers between devices, shift(): return lax.ppermute(value, 'seq', pairs)  5.84 us
    ppermute x2, waiting for transfers between devices, shift(): return lax.ppermute(value, 'seq', pairs)  5.41 us
    pallas_call x1, Pallas kernels, pack(): pl.pallas_call(pack_kernel, grid=(channels // LANES,), in_specs=[whole] *...  4.02 us
    all_to_all x1, starting transfers between devices, per_device(): results = lax.all_to_all(operator(taps, received), 'seq', 0, 0, tiled=True)  3.79 us
  transfers between devices with their start and end apart: 5, of which 3 were waited for; matrix products, arithmetic and copies ran while one was open for 0% of the time, Pallas kernels for 0%

profile of v3, /device:TPU:0, one launch (start us, length us, event | category | flops | bytes accessed | tf_op | source)
XLA Modules:
  0.0 84.0 jit_solution(8537402864360079441)
XLA Ops:
  0.6 4.0 %shard_map.144 = (bf16[8,656,128]{2,1,0:T(8,128)(2,1)}, bf16[3,16,512]{2,1,0:T(8,128)(2,1)}, bf16[4,16,512]{2,1,0:T(8,128)(2,1)}) custom-call(bf16[256,512]{1,0:T(8,128)(2,1)} %query_ref.3, bf16[256,512]{1,0:T(8,128)(2,1)} %key_ref.3, bf16[256,512]{1,0:T(8,128)(2,1)} %value_ref.3, bf16[256,512]{1,0:T(8,128)(2,1)} %cot_ref.3, f32[256,512]{1,0:T(8,128)} %filter_ref.1), custom_call_target="tpu_custom_call" | custom-call | tf_op jit(solution)/shard_map/pallas_call | solution.py:100
  4.7 0.0 copy-start.6
  4.7 0.0 copy-start.7
  4.7 0.0 copy-start.8
  4.7 0.0 copy-start.4
  4.7 0.0 copy-start.5
  4.7 7.4 %all-to-all-start = ((bf16[8,656,128]{2,1,0:T(8,128)(2,1)}), bf16[8,656,128]{2,1,0:T(8,128)(2,1)S(1)}, u32[]{:S(2)}, u32[]{:S(2)}) async-start(bf16[8,656,128]{2,1,0:T(8,128)(2,1)} %get-tuple-element.17), calls=%async_computation | async-start | bytes 2686976 | tf_op jit(solution)/shard_map/all_to_all | solution.py:523
  12.1 0.1 pad.6.clone
  12.2 0.0 copy-done.6
  12.2 0.0 copy-done.7
  12.2 0.0 copy-done.8
  12.2 0.1 maximum_maximum_fusion
  12.3 0.7 collective-permute-start
  12.9 0.0 collective-permute-done.taps_ref
  12.9 31.4 %all-to-all-done.in_ref = bf16[8,656,128]{2,1,0:T(8,128)(2,1)S(1)} async-done(((bf16[8,656,128]{2,1,0:T(8,128)(2,1)}), bf16[8,656,128]{2,1,0:T(8,128)(2,1)S(1)}, u32[]{:S(2)}, u32[]{:S(2)}) %all-to-all-start) | async-done | bytes 1343520 | tf_op jit(solution)/shard_map/all_to_all | solution.py:523
  44.3 0.0 copy-done.4
  44.3 0.0 copy-done.5
  44.3 9.9 %shard_map.145 = bf16[8,416,128]{2,1,0:T(8,128)(2,1)} custom-call(bf16[512,768]{1,0:T(8,128)(2,1)S(1)} %copy-done.5, bf16[256,1536]{1,0:T(8,128)(2,1)S(1)} %copy-done.4, f32[8,128]{1,0:T(8,128)S(1)} %collective-permute-done.taps_ref, bf16[8,656,128]{2,1,0:T(8,128)(2,1)S(1)} %all-to-all-done.in_ref), custom_call_target="tpu_custom_call" | custom-call | tf_op jit(solution)/shard_map/pallas_call | solution.py:447
  54.2 0.0 copy-start.9
  54.2 0.0 copy-start.10
  54.2 0.0 copy-start
  54.2 0.0 copy-start.1
  54.2 0.0 copy-start.2
  54.2 0.0 copy-start.3
  54.2 3.8 %all-to-all-start.1 = ((bf16[8,416,128]{2,1,0:T(8,128)(2,1)}), bf16[8,416,128]{2,1,0:T(8,128)(2,1)S(1)}, u32[]{:S(2)}, u32[]{:S(2)}) async-start(bf16[8,416,128]{2,1,0:T(8,128)(2,1)} %shard_map.145), calls=%async_computation.1 | async-start | bytes 1703936 | tf_op jit(solution)/shard_map/all_to_all | solution.py:526
  58.0 0.0 copy-done.9
  58.0 1.3 %collective-permute-start.2 = (bf16[4,16,512]{2,1,0:T(8,128)(2,1)S(1)}, bf16[4,16,512]{2,1,0:T(8,128)(2,1)S(1)}, u32[]{:S(2)}, u32[]{:S(2)}) collective-permute-start(bf16[4,16,512]{2,1,0:T(8,128)(2,1)S(1)} %copy-done.9), channel_id=1, source_target_pairs={{4,0},{8,4},{12,8},{16,12},{20,16},{24,20},{28,24},{5,1},{9,5},{13... | collective-permute-start | bytes 196616 | tf_op jit(solution)/shard_map/ppermute | solution.py:513
  59.3 0.0 copy-done.10
  59.3 4.5 %collective-permute-start.1 = (bf16[3,16,512]{2,1,0:T(8,128)(2,1)S(1)}, bf16[3,16,512]{2,1,0:T(8,128)(2,1)S(1)}, u32[]{:S(2)}, u32[]{:S(2)}) collective-permute-start(bf16[3,16,512]{2,1,0:T(8,128)(2,1)S(1)} %copy-done.10), channel_id=1, source_target_pairs={{0,4},{4,8},{8,12},{12,16},{16,20},{20,24},{24,28},{1,5},{5,9},{9,... | collective-permute-start | bytes 147464 | tf_op jit(solution)/shard_map/ppermute | solution.py:513
  63.9 5.4 %collective-permute-done.1.last_ref = bf16[3,16,512]{2,1,0:T(8,128)(2,1)S(1)} collective-permute-done((bf16[3,16,512]{2,1,0:T(8,128)(2,1)S(1)}, bf16[3,16,512]{2,1,0:T(8,128)(2,1)S(1)}, u32[]{:S(2)}, u32[]{:S(2)}) %collective-permute-start.1) | collective-permute-done | bytes 49184 | tf_op jit(solution)/shard_map/ppermute | solution.py:513
  69.3 0.0 collective-permute-done.2.first_ref
  69.3 11.7 %all-to-all-done.1.in_ref = bf16[8,416,128]{2,1,0:T(8,128)(2,1)S(1)} async-done(((bf16[8,416,128]{2,1,0:T(8,128)(2,1)}), bf16[8,416,128]{2,1,0:T(8,128)(2,1)S(1)}, u32[]{:S(2)}, u32[]{:S(2)}) %all-to-all-start.1) | async-done | bytes 852000 | tf_op jit(solution)/shard_map/all_to_all | solution.py:526
  81.0 0.0 copy-done
  81.0 0.0 copy-done.1
  81.0 0.0 copy-done.2
  81.0 0.0 copy-done.3
  81.0 3.0 %shard_map.146 = (bf16[256,512]{1,0:T(8,128)(2,1)}, bf16[256,512]{1,0:T(8,128)(2,1)}, bf16[256,512]{1,0:T(8,128)(2,1)}, bf16[256,512]{1,0:T(8,128)(2,1)}, f32[25...) custom-call(bf16[8,416,128]{2,1,0:T(8,128)(2,1)S(1)} %all-to-all-done.1.in_ref, ...), custom_call_target="tpu_custom_call" | custom-call | tf_op jit(solution)/shard_map/pallas_call | solution.py:191
  (1 shorter events, 0.0 us)
Async XLA Ops:
  4.7 7.5 %copy-start.6 = (f32[3,3,64]{2,1,0:T(4,128)S(1)}, f32[3,3,64]{2,1,0:T(4,128)}, u32[]{:S(2)}) copy-start(f32[3,3,64]{2,1,0:T(4,128)} %param.13) | copy-start | bytes 6916
  4.7 7.5 %copy-start.7 = (f32[3,64]{1,0:T(4,128)S(1)}, f32[3,64]{1,0:T(4,128)}, u32[]{:S(2)}) copy-start(f32[3,64]{1,0:T(4,128)} %constant.4.clone.1) | copy-start | bytes 2308
  4.7 7.5 %copy-start.8 = (f32[64]{0:T(128)S(1)}, f32[64]{0:T(128)}, u32[]{:S(2)}) copy-start(f32[64]{0:T(128)} %param.14) | copy-start | bytes 772
  4.7 39.6 %copy-start.4 = (bf16[256,1536]{1,0:T(8,128)(2,1)S(1)}, bf16[256,1536]{1,0:T(8,128)(2,1)}, u32[]{:S(2)}) copy-start(bf16[256,1536]{1,0:T(8,128)(2,1)} %constant.10.clone.inverse_ref) | copy-start | bytes 2359300
  4.7 39.6 %copy-start.5 = (bf16[512,768]{1,0:T(8,128)(2,1)S(1)}, bf16[512,768]{1,0:T(8,128)(2,1)}, u32[]{:S(2)}) copy-start(bf16[512,768]{1,0:T(8,128)(2,1)} %constant.3.clone.forward_ref) | copy-start | bytes 2359300
  4.7 39.6 %all-to-all-start = ((bf16[8,656,128]{2,1,0:T(8,128)(2,1)}), bf16[8,656,128]{2,1,0:T(8,128)(2,1)S(1)}, u32[]{:S(2)}, u32[]{:S(2)}) async-start(bf16[8,656,128]{2,1,0:T(8,128)(2,1)} %get-tuple-element.17), calls=%async_computation | async-start | bytes 2686976 | tf_op jit(solution)/shard_map/all_to_all | solution.py:523
  12.3 0.7 collective-permute-start
  54.2 3.8 %copy-start.9 = (bf16[4,16,512]{2,1,0:T(8,128)(2,1)S(1)}, bf16[4,16,512]{2,1,0:T(8,128)(2,1)}, u32[]{:S(2)}) copy-start(bf16[4,16,512]{2,1,0:T(8,128)(2,1)} %get-tuple-element.19) | copy-start | bytes 196612
  54.2 5.1 %copy-start.10 = (bf16[3,16,512]{2,1,0:T(8,128)(2,1)S(1)}, bf16[3,16,512]{2,1,0:T(8,128)(2,1)}, u32[]{:S(2)}) copy-start(bf16[3,16,512]{2,1,0:T(8,128)(2,1)} %get-tuple-element.18) | copy-start | bytes 147460
  54.2 26.8 %copy-start = (bf16[256,512]{1,0:T(8,128)(2,1)S(1)}, bf16[256,512]{1,0:T(8,128)(2,1)}, u32[]{:S(2)}) copy-start(bf16[256,512]{1,0:T(8,128)(2,1)} %query_ref.3) | copy-start | bytes 786436
  54.2 26.8 %copy-start.1 = (bf16[256,512]{1,0:T(8,128)(2,1)S(1)}, bf16[256,512]{1,0:T(8,128)(2,1)}, u32[]{:S(2)}) copy-start(bf16[256,512]{1,0:T(8,128)(2,1)} %key_ref.3) | copy-start | bytes 786436
  54.2 26.8 %copy-start.2 = (bf16[256,512]{1,0:T(8,128)(2,1)S(1)}, bf16[256,512]{1,0:T(8,128)(2,1)}, u32[]{:S(2)}) copy-start(bf16[256,512]{1,0:T(8,128)(2,1)} %value_ref.3) | copy-start | bytes 786436
  54.2 26.8 %copy-start.3 = (bf16[256,512]{1,0:T(8,128)(2,1)S(1)}, bf16[256,512]{1,0:T(8,128)(2,1)}, u32[]{:S(2)}) copy-start(bf16[256,512]{1,0:T(8,128)(2,1)} %cot_ref.3) | copy-start | bytes 786436
  54.2 26.7 %all-to-all-start.1 = ((bf16[8,416,128]{2,1,0:T(8,128)(2,1)}), bf16[8,416,128]{2,1,0:T(8,128)(2,1)S(1)}, u32[]{:S(2)}, u32[]{:S(2)}) async-start(bf16[8,416,128]{2,1,0:T(8,128)(2,1)} %shard_map.145), calls=%async_computation.1 | async-start | bytes 1703936 | tf_op jit(solution)/shard_map/all_to_all | solution.py:526
  58.0 11.3 %collective-permute-start.2 = (bf16[4,16,512]{2,1,0:T(8,128)(2,1)S(1)}, bf16[4,16,512]{2,1,0:T(8,128)(2,1)S(1)}, u32[]{:S(2)}, u32[]{:S(2)}) collective-permute-start(bf16[4,16,512]{2,1,0:T(8,128)(2,1)S(1)} %copy-done.9), channel_id=1, source_target_pairs={{4,0},{8,4},{12,8},{16,12},{20,16},{24,20},{28,24},{5,1},{9,5},{13... | collective-permute-start | bytes 196616 | tf_op jit(solution)/shard_map/ppermute | solution.py:513
  59.3 10.0 %collective-permute-start.1 = (bf16[3,16,512]{2,1,0:T(8,128)(2,1)S(1)}, bf16[3,16,512]{2,1,0:T(8,128)(2,1)S(1)}, u32[]{:S(2)}, u32[]{:S(2)}) collective-permute-start(bf16[3,16,512]{2,1,0:T(8,128)(2,1)S(1)} %copy-done.10), channel_id=1, source_target_pairs={{0,4},{4,8},{8,12},{12,16},{16,20},{20,24},{24,28},{1,5},{5,9},{9,... | collective-permute-start | bytes 147464 | tf_op jit(solution)/shard_map/ppermute | solution.py:513

commit v4 on v3

v4 whole, which is shorter than its diff:
```python
import math

import jax
import jax.numpy as jnp
import numpy as np
from jax import lax
from jax.experimental import pallas as pl
from jax.experimental.pallas import tpu as pltpu
from jax.sharding import PartitionSpec as P

HALF = 64
LANES = 2 * HALF
ENDS = 16
MISC = 16
SPAN = 252.0
FLOOR = 125.0
MEBIBYTE = 1024 * 1024
VMEM_BYTES = 62 * MEBIBYTE
LISTED = 8
ORDER = (0, 7, 6, 3, 2, 5, 4, 1)


def swap(value):
    return pltpu.roll(value, HALF, 1)


def left_lanes(shape):
    return lax.broadcasted_iota(jnp.int32, shape, 1) < HALF


def head_tail(value):
    head = value.astype(jnp.bfloat16)
    tail = (value - head.astype(jnp.float32)).astype(jnp.bfloat16)
    return head, tail


def transform_matrices(rows):
    freq = np.concatenate([np.arange(0, rows, 2), np.arange(1, rows, 2)])
    turn = (2 * freq[:, None] + 1) * np.arange(rows)[None, :] % (4 * rows)
    theta = turn * (math.pi / (2 * rows))
    forward = np.concatenate([np.cos(theta), -np.sin(theta)])
    inverse = forward.T / rows

    def split(matrix):
        single = matrix.astype(np.float32)
        head = single.astype(jnp.bfloat16)
        tail = (single - head.astype(np.float32)).astype(jnp.bfloat16)
        return np.concatenate([head, head, tail], axis=1)

    return split(forward), split(inverse)


def encode(value, scale):
    code = jnp.exp2(jnp.abs(value) * (SPAN / scale) - FLOOR)
    return jnp.where(value < 0.0, -code, code)


def decode(code, scale):
    size = (jnp.log2(jnp.abs(code)) + FLOOR) * (scale * (1.0 / SPAN))
    return jnp.where(code < 0.0, -size, size)


def scale_of(value):
    peak = jnp.max(jnp.abs(value), axis=0, keepdims=True)
    return jnp.maximum(peak * 1.0001, 1e-30)


def loop(count, body, carry, unrolled):
    if unrolled:
        for index in range(count):
            carry = body(index, carry)
        return carry
    return lax.fori_loop(0, count, body, carry)


def piece(refs, index, place):
    return refs[index] if len(refs) > 1 else refs[0].at[index ^ place]


def exchange(pieces):
    if len(pieces) == 1:
        return [lax.all_to_all(pieces[0], "seq", 0, 0, tiled=True)]
    others = [
        lax.ppermute(value, "seq", [(one, one ^ index) for one in range(len(pieces))])
        for index, value in enumerate(pieces[1:], 1)
    ]
    return [pieces[0], *others]


def in_order(pieces):
    return [pieces[index] for index in ORDER] if len(pieces) > 1 else pieces


def by_index(refs):
    if len(refs) == 1:
        return refs
    return [refs[ORDER.index(index)] for index in range(len(refs))]


def piece_shapes(devices, rows):
    if devices == LISTED:
        return [jax.ShapeDtypeStruct((rows, LANES), jnp.bfloat16)] * devices
    return [jax.ShapeDtypeStruct((devices, rows, LANES), jnp.bfloat16)]


def join(mask, one, two, side):
    return jnp.where(mask, pltpu.roll(one, side * HALF, 1), pltpu.roll(two, HALF - side * HALF, 1))


def pack_kernel(query_ref, key_ref, value_ref, cot_ref, filter_ref, *out_refs):
    rows, channels = query_ref.shape
    devices = channels // HALF
    half = rows // 2
    place = lax.axis_index("seq")
    left = left_lanes((rows, LANES))
    left_half = left_lanes((half, LANES))

    def one_piece(index, _):
        out_ref = piece(out_refs, index, place)
        dest = index ^ place
        side = lax.rem(dest, 2)
        at = pl.ds(pl.multiple_of(dest // 2 * LANES, LANES), LANES)
        for first, second, start in ((query_ref, key_ref, 0), (cot_ref, value_ref, rows)):
            one = first[:, at].astype(jnp.float32)
            two = second[:, at].astype(jnp.float32)
            out_ref[pl.ds(start, rows), :] = join(left, one, two, side).astype(jnp.bfloat16)
        upper = filter_ref[pl.ds(0, half), at]
        lower = filter_ref[pl.ds(half, half), at]
        pair = join(left_half, upper, lower, side)
        scale = scale_of(pair)
        out_ref[pl.ds(2 * rows, half), :] = encode(pair, scale).astype(jnp.bfloat16)
        head, tail = head_tail(jnp.broadcast_to(scale, (8, LANES)))
        both = jnp.concatenate([head.astype(jnp.float32), tail.astype(jnp.float32)], axis=0)
        out_ref[pl.ds(2 * rows + half, 16), :] = both.astype(jnp.bfloat16)
        return 0

    loop(devices, one_piece, 0, len(out_refs) > 1)


def pack(streams, cotangent, long_filter, devices):
    rows = cotangent.shape[0]
    return pl.pallas_call(
        pack_kernel,
        out_shape=piece_shapes(devices, 2 * rows + rows // 2 + 16),
        compiler_params=pltpu.CompilerParams(vmem_limit_bytes=VMEM_BYTES),
    )(*streams, cotangent, long_filter)


def finish_kernel(
    pieces, query_ref, key_ref, value_ref, cot_ref, gated_out, query_out, key_out, value_out,
    filter_out, taps_out, skip_out, before, after,
):
    in_refs = by_index(pieces)
    rows, channels = query_ref.shape
    half = rows // 2
    place = lax.axis_index("seq")
    odd = lax.rem(place, 2) == 1
    left = left_lanes((rows, LANES))
    left_half = left_lanes((half, LANES))
    left_misc = left_lanes((MISC, LANES))

    def one_tile(step, _):
        refs = piece(in_refs, 2 * step, place), piece(in_refs, 2 * step + 1, place)
        at = pl.ds(pl.multiple_of((step ^ (place // 2)) * LANES, LANES), LANES)

        def both(start, count):
            one, two = (ref[pl.ds(start, count), :].astype(jnp.float32) for ref in refs)
            return jnp.where(odd, two, one), jnp.where(odd, one, two)

        def sides(mask, values):
            one, two = values
            return jnp.where(mask, one, swap(two)), jnp.where(mask, swap(one), two)

        miscs = [
            head + tail
            for head, tail in zip(both(rows + half, MISC), both(rows + half + MISC, MISC))
        ]
        codes = both(0, rows)
        back, mixed = sides(left, [decode(code, misc[0:1]) for code, misc in zip(codes, miscs)])
        codes = both(rows, half)
        upper, lower = sides(
            left_half, [decode(code, misc[1:2]) for code, misc in zip(codes, miscs)]
        )
        filter_out[pl.ds(0, half), at] = upper
        filter_out[pl.ds(half, half), at] = lower
        ends = sides(left_misc, both(rows + half + 2 * MISC, ENDS))
        lefts, rights = sides(left_misc, miscs)
        taps = (lefts[4:7], rights[4:7], rights[7:10])
        for offset in range(3):
            taps_out[0, offset : offset + 1, at] = lefts[10 + offset : 11 + offset]
            taps_out[1, offset : offset + 1, at] = rights[10 + offset : 11 + offset]
            taps_out[2, offset : offset + 1, at] = rights[13 + offset : 14 + offset]
        skip_out[0:1, at] = lefts[13:14]
        back_edge, mixed_edge = lefts[2:4], rights[2:4]
        convs, edges = [], []
        for stream, (source, end, row) in enumerate(
            ((query_ref, ends[0], 0), (key_ref, ends[1], 0), (value_ref, ends[1], 2))
        ):
            now = source[:, at].astype(jnp.float32)
            before[stream, 6:8, :] = end[row : row + 2]
            before[stream, pl.ds(8, rows), :] = now
            before[stream, pl.ds(8 + rows, 2), :] = end[row + 4 : row + 6]
            conv = taps[stream][0:1] * now
            edge = taps[stream][0:1] * end[row + 4 : row + 6]
            for offset in (1, 2):
                weight = taps[stream][offset : offset + 1]
                conv = conv + weight * before[stream, pl.ds(8 - offset, rows), :]
                edge = edge + weight * before[stream, pl.ds(8 + rows - offset, 2), :]
            convs.append(conv)
            edges.append(edge)
        cotangent = cot_ref[:, at].astype(jnp.float32)
        cot_edge = ends[0][6:8]
        gated_out[:, at] = (convs[0] * mixed).astype(jnp.bfloat16)
        for stream, (out, grad, edge) in enumerate(
            (
                (query_out, cotangent * mixed, cot_edge * mixed_edge),
                (key_out, back * convs[2], back_edge * edges[2]),
                (value_out, back * convs[1], back_edge * edges[1]),
            )
        ):
            after[stream, pl.ds(0, rows), :] = grad
            after[stream, pl.ds(rows, 2), :] = edge
            total = taps[stream][0:1] * grad
            for offset in (1, 2):
                weight = taps[stream][offset : offset + 1]
                total = total + weight * after[stream, pl.ds(offset, rows), :]
            out[:, at] = total.astype(jnp.bfloat16)
        return 0

    loop(channels // LANES, one_tile, 0, len(in_refs) > 1)


def finish(received, streams, cotangent):
    rows, channels = cotangent.shape
    count = len(received)
    low = jax.ShapeDtypeStruct((rows, channels), jnp.bfloat16)

    def kernel(*refs):
        finish_kernel(refs[:count], *refs[count:])

    return pl.pallas_call(
        kernel,
        out_shape=(
            low,
            low,
            low,
            low,
            jax.ShapeDtypeStruct((rows, channels), jnp.float32),
            jax.ShapeDtypeStruct((3, 3, channels), jnp.float32),
            jax.ShapeDtypeStruct((1, channels), jnp.float32),
        ),
        scratch_shapes=[
            pltpu.VMEM((3, rows + 16, LANES), jnp.float32),
            pltpu.VMEM((3, rows + 8, LANES), jnp.float32),
        ],
        compiler_params=pltpu.CompilerParams(
            vmem_limit_bytes=3 * (channels // HALF) * MEBIBYTE // 2
        ),
    )(*in_order(received), *streams, cotangent)


def operator_kernel(
    pieces, out_refs, forward_ref, inverse_ref, taps_ref,
    ends, starts, edged, first_ref, second_ref, fields, spectra, filters, rhs, rhs_back,
    shared, misc,
):
    in_refs = by_index(pieces)
    blocks = fields.shape[0]
    place = lax.axis_index("seq")
    rows = forward_ref.shape[0] // 2
    half = blocks // 2
    half_rows = rows // 2
    unrolled = len(in_refs) > 1
    grad_scale = 1.0 / math.sqrt(blocks * rows)
    left = left_lanes((rows, LANES))
    left_half = left_lanes((half_rows, LANES))
    taps = taps_ref[...]
    query_taps = [taps[i : i + 1] for i in range(3)]
    value_taps = [taps[3 + i : 4 + i] for i in range(3)]
    gain = taps[6:7]
    nothing = jnp.zeros((8, LANES), jnp.float32)

    def lay(buffer, side, place, value):
        head, tail = head_tail(value)
        count = value.shape[0]
        at = pl.ds(side * LANES, LANES)
        rhs[buffer, pl.ds(place, count), at] = head
        rhs[buffer, pl.ds(rows + place, count), at] = tail
        rhs[buffer, pl.ds(2 * rows + place, count), at] = head

    def transformed(buffer):
        return jnp.dot(forward_ref[...], rhs[buffer], preferred_element_type=jnp.float32)

    def keep_ends(index, _):
        ref = piece(in_refs, index, place)
        block = index ^ place
        for stream in (0, 1):
            start = stream * rows
            last = ref[pl.ds(start + rows - 16, 16), :].astype(jnp.float32)
            first = ref[pl.ds(start, 16), :].astype(jnp.float32)
            ends[block + 1, 2 * stream : 2 * stream + 2, :] = last[14:16]
            ends[block + 1, 2 * stream + 4 : 2 * stream + 6, :] = first[0:2]
        return 0

    ends[0] = nothing
    ends[blocks + 1] = nothing
    loop(blocks, keep_ends, 0, unrolled)

    def transform(pair, _):
        spot = 2 * pair if unrolled else 0
        for side in range(2):
            ref = piece(in_refs, 2 * pair + side, place)
            scale = ref[pl.ds(2 * rows + half_rows, 16), :].astype(jnp.float32)
            code = ref[pl.ds(2 * rows, half_rows), :].astype(jnp.float32)
            taken = decode(code, scale[0:1] + scale[8:9])
            turned = swap(taken)
            lay(spot, side, 0, jnp.where(left_half, taken, turned))
            lay(spot, side, half_rows, jnp.where(left_half, turned, taken))
        result = transformed(spot)
        for side in range(2):
            filters[(2 * pair + side) ^ place] = result[:, side * LANES : (side + 1) * LANES]
        for side in range(2):
            index = 2 * pair + side
            ref = piece(in_refs, index, place)
            outs = []
            for stream, weights in ((0, query_taps), (1, value_taps)):
                now = ref[pl.ds(stream * rows, rows), :].astype(jnp.float32)
                last = ends[index ^ place, 2 * stream : 2 * stream + 2, :]
                edged[index, stream, 6:8, :] = last
                edged[index, stream, pl.ds(8, rows), :] = now
                total = weights[0] * now
                for offset in (1, 2):
                    shifted = edged[index, stream, pl.ds(8 - offset, rows), :]
                    total = total + weights[offset] * shifted
                outs.append(total)
            first_ref[index] = outs[0]
            second_ref[index] = outs[1]
            field = outs[0] * outs[1]
            fields[index] = field
            lay(spot + 1, side, 0, field)
        result = transformed(spot + 1)
        for side in range(2):
            spectra[(2 * pair + side) ^ place] = result[:, side * LANES : (side + 1) * LANES]
        return 0

    loop(half, transform, 0, unrolled)

    chunk = 8
    left_chunk = left_lanes((chunk, LANES))
    conjugate = jnp.where(left_chunk, -1.0, 1.0)

    def products(pairs):
        one = two = three = None
        for (re, im, both), (join_re, join_less, join_more) in pairs:
            terms = join_re * both, re * join_less, im * join_more
            if one is None:
                one, two, three = terms
            else:
                one, two, three = one + terms[0], two + terms[1], three + terms[2]
        return one - three, one + two

    def spectral(step, sign):
        real_at = pl.ds(pl.multiple_of(step * chunk, chunk), chunk)
        imag_at = pl.ds(pl.multiple_of(rows + step * chunk, chunk), chunk)
        field_re = [spectra[block, real_at, :] for block in range(blocks)]
        field_im = [spectra[block, imag_at, :] for block in range(blocks)]

        def joined(re, im, block):
            if block == 0:
                return re[0], im[0]
            if sign > 0:
                return re[block] - im[block - 1], im[block] + re[block - 1]
            return re[block] + im[block - 1], im[block] - re[block - 1]

        turned = []
        for block in range(blocks):
            re = jnp.where(left_chunk, field_re[blocks - 1 - block], field_re[block])
            im = jnp.where(left_chunk, field_im[blocks - 1 - block], field_im[block])
            turned.append((re, im, re + im))
        filt_re = [filters[block, real_at, :] for block in range(blocks)]
        filt_im = [filters[block, imag_at, :] for block in range(blocks)]
        joins = []
        for block in range(blocks):
            re, im = joined(filt_re, filt_im, block)
            im = im * conjugate
            joins.append((re, im - re, re + im))
        outs = [
            products([(turned[block - lag], joins[lag]) for lag in range(block + 1)])
            for block in range(blocks)
        ]
        grads = []
        for block in range(blocks):
            re = jnp.where(left_chunk, field_re[block], swap(field_re[block]))
            im = jnp.where(left_chunk, field_im[block], swap(field_im[block]))
            grads.append((re, im, re + im))
        sums = [joined(field_re, field_im, block) for block in range(blocks)]
        joins = []
        for block in range(blocks):
            parts = []
            for part in range(2):
                far = sums[block - half][part] if block >= half else 0.0
                parts.append(jnp.where(left_chunk, swap(sums[block][part]), far))
            re, im = parts
            joins.append((re, -im - re, re - im))
        for block in range(blocks):
            for part, at in ((0, real_at), (1, imag_at)):
                spectra[block, at, :] = jnp.where(
                    left_chunk, outs[blocks - 1 - block][part], outs[block][part]
                )
        for lag in range(half):
            out = products([(grads[block], joins[block - lag]) for block in range(lag, blocks)])
            filters[lag, real_at, :] = out[0]
            filters[lag, imag_at, :] = out[1]

    def even(step, _):
        spectral(step, 1)
        return 0

    def odd(step, _):
        spectral(step, -1)
        return 0

    steps = rows // chunk
    lax.fori_loop(0, steps // 2, even, 0)
    lax.fori_loop(steps // 2, steps, odd, 0)

    def back(values, buffer):
        for side, value in enumerate(values):
            head, tail = head_tail(value)
            at = pl.ds(side * LANES, LANES)
            rhs_back[buffer, pl.ds(0, 2 * rows), at] = head
            rhs_back[buffer, pl.ds(2 * rows, 2 * rows), at] = tail
            rhs_back[buffer, pl.ds(4 * rows, 2 * rows), at] = head
        result = jnp.dot(inverse_ref[...], rhs_back[buffer], preferred_element_type=jnp.float32)
        return result[:, :LANES], result[:, LANES:]

    def filter_grads(pair, _):
        values = filters[2 * pair], filters[2 * pair + 1]
        for side, value in enumerate(back(values, pair if unrolled else 0)):
            filters[2 * pair + side, pl.ds(0, rows), :] = value * grad_scale
        return 0

    loop(half // 2, filter_grads, 0, unrolled)

    def fold(value):
        return jnp.sum(value.reshape(rows // 8, 8, LANES), axis=0)

    def outputs(pair, totals):
        values = [spectra[(2 * pair + side) ^ place] for side in range(2)]
        results = back(values, (half // 2 + pair) if unrolled else 0)
        for side, result in enumerate(results):
            index = 2 * pair + side
            block = index ^ place
            out_ref = piece(out_refs, index, place)
            field = fields[index]
            result = result + gain * field
            scale = scale_of(result)
            out_ref[pl.ds(0, rows), :] = encode(result, scale).astype(jnp.bfloat16)
            misc[index, 0:1, :] = scale
            starts[block] = result[:8]
            turned = swap(result)
            grads = (second_ref[index] * turned, first_ref[index] * turned)
            new_totals = []
            for stream in (0, 1):
                for offset in range(3):
                    earlier = edged[index, stream, pl.ds(8 - offset, rows), :]
                    total = totals[3 * stream + offset]
                    new_totals.append(total + fold(grads[stream] * earlier))
            new_totals.append(totals[6] + fold(field * swap(field)))
            totals = tuple(new_totals)

            upper_half = block // half
            value = filters[lax.rem(block, half), pl.ds(0, rows), :]
            halves = join(left_half, value[:half_rows], value[half_rows:], upper_half)
            scale = scale_of(halves)
            code = encode(halves, scale).astype(jnp.bfloat16)
            out_ref[pl.ds(rows, half_rows), :] = code
            misc[index, 1:2, :] = scale
        return totals

    starts[blocks] = nothing
    totals = loop(half, outputs, (nothing,) * 7, unrolled)
    sums = [grad_scale * jnp.sum(total, axis=0, keepdims=True) for total in totals]
    shared[0:6, :] = taps[0:6]
    for row in range(6):
        value = sums[row]
        if row == 3:
            value = jnp.where(left_lanes((1, LANES)), sums[6], value)
        shared[6 + row : 7 + row, :] = value

    def close(index, _):
        out_ref = piece(out_refs, index, place)
        block = index ^ place
        misc[index, 2:4, :] = starts[block + 1, 0:2, :]
        misc[index, 4:16, :] = shared[0:12, :]
        head, tail = head_tail(misc[index])
        here = rows + half_rows
        out_ref[pl.ds(here, MISC), :] = head
        out_ref[pl.ds(here + MISC, MISC), :] = tail
        near = jnp.concatenate([ends[block, 0:4, :], ends[block + 2, 4:8, :], nothing], axis=0)
        out_ref[pl.ds(here + 2 * MISC, ENDS), :] = near.astype(jnp.bfloat16)
        return 0

    loop(blocks, close, 0, unrolled)


def operator(taps, received, devices):
    count = len(received)
    blocks = devices
    rows = (received[0].shape[-2] - 16) * 2 // 5
    forward, inverse = transform_matrices(rows)
    wide = (blocks, rows, LANES)
    listed = count > 1

    def kernel(*refs):
        ins, (forward_ref, inverse_ref, taps_ref) = refs[:count], refs[count : count + 3]
        outs, scratch = refs[count + 3 : 2 * count + 3], refs[2 * count + 3 :]
        operator_kernel(ins, outs, forward_ref, inverse_ref, taps_ref, *scratch)

    return pl.pallas_call(
        kernel,
        out_shape=piece_shapes(devices, rows + rows // 2 + 2 * MISC + ENDS),
        scratch_shapes=[
            pltpu.VMEM((blocks + 2, 8, LANES), jnp.float32),
            pltpu.VMEM((blocks + 1, 8, LANES), jnp.float32),
            pltpu.VMEM((blocks, 2, rows + 8, LANES), jnp.float32),
            pltpu.VMEM(wide, jnp.float32),
            pltpu.VMEM(wide, jnp.float32),
            pltpu.VMEM(wide, jnp.float32),
            pltpu.VMEM((blocks, 2 * rows, LANES), jnp.float32),
            pltpu.VMEM((blocks, 2 * rows, LANES), jnp.float32),
            pltpu.VMEM((blocks if listed else 2, 3 * rows, 2 * LANES), jnp.bfloat16),
            pltpu.VMEM((3 * blocks // 4 if listed else 1, 6 * rows, 2 * LANES), jnp.bfloat16),
            pltpu.VMEM((16, LANES), jnp.float32),
            pltpu.VMEM((blocks, MISC, LANES), jnp.float32),
        ],
        compiler_params=pltpu.CompilerParams(
            vmem_limit_bytes=min(4 * blocks * MEBIBYTE, VMEM_BYTES)
        ),
    )(*in_order(received), jnp.asarray(forward), jnp.asarray(inverse), taps)


def own_taps(short_taps, skip_gain):
    places = lax.axis_size("seq")
    columns = lax.axis_size("chan")
    share = skip_gain.shape[0]

    def pair(one, two):
        fill = ((0, 0), (0, HALF - share))
        return jnp.concatenate([jnp.pad(one, fill), jnp.pad(two, fill)], axis=1)

    straight = jnp.concatenate([jnp.ones((1, share)), jnp.zeros((2, share))]).astype(jnp.float32)
    rows = jnp.concatenate(
        [
            pair(short_taps[0], short_taps[1]),
            pair(straight, short_taps[2]),
            pair(skip_gain[None], skip_gain[None]),
            jnp.zeros((1, LANES), jnp.float32),
        ]
    )
    route = [
        (flat, (flat % places) * columns + flat // places) for flat in range(places * columns)
    ]
    return lax.ppermute(rows, ("seq", "chan"), route)


def spread(value, devices):
    rows, channels = value.shape
    share = channels // devices
    if share == HALF:
        return value
    wide = jnp.pad(value.reshape(rows, devices, share), ((0, 0), (0, 0), (0, HALF - share)))
    return wide.reshape(rows, devices * HALF)


def gathered(value, share):
    if share == HALF:
        return value
    groups = value.reshape(*value.shape[:-1], value.shape[-1] // HALF, HALF)[..., :share]
    return groups.reshape(*value.shape[:-1], -1)


def per_device(query_rows, key_rows, value_rows, long_filter, short_taps, skip_gain, cotangent):
    devices = lax.axis_size("seq")
    share = query_rows.shape[1] // devices
    taps = own_taps(short_taps, skip_gain)
    streams = [spread(value, devices) for value in (query_rows, key_rows, value_rows)]
    upstream = spread(cotangent, devices)
    received = exchange(pack(streams, upstream, spread(long_filter, devices), devices))
    results = exchange(operator(taps, received, devices))
    outs = finish(results, streams, upstream)
    *outs, skip_grad = (gathered(value, share) for value in outs)
    return (*outs, skip_grad[0])


def solution(mesh):
    in_specs = (
        P("seq", "chan"),
        P("seq", "chan"),
        P("seq", "chan"),
        P("seq", "chan"),
        P(None, None, ("seq", "chan")),
        P(("seq", "chan")),
        P("seq", "chan"),
    )
    out_specs = (
        P("seq", "chan"),
        P("seq", "chan"),
        P("seq", "chan"),
        P("seq", "chan"),
        P("seq", "chan"),
        P(None, None, "chan"),
        P("chan"),
    )
    return jax.shard_map(
        per_device, mesh=mesh, in_specs=in_specs, out_specs=out_specs, check_vma=False
    )
```

time: 84.4 us -> 75.9 us (0.90)
  waiting for transfers between devices: 48.5 us -> 26.6 us
  starting transfers between devices: 17.7 us -> 30.4 us
  local copies, waits for them, and re-layouts: 0.13 us -> 2.41 us
  Pallas kernels: 16.9 us -> 15.5 us
    all_to_all x2 -> x0, waiting for transfers between devices: 43 us -> none  [the longest x1 31.4 us: per_device(): received = lax.all_to_all(sent, 'seq', 0, 0, tiled=True)]
    ppermute x2 -> x14, starting transfers between devices: 5.84 us -> 29.8 us  [exchange(): lax.ppermute(value, 'seq', [(one, one ^ index) for one in range(len(piece...]
    ppermute x2 -> x14, waiting for transfers between devices: 5.41 us -> 26.6 us  [exchange(): lax.ppermute(value, 'seq', [(one, one ^ index) for one in range(len(piece...]
    all_to_all x2 -> x0, starting transfers between devices: 11.2 us -> none  [the longest x1 7.4 us: per_device(): received = lax.all_to_all(sent, 'seq', 0, 0, tiled=True)]
    unnamed x22 -> x18, local copies, waits for them, and re-layouts: 0.06 us -> 1.62 us
    pallas_call x3, Pallas kernels: 16.9 us -> 15.5 us  [the longest x1 9.29 us: operator(): pl.pallas_call(kernel, out_shape=piece_shapes(devices, rows + rows // 2 +...]
  transfers between devices with their start and end apart: 5 -> 15, of which waited for: 3 -> 5; matrix products, arithmetic and copies ran while one was open for 0% -> 1% of each run, Pallas kernels for 0% -> 0%
where the time goes in v4:
time: 75.9 us; the launch traced here: 75.7 us
  starting transfers between devices  30.4 us (40%)
  waiting for transfers between devices  26.6 us (35%)
  Pallas kernels  15.5 us (20%)
  local copies, waits for them, and re-layouts  2.41 us (3%)
    ppermute x14, starting transfers between devices, exchange(): lax.ppermute(value, 'seq', [(one, one ^ index) for one in range(len(piece...  29.8 us
    ppermute x14, waiting for transfers between devices, exchange(): lax.ppermute(value, 'seq', [(one, one ^ index) for one in range(len(piece...  26.6 us
    pallas_call x1, Pallas kernels, operator(): pl.pallas_call(kernel, out_shape=piece_shapes(devices, rows + rows // 2 +...  9.29 us
    pallas_call x1, Pallas kernels, pack(): pl.pallas_call(pack_kernel, out_shape=piece_shapes(devices, 2 * rows + ro...  3.17 us
    pallas_call x1, Pallas kernels, finish(): pl.pallas_call(kernel, out_shape=(low, low, low, low, jax.ShapeDtypeStruc...  3 us
    unnamed x18, local copies, waits for them, and re-layouts  1.62 us
  transfers between devices with their start and end apart: 15, of which 5 were waited for; matrix products, arithmetic and copies ran while one was open for 1% of the time, Pallas kernels for 0%

profile of v4, /device:TPU:0, one launch (start us, length us, event | category | flops | bytes accessed | tf_op | source)
XLA Modules:
  0.0 75.7 jit_solution(9510139579510365626)
XLA Ops:
  0.6 0.0 copy-start.4
  0.6 0.0 copy-start.5
  0.7 3.2 %shard_map.144 = (bf16[656,128]{1,0:T(8,128)(2,1)}, bf16[656,128]{1,0:T(8,128)(2,1)}, bf16[656,128]{1,0:T(8,128)(2,1)}, bf16[656,128]{1,0:T(8,128)(2,1)}, bf16[6...) custom-call(bf16[256,512]{1,0:T(8,128)(2,1)} %refs_8_.2, ...), custom_call_target="tpu_custom_call" | custom-call | tf_op jit(solution)/shard_map/pallas_call | solution.py:142
  3.8 6.0 %collective-permute-start = (bf16[656,128]{1,0:T(8,128)(2,1)}, bf16[656,128]{1,0:T(8,128)(2,1)S(1)}, u32[]{:S(2)}, u32[]{:S(2)}) collective-permute-start(bf16[656,128]{1,0:T(8,128)(2,1)} %get-tuple-element.31), channel_id=1, source_target_pairs={{0,28},{4,24},{8,20},{12,16},{16,12},{20,8},{24,4},{28,0},{1,29},{... | collective-permute-start | bytes 503816 | tf_op jit(solution)/shard_map/ppermute | solution.py:84
  9.8 0.2 collective-permute-start.1
  10.0 0.7 slice_bitcast_fusion.2
  10.7 0.1 pad.6.clone
  10.8 0.7 copy-done.7
  11.5 0.0 copy-done.8
  11.5 0.1 maximum_maximum_fusion
  11.6 0.7 collective-permute-start.7
  12.2 2.4 %collective-permute-start.2 = (bf16[656,128]{1,0:T(8,128)(2,1)}, bf16[656,128]{1,0:T(8,128)(2,1)S(1)}, u32[]{:S(2)}, u32[]{:S(2)}) collective-permute-start(bf16[656,128]{1,0:T(8,128)(2,1)} %get-tuple-element.33), channel_id=1, source_target_pairs={{0,12},{4,8},{8,4},{12,0},{16,28},{20,24},{24,20},{28,16},{1,13},{... | collective-permute-start | bytes 503816 | tf_op jit(solution)/shard_map/ppermute | solution.py:84
  14.7 2.6 %collective-permute-start.3 = (bf16[656,128]{1,0:T(8,128)(2,1)}, bf16[656,128]{1,0:T(8,128)(2,1)S(1)}, u32[]{:S(2)}, u32[]{:S(2)}) collective-permute-start(bf16[656,128]{1,0:T(8,128)(2,1)} %get-tuple-element.34), channel_id=1, source_target_pairs={{0,8},{4,12},{8,0},{12,4},{16,24},{20,28},{24,16},{28,20},{1,9},{5... | collective-permute-start | bytes 503816 | tf_op jit(solution)/shard_map/ppermute | solution.py:84
  17.3 0.0 collective-permute-done.7.refs_10_
  17.3 3.1 %collective-permute-start.4 = (bf16[656,128]{1,0:T(8,128)(2,1)}, bf16[656,128]{1,0:T(8,128)(2,1)S(1)}, u32[]{:S(2)}, u32[]{:S(2)}) collective-permute-start(bf16[656,128]{1,0:T(8,128)(2,1)} %get-tuple-element.35), channel_id=1, source_target_pairs={{0,20},{4,16},{8,28},{12,24},{16,4},{20,0},{24,12},{28,8},{1,21},{... | collective-permute-start | bytes 503816 | tf_op jit(solution)/shard_map/ppermute | solution.py:84
  20.4 0.0 collective-permute-done.refs_1_
  20.4 4.0 %collective-permute-start.5 = (bf16[656,128]{1,0:T(8,128)(2,1)}, bf16[656,128]{1,0:T(8,128)(2,1)S(1)}, u32[]{:S(2)}, u32[]{:S(2)}) collective-permute-start(bf16[656,128]{1,0:T(8,128)(2,1)} %get-tuple-element.36), channel_id=1, source_target_pairs={{0,16},{4,20},{8,24},{12,28},{16,0},{20,4},{24,8},{28,12},{1,17},{... | collective-permute-start | bytes 503816 | tf_op jit(solution)/shard_map/ppermute | solution.py:84
  24.3 0.0 collective-permute-done.1.refs_2_
  24.3 1.5 %collective-permute-start.6 = (bf16[656,128]{1,0:T(8,128)(2,1)}, bf16[656,128]{1,0:T(8,128)(2,1)S(1)}, u32[]{:S(2)}, u32[]{:S(2)}) collective-permute-start(bf16[656,128]{1,0:T(8,128)(2,1)} %get-tuple-element.37), channel_id=1, source_target_pairs={{0,4},{4,0},{8,12},{12,8},{16,20},{20,16},{24,28},{28,24},{1,5},{5... | collective-permute-start | bytes 503816 | tf_op jit(solution)/shard_map/ppermute | solution.py:84
  25.9 0.0 collective-permute-done.2.refs_3_
  25.9 0.0 collective-permute-done.3.refs_4_
  25.9 3.1 %collective-permute-done.4.refs_5_ = bf16[656,128]{1,0:T(8,128)(2,1)S(1)} collective-permute-done((bf16[656,128]{1,0:T(8,128)(2,1)}, bf16[656,128]{1,0:T(8,128)(2,1)S(1)}, u32[]{:S(2)}, u32[]{:S(2)}) %collective-permute-start.4) | collective-permute-done | bytes 167968 | tf_op jit(solution)/shard_map/ppermute | solution.py:84
  29.0 10.4 %collective-permute-done.5.refs_6_ = bf16[656,128]{1,0:T(8,128)(2,1)S(1)} collective-permute-done((bf16[656,128]{1,0:T(8,128)(2,1)}, bf16[656,128]{1,0:T(8,128)(2,1)S(1)}, u32[]{:S(2)}, u32[]{:S(2)}) %collective-permute-start.5) | collective-permute-done | bytes 167968 | tf_op jit(solution)/shard_map/ppermute | solution.py:84
  39.4 0.0 collective-permute-done.6.refs_7_
  39.4 0.0 copy-done.4
  39.4 0.0 copy-done.5
  39.4 0.0 copy-start.6
  39.4 0.9 %copy-done.6 = bf16[656,128]{1,0:T(8,128)(2,1)S(1)} copy-done((bf16[656,128]{1,0:T(8,128)(2,1)S(1)}, bf16[656,128]{1,0:T(8,128)(2,1)}, u32[]{:S(2)}) %copy-start.6) | copy-done | bytes 167960
  40.3 9.3 %shard_map.145 = (bf16[432,128]{1,0:T(8,128)(2,1)S(1)}, bf16[432,128]{1,0:T(8,128)(2,1)S(1)}, bf16[432,128]{1,0:T(8,128)(2,1)S(1)}, bf16[432,128]{1,0:T(8,128)(2...) custom-call(bf16[656,128]{1,0:T(8,128)(2,1)S(1)} %copy-done.6, ...), custom_call_target="tpu_custom_call" | custom-call | tf_op jit(solution)/shard_map/pallas_call | solution.py:520
  49.6 4.0 %collective-permute-start.8 = (bf16[432,128]{1,0:T(8,128)(2,1)S(1)}, bf16[432,128]{1,0:T(8,128)(2,1)S(1)}, u32[]{:S(2)}, u32[]{:S(2)}) collective-permute-start(bf16[432,128]{1,0:T(8,128)(2,1)S(1)} %get-tuple-element.39), channel_id=1, source_target_pairs={{0,28},{4,24},{8,20},{12,16},{16,12},{20,8},{24,4},{28,0},{1,29},{... | collective-permute-start | bytes 331784 | tf_op jit(solution)/shard_map/ppermute | solution.py:84
  53.6 0.0 collective-permute-start.9
  53.6 0.0 collective-permute-start.10
  53.6 2.8 %collective-permute-start.11 = (bf16[432,128]{1,0:T(8,128)(2,1)S(1)}, bf16[432,128]{1,0:T(8,128)(2,1)S(1)}, u32[]{:S(2)}, u32[]{:S(2)}) collective-permute-start(bf16[432,128]{1,0:T(8,128)(2,1)S(1)} %get-tuple-element.42), channel_id=1, source_target_pairs={{0,8},{4,12},{8,0},{12,4},{16,24},{20,28},{24,16},{28,20},{1,9},{5... | collective-permute-start | bytes 331784 | tf_op jit(solution)/shard_map/ppermute | solution.py:84
  56.4 2.4 %collective-permute-start.12 = (bf16[432,128]{1,0:T(8,128)(2,1)S(1)}, bf16[432,128]{1,0:T(8,128)(2,1)S(1)}, u32[]{:S(2)}, u32[]{:S(2)}) collective-permute-start(bf16[432,128]{1,0:T(8,128)(2,1)S(1)} %get-tuple-element.43), channel_id=1, source_target_pairs={{0,20},{4,16},{8,28},{12,24},{16,4},{20,0},{24,12},{28,8},{1,21},{... | collective-permute-start | bytes 331784 | tf_op jit(solution)/shard_map/ppermute | solution.py:84
  58.9 0.0 collective-permute-done.8.refs_1_
  58.9 0.6 collective-permute-start.13
  59.5 1.8 %collective-permute-done.9.refs_2_ = bf16[432,128]{1,0:T(8,128)(2,1)S(1)} collective-permute-done((bf16[432,128]{1,0:T(8,128)(2,1)S(1)}, bf16[432,128]{1,0:T(8,128)(2,1)S(1)}, u32[]{:S(2)}, u32[]{:S(2)}) %collective-permute-start.9) | collective-permute-done | bytes 110624 | tf_op jit(solution)/shard_map/ppermute | solution.py:84
  61.3 0.1 collective-permute-start.14
  61.4 5.8 %collective-permute-done.10.refs_3_ = bf16[432,128]{1,0:T(8,128)(2,1)S(1)} collective-permute-done((bf16[432,128]{1,0:T(8,128)(2,1)S(1)}, bf16[432,128]{1,0:T(8,128)(2,1)S(1)}, u32[]{:S(2)}, u32[]{:S(2)}) %collective-permute-start.10) | collective-permute-done | bytes 110624 | tf_op jit(solution)/shard_map/ppermute | solution.py:84
  67.2 0.0 collective-permute-done.11.refs_4_
  67.2 0.0 collective-permute-done.12.refs_5_
  67.3 5.4 %collective-permute-done.13.refs_6_ = bf16[432,128]{1,0:T(8,128)(2,1)S(1)} collective-permute-done((bf16[432,128]{1,0:T(8,128)(2,1)S(1)}, bf16[432,128]{1,0:T(8,128)(2,1)S(1)}, u32[]{:S(2)}, u32[]{:S(2)}) %collective-permute-start.13) | collective-permute-done | bytes 110624 | tf_op jit(solution)/shard_map/ppermute | solution.py:84
  72.7 0.0 collective-permute-done.14.refs_7_
  72.7 0.0 copy-done
  72.7 0.0 copy-done.1
  72.7 0.0 copy-done.2
  72.7 0.0 copy-done.3
  72.7 3.0 %shard_map.146 = (bf16[256,512]{1,0:T(8,128)(2,1)}, bf16[256,512]{1,0:T(8,128)(2,1)}, bf16[256,512]{1,0:T(8,128)(2,1)}, bf16[256,512]{1,0:T(8,128)(2,1)}, f32[25...) custom-call(bf16[432,128]{1,0:T(8,128)(2,1)S(1)} %get-tuple-element.38.refs_0_, ...), custom_call_target="tpu_custom_call" | custom-call | tf_op jit(solution)/shard_map/pallas_call | solution.py:241
  (6 shorter events, 0.0 us)
Async XLA Ops:
  0.6 38.8 %copy-start.4 = (bf16[256,1536]{1,0:T(8,128)(2,1)S(1)}, bf16[256,1536]{1,0:T(8,128)(2,1)}, u32[]{:S(2)}) copy-start(bf16[256,1536]{1,0:T(8,128)(2,1)} %constant.10.clone.refs_9_) | copy-start | bytes 2359300
  0.6 38.8 %copy-start.5 = (bf16[512,768]{1,0:T(8,128)(2,1)S(1)}, bf16[512,768]{1,0:T(8,128)(2,1)}, u32[]{:S(2)}) copy-start(bf16[512,768]{1,0:T(8,128)(2,1)} %constant.3.clone.refs_8_) | copy-start | bytes 2359300
  3.8 16.5 %collective-permute-start = (bf16[656,128]{1,0:T(8,128)(2,1)}, bf16[656,128]{1,0:T(8,128)(2,1)S(1)}, u32[]{:S(2)}, u32[]{:S(2)}) collective-permute-start(bf16[656,128]{1,0:T(8,128)(2,1)} %get-tuple-element.31), channel_id=1, source_target_pairs={{0,28},{4,24},{8,20},{12,16},{16,12},{20,8},{24,4},{28,0},{1,29},{... | collective-permute-start | bytes 503816 | tf_op jit(solution)/shard_map/ppermute | solution.py:84
  9.8 14.5 %collective-permute-start.1 = (bf16[656,128]{1,0:T(8,128)(2,1)}, bf16[656,128]{1,0:T(8,128)(2,1)S(1)}, u32[]{:S(2)}, u32[]{:S(2)}) collective-permute-start(bf16[656,128]{1,0:T(8,128)(2,1)} %get-tuple-element.32), channel_id=1, source_target_pairs={{0,24},{4,28},{8,16},{12,20},{16,8},{20,12},{24,0},{28,4},{1,25},{... | collective-permute-start | bytes 503816 | tf_op jit(solution)/shard_map/ppermute | solution.py:84
  10.8 0.7 copy-start.7
  10.8 0.7 copy-start.8
  11.6 5.7 %collective-permute-start.7 = (f32[8,128]{1,0:T(8,128)S(1)}, f32[8,128]{1,0:T(8,128)S(1)}, u32[]{:S(2)}, u32[]{:S(2)}) collective-permute-start(f32[8,128]{1,0:T(8,128)S(1)} %maximum_maximum_fusion), channel_id=1, source_target_pairs={{0,0},{1,4},{2,8},{3,12},{4,16},{5,20},{6,24},{7,28},{8,1},{9,5},{... | collective-permute-start | bytes 12296 | tf_op jit(solution)/shard_map/ppermute | solution.py:564
  12.2 13.6 %collective-permute-start.2 = (bf16[656,128]{1,0:T(8,128)(2,1)}, bf16[656,128]{1,0:T(8,128)(2,1)S(1)}, u32[]{:S(2)}, u32[]{:S(2)}) collective-permute-start(bf16[656,128]{1,0:T(8,128)(2,1)} %get-tuple-element.33), channel_id=1, source_target_pairs={{0,12},{4,8},{8,4},{12,0},{16,28},{20,24},{24,20},{28,16},{1,13},{... | collective-permute-start | bytes 503816 | tf_op jit(solution)/shard_map/ppermute | solution.py:84
  14.7 11.2 %collective-permute-start.3 = (bf16[656,128]{1,0:T(8,128)(2,1)}, bf16[656,128]{1,0:T(8,128)(2,1)S(1)}, u32[]{:S(2)}, u32[]{:S(2)}) collective-permute-start(bf16[656,128]{1,0:T(8,128)(2,1)} %get-tuple-element.34), channel_id=1, source_target_pairs={{0,8},{4,12},{8,0},{12,4},{16,24},{20,28},{24,16},{28,20},{1,9},{5... | collective-permute-start | bytes 503816 | tf_op jit(solution)/shard_map/ppermute | solution.py:84
  17.3 11.7 %collective-permute-start.4 = (bf16[656,128]{1,0:T(8,128)(2,1)}, bf16[656,128]{1,0:T(8,128)(2,1)S(1)}, u32[]{:S(2)}, u32[]{:S(2)}) collective-permute-start(bf16[656,128]{1,0:T(8,128)(2,1)} %get-tuple-element.35), channel_id=1, source_target_pairs={{0,20},{4,16},{8,28},{12,24},{16,4},{20,0},{24,12},{28,8},{1,21},{... | collective-permute-start | bytes 503816 | tf_op jit(solution)/shard_map/ppermute | solution.py:84
  20.4 19.0 %collective-permute-start.5 = (bf16[656,128]{1,0:T(8,128)(2,1)}, bf16[656,128]{1,0:T(8,128)(2,1)S(1)}, u32[]{:S(2)}, u32[]{:S(2)}) collective-permute-start(bf16[656,128]{1,0:T(8,128)(2,1)} %get-tuple-element.36), channel_id=1, source_target_pairs={{0,16},{4,20},{8,24},{12,28},{16,0},{20,4},{24,8},{28,12},{1,17},{... | collective-permute-start | bytes 503816 | tf_op jit(solution)/shard_map/ppermute | solution.py:84
  24.3 15.1 %collective-permute-start.6 = (bf16[656,128]{1,0:T(8,128)(2,1)}, bf16[656,128]{1,0:T(8,128)(2,1)S(1)}, u32[]{:S(2)}, u32[]{:S(2)}) collective-permute-start(bf16[656,128]{1,0:T(8,128)(2,1)} %get-tuple-element.37), channel_id=1, source_target_pairs={{0,4},{4,0},{8,12},{12,8},{16,20},{20,16},{24,28},{28,24},{1,5},{5... | collective-permute-start | bytes 503816 | tf_op jit(solution)/shard_map/ppermute | solution.py:84
  39.4 0.9 %copy-start.6 = (bf16[656,128]{1,0:T(8,128)(2,1)S(1)}, bf16[656,128]{1,0:T(8,128)(2,1)}, u32[]{:S(2)}) copy-start(bf16[656,128]{1,0:T(8,128)(2,1)} %get-tuple-element.30.refs_0_) | copy-start | bytes 503812
  40.3 32.4 %copy-start = (bf16[256,512]{1,0:T(8,128)(2,1)S(1)}, bf16[256,512]{1,0:T(8,128)(2,1)}, u32[]{:S(2)}) copy-start(bf16[256,512]{1,0:T(8,128)(2,1)} %refs_8_.2) | copy-start | bytes 786436
  40.3 32.4 %copy-start.1 = (bf16[256,512]{1,0:T(8,128)(2,1)S(1)}, bf16[256,512]{1,0:T(8,128)(2,1)}, u32[]{:S(2)}) copy-start(bf16[256,512]{1,0:T(8,128)(2,1)} %refs_9_.2) | copy-start | bytes 786436
  40.3 32.4 %copy-start.2 = (bf16[256,512]{1,0:T(8,128)(2,1)S(1)}, bf16[256,512]{1,0:T(8,128)(2,1)}, u32[]{:S(2)}) copy-start(bf16[256,512]{1,0:T(8,128)(2,1)} %refs_10_.1) | copy-start | bytes 786436
  40.3 32.4 %copy-start.3 = (bf16[256,512]{1,0:T(8,128)(2,1)S(1)}, bf16[256,512]{1,0:T(8,128)(2,1)}, u32[]{:S(2)}) copy-start(bf16[256,512]{1,0:T(8,128)(2,1)} %refs_11_.1) | copy-start | bytes 786436
  49.6 9.3 %collective-permute-start.8 = (bf16[432,128]{1,0:T(8,128)(2,1)S(1)}, bf16[432,128]{1,0:T(8,128)(2,1)S(1)}, u32[]{:S(2)}, u32[]{:S(2)}) collective-permute-start(bf16[432,128]{1,0:T(8,128)(2,1)S(1)} %get-tuple-element.39), channel_id=1, source_target_pairs={{0,28},{4,24},{8,20},{12,16},{16,12},{20,8},{24,4},{28,0},{1,29},{... | collective-permute-start | bytes 331784 | tf_op jit(solution)/shard_map/ppermute | solution.py:84
  53.6 7.7 %collective-permute-start.9 = (bf16[432,128]{1,0:T(8,128)(2,1)S(1)}, bf16[432,128]{1,0:T(8,128)(2,1)S(1)}, u32[]{:S(2)}, u32[]{:S(2)}) collective-permute-start(bf16[432,128]{1,0:T(8,128)(2,1)S(1)} %get-tuple-element.40), channel_id=1, source_target_pairs={{0,24},{4,28},{8,16},{12,20},{16,8},{20,12},{24,0},{28,4},{1,25},{... | collective-permute-start | bytes 331784 | tf_op jit(solution)/shard_map/ppermute | solution.py:84
  53.6 13.6 %collective-permute-start.10 = (bf16[432,128]{1,0:T(8,128)(2,1)S(1)}, bf16[432,128]{1,0:T(8,128)(2,1)S(1)}, u32[]{:S(2)}, u32[]{:S(2)}) collective-permute-start(bf16[432,128]{1,0:T(8,128)(2,1)S(1)} %get-tuple-element.41), channel_id=1, source_target_pairs={{0,12},{4,8},{8,4},{12,0},{16,28},{20,24},{24,20},{28,16},{1,13},{... | collective-permute-start | bytes 331784 | tf_op jit(solution)/shard_map/ppermute | solution.py:84
  53.6 13.6 %collective-permute-start.11 = (bf16[432,128]{1,0:T(8,128)(2,1)S(1)}, bf16[432,128]{1,0:T(8,128)(2,1)S(1)}, u32[]{:S(2)}, u32[]{:S(2)}) collective-permute-start(bf16[432,128]{1,0:T(8,128)(2,1)S(1)} %get-tuple-element.42), channel_id=1, source_target_pairs={{0,8},{4,12},{8,0},{12,4},{16,24},{20,28},{24,16},{28,20},{1,9},{5... | collective-permute-start | bytes 331784 | tf_op jit(solution)/shard_map/ppermute | solution.py:84
  56.4 10.8 %collective-permute-start.12 = (bf16[432,128]{1,0:T(8,128)(2,1)S(1)}, bf16[432,128]{1,0:T(8,128)(2,1)S(1)}, u32[]{:S(2)}, u32[]{:S(2)}) collective-permute-start(bf16[432,128]{1,0:T(8,128)(2,1)S(1)} %get-tuple-element.43), channel_id=1, source_target_pairs={{0,20},{4,16},{8,28},{12,24},{16,4},{20,0},{24,12},{28,8},{1,21},{... | collective-permute-start | bytes 331784 | tf_op jit(solution)/shard_map/ppermute | solution.py:84
  58.9 13.8 %collective-permute-start.13 = (bf16[432,128]{1,0:T(8,128)(2,1)S(1)}, bf16[432,128]{1,0:T(8,128)(2,1)S(1)}, u32[]{:S(2)}, u32[]{:S(2)}) collective-permute-start(bf16[432,128]{1,0:T(8,128)(2,1)S(1)} %get-tuple-element.44), channel_id=1, source_target_pairs={{0,16},{4,20},{8,24},{12,28},{16,0},{20,4},{24,8},{28,12},{1,17},{... | collective-permute-start | bytes 331784 | tf_op jit(solution)/shard_map/ppermute | solution.py:84
  61.3 11.4 %collective-permute-start.14 = (bf16[432,128]{1,0:T(8,128)(2,1)S(1)}, bf16[432,128]{1,0:T(8,128)(2,1)S(1)}, u32[]{:S(2)}, u32[]{:S(2)}) collective-permute-start(bf16[432,128]{1,0:T(8,128)(2,1)S(1)} %get-tuple-element.45), channel_id=1, source_target_pairs={{0,4},{4,0},{8,12},{12,8},{16,20},{20,16},{24,28},{28,24},{1,5},{5... | collective-permute-start | bytes 331784 | tf_op jit(solution)/shard_map/ppermute | solution.py:84

commit v5 on v4

--- a/solution.py
+++ b/solution.py
@@ -17,7 +17,8 @@
 MEBIBYTE = 1024 * 1024
 VMEM_BYTES = 62 * MEBIBYTE
 LISTED = 8
-ORDER = (0, 7, 6, 3, 2, 5, 4, 1)
+OUT_ORDER = (0, 7, 6, 3, 2, 5, 4, 1)
+BACK_ORDER = (0, 7, 6, 4, 2, 5, 3, 1)
 
 
 def swap(value):
@@ -87,14 +88,14 @@
     return [pieces[0], *others]
 
 
-def in_order(pieces):
-    return [pieces[index] for index in ORDER] if len(pieces) > 1 else pieces
-
-
-def by_index(refs):
+def in_order(pieces, order):
+    return [pieces[index] for index in order] if len(pieces) > 1 else pieces
+
+
+def by_index(refs, order):
     if len(refs) == 1:
         return refs
-    return [refs[ORDER.index(index)] for index in range(len(refs))]
+    return [refs[order.index(index)] for index in range(len(refs))]
 
 
 def piece_shapes(devices, rows):
@@ -150,7 +151,7 @@
     pieces, query_ref, key_ref, value_ref, cot_ref, gated_out, query_out, key_out, value_out,
     filter_out, taps_out, skip_out, before, after,
 ):
-    in_refs = by_index(pieces)
+    in_refs = by_index(pieces, BACK_ORDER)
     rows, channels = query_ref.shape
     half = rows // 2
     place = lax.axis_index("seq")
@@ -256,7 +257,7 @@
         compiler_params=pltpu.CompilerParams(
             vmem_limit_bytes=3 * (channels // HALF) * MEBIBYTE // 2
         ),
-    )(*in_order(received), *streams, cotangent)
+    )(*in_order(received, BACK_ORDER), *streams, cotangent)
 
 
 def operator_kernel(
@@ -264,7 +265,7 @@
     ends, starts, edged, first_ref, second_ref, fields, spectra, filters, rhs, rhs_back,
     shared, misc,
 ):
-    in_refs = by_index(pieces)
+    in_refs = by_index(pieces, OUT_ORDER)
     blocks = fields.shape[0]
     place = lax.axis_index("seq")
     rows = forward_ref.shape[0] // 2
@@ -412,17 +413,20 @@
             filters[lag, real_at, :] = out[0]
             filters[lag, imag_at, :] = out[1]
 
-    def even(step, _):
-        spectral(step, 1)
-        return 0
-
-    def odd(step, _):
-        spectral(step, -1)
-        return 0
-
-    steps = rows // chunk
-    lax.fori_loop(0, steps // 2, even, 0)
-    lax.fori_loop(steps // 2, steps, odd, 0)
+    trips = rows // chunk // 4
+
+    def even(trip, _):
+        for part in range(2):
+            spectral(2 * trip + part, 1)
+        return 0
+
+    def odd(trip, _):
+        for part in range(2):
+            spectral(2 * trip + part, -1)
+        return 0
+
+    lax.fori_loop(0, trips, even, 0)
+    lax.fori_loop(trips, 2 * trips, odd, 0)
 
     def back(values, buffer):
         for side, value in enumerate(values):
@@ -537,10 +541,10 @@
         compiler_params=pltpu.CompilerParams(
             vmem_limit_bytes=min(4 * blocks * MEBIBYTE, VMEM_BYTES)
         ),
-    )(*in_order(received), jnp.asarray(forward), jnp.asarray(inverse), taps)
-
-
-def own_taps(short_taps, skip_gain):
+    )(*in_order(received, OUT_ORDER), jnp.asarray(forward), jnp.asarray(inverse), taps)
+
+
+def own_taps(short_taps, skip_gain, received):
     places = lax.axis_size("seq")
     columns = lax.axis_size("chan")
     share = skip_gain.shape[0]
@@ -561,7 +565,9 @@
     route = [
         (flat, (flat % places) * columns + flat // places) for flat in range(places * columns)
     ]
-    return lax.ppermute(rows, ("seq", "chan"), route)
+    if len(received) > 1:
+        rows, received[-1] = lax.optimization_barrier((rows, received[-1]))
+    return lax.ppermute(rows, ("seq", "chan"), route), received
 
 
 def spread(value, devices):
@@ -583,10 +589,10 @@
 def per_device(query_rows, key_rows, value_rows, long_filter, short_taps, skip_gain, cotangent):
     devices = lax.axis_size("seq")
     share = query_rows.shape[1] // devices
-    taps = own_taps(short_taps, skip_gain)
     streams = [spread(value, devices) for value in (query_rows, key_rows, value_rows)]
     upstream = spread(cotangent, devices)
     received = exchange(pack(streams, upstream, spread(long_filter, devices), devices))
+    taps, received = own_taps(short_taps, skip_gain, received)
     results = exchange(operator(taps, received, devices))
     outs = finish(results, streams, upstream)
     *outs, skip_grad = (gathered(value, share) for value in outs)

time: 75.9 us -> 72.3 us (0.953)
  waiting for transfers between devices: 26.6 us -> 20.4 us
  starting transfers between devices: 30.4 us -> 35 us
  Pallas kernels: 15.5 us -> 14.2 us
    ppermute x14, waiting for transfers between devices: 26.6 us -> 20.4 us  [exchange(): lax.ppermute(value, 'seq', [(one, one ^ index) for one in range(len(piece...]
    ppermute x14, starting transfers between devices: 29.8 us -> 34.4 us  [exchange(): lax.ppermute(value, 'seq', [(one, one ^ index) for one in range(len(piece...]
    pallas_call x1, Pallas kernels: 9.29 us -> 8.01 us  [operator(): pl.pallas_call(kernel, out_shape=piece_shapes(devices, rows + rows // 2 +...]
    unnamed x18 -> x20, local copies, waits for them, and re-layouts: 1.62 us -> 1.63 us
  transfers between devices with their start and end apart: 15 -> 15, of which waited for: 5 -> 4; matrix products, arithmetic and copies ran while one was open for 1% -> 0% of each run, Pallas kernels for 0% -> 0%
where the time goes in v5:
time: 72.3 us; the launch traced here: 72.2 us
  starting transfers between devices  35 us (48%)
  waiting for transfers between devices  20.4 us (28%)
  Pallas kernels  14.2 us (20%)
  local copies, waits for them, and re-layouts  1.7 us (2%)
  between operations  0.74 us (1%)
    ppermute x14, starting transfers between devices, exchange(): lax.ppermute(value, 'seq', [(one, one ^ index) for one in range(len(piece...  34.4 us
    ppermute x14, waiting for transfers between devices, exchange(): lax.ppermute(value, 'seq', [(one, one ^ index) for one in range(len(piece...  20.4 us
    pallas_call x1, Pallas kernels, operator(): pl.pallas_call(kernel, out_shape=piece_shapes(devices, rows + rows // 2 +...  8.01 us
    pallas_call x1, Pallas kernels, pack(): pl.pallas_call(pack_kernel, out_shape=piece_shapes(devices, 2 * rows + ro...  3.17 us
    pallas_call x1, Pallas kernels, finish(): pl.pallas_call(kernel, out_shape=(low, low, low, low, jax.ShapeDtypeStruc...  3 us
    unnamed x20, local copies, waits for them, and re-layouts  1.63 us
  transfers between devices with their start and end apart: 15, of which 4 were waited for; matrix products, arithmetic and copies ran while one was open for 0% of the time, Pallas kernels for 0%

profile of v5, /device:TPU:0, one launch (start us, length us, event | category | flops | bytes accessed | tf_op | source)
XLA Modules:
  0.0 72.2 jit_solution(4673170459997394662)
XLA Ops:
  0.6 0.0 copy-start.4
  0.6 0.0 copy-start.5
  0.7 3.2 %shard_map.144 = (bf16[656,128]{1,0:T(8,128)(2,1)}, bf16[656,128]{1,0:T(8,128)(2,1)}, bf16[656,128]{1,0:T(8,128)(2,1)}, bf16[656,128]{1,0:T(8,128)(2,1)}, bf16[6...) custom-call(bf16[256,512]{1,0:T(8,128)(2,1)} %refs_8_.2, ...), custom_call_target="tpu_custom_call" | custom-call | tf_op jit(solution)/shard_map/pallas_call | solution.py:143
  3.8 6.0 %collective-permute-start = (bf16[656,128]{1,0:T(8,128)(2,1)}, bf16[656,128]{1,0:T(8,128)(2,1)S(1)}, u32[]{:S(2)}, u32[]{:S(2)}) collective-permute-start(bf16[656,128]{1,0:T(8,128)(2,1)} %get-tuple-element.33), channel_id=1, source_target_pairs={{0,28},{4,24},{8,20},{12,16},{16,12},{20,8},{24,4},{28,0},{1,29},{... | collective-permute-start | bytes 503816 | tf_op jit(solution)/shard_map/ppermute | solution.py:85
  9.8 0.2 collective-permute-start.1
  10.0 0.0 collective-permute-start.2
  10.0 1.9 %collective-permute-start.3 = (bf16[656,128]{1,0:T(8,128)(2,1)}, bf16[656,128]{1,0:T(8,128)(2,1)S(1)}, u32[]{:S(2)}, u32[]{:S(2)}) collective-permute-start(bf16[656,128]{1,0:T(8,128)(2,1)} %get-tuple-element.37), channel_id=1, source_target_pairs={{0,8},{4,12},{8,0},{12,4},{16,24},{20,28},{24,16},{28,20},{1,9},{5... | collective-permute-start | bytes 503816 | tf_op jit(solution)/shard_map/ppermute | solution.py:85
  11.9 3.2 %collective-permute-start.4 = (bf16[656,128]{1,0:T(8,128)(2,1)}, bf16[656,128]{1,0:T(8,128)(2,1)S(1)}, u32[]{:S(2)}, u32[]{:S(2)}) collective-permute-start(bf16[656,128]{1,0:T(8,128)(2,1)} %get-tuple-element.38), channel_id=1, source_target_pairs={{0,20},{4,16},{8,28},{12,24},{16,4},{20,0},{24,12},{28,8},{1,21},{... | collective-permute-start | bytes 503816 | tf_op jit(solution)/shard_map/ppermute | solution.py:85
  15.1 0.1 pad.6.clone
  15.2 0.0 copy-done.7
  15.2 0.0 collective-permute-done.refs_1_
  15.2 8.5 %collective-permute-start.5 = (bf16[656,128]{1,0:T(8,128)(2,1)}, bf16[656,128]{1,0:T(8,128)(2,1)S(1)}, u32[]{:S(2)}, u32[]{:S(2)}) collective-permute-start(bf16[656,128]{1,0:T(8,128)(2,1)} %get-tuple-element.39), channel_id=1, source_target_pairs={{0,16},{4,20},{8,24},{12,28},{16,0},{20,4},{24,8},{28,12},{1,17},{... | collective-permute-start | bytes 503816 | tf_op jit(solution)/shard_map/ppermute | solution.py:85
  23.7 0.0 collective-permute-done.1.refs_2_
  23.7 1.4 %collective-permute-start.6 = (bf16[656,128]{1,0:T(8,128)(2,1)}, bf16[656,128]{1,0:T(8,128)(2,1)S(1)}, u32[]{:S(2)}, u32[]{:S(2)}) collective-permute-start(bf16[656,128]{1,0:T(8,128)(2,1)} %get-tuple-element.40), channel_id=1, source_target_pairs={{0,4},{4,0},{8,12},{12,8},{16,20},{20,16},{24,28},{28,24},{1,5},{5... | collective-permute-start | bytes 503816 | tf_op jit(solution)/shard_map/ppermute | solution.py:85
  25.1 0.7 copy-done.8
  25.8 0.0 copy-done.9
  25.8 0.1 maximum_maximum_fusion
  25.9 0.0 collective-permute-done.2.refs_3_
  25.9 0.7 collective-permute-start.7
  26.5 0.0 collective-permute-done.3.refs_4_
  26.5 9.5 %collective-permute-done.4.refs_5_ = bf16[656,128]{1,0:T(8,128)(2,1)S(1)} collective-permute-done((bf16[656,128]{1,0:T(8,128)(2,1)}, bf16[656,128]{1,0:T(8,128)(2,1)S(1)}, u32[]{:S(2)}, u32[]{:S(2)}) %collective-permute-start.4) | collective-permute-done | bytes 167968 | tf_op jit(solution)/shard_map/ppermute | solution.py:85
  36.0 2.8 %collective-permute-done.5.refs_6_ = bf16[656,128]{1,0:T(8,128)(2,1)S(1)} collective-permute-done((bf16[656,128]{1,0:T(8,128)(2,1)}, bf16[656,128]{1,0:T(8,128)(2,1)S(1)}, u32[]{:S(2)}, u32[]{:S(2)}) %collective-permute-start.5) | collective-permute-done | bytes 167968 | tf_op jit(solution)/shard_map/ppermute | solution.py:85
  38.8 0.0 collective-permute-done.6.refs_7_
  38.8 0.0 collective-permute-done.7.refs_10_
  38.8 0.0 copy-done.4
  38.8 0.0 copy-done.5
  38.8 0.0 copy-start.6
  38.8 0.9 %copy-done.6 = bf16[656,128]{1,0:T(8,128)(2,1)S(1)} copy-done((bf16[656,128]{1,0:T(8,128)(2,1)S(1)}, bf16[656,128]{1,0:T(8,128)(2,1)}, u32[]{:S(2)}) %copy-start.6) | copy-done | bytes 167960
  39.7 8.0 %shard_map.145 = (bf16[432,128]{1,0:T(8,128)(2,1)S(1)}, bf16[432,128]{1,0:T(8,128)(2,1)S(1)}, bf16[432,128]{1,0:T(8,128)(2,1)S(1)}, bf16[432,128]{1,0:T(8,128)(2...) custom-call(bf16[656,128]{1,0:T(8,128)(2,1)S(1)} %copy-done.6, ...), custom_call_target="tpu_custom_call" | custom-call | tf_op jit(solution)/shard_map/pallas_call | solution.py:524
  47.8 2.5 %collective-permute-start.8 = (bf16[432,128]{1,0:T(8,128)(2,1)S(1)}, bf16[432,128]{1,0:T(8,128)(2,1)S(1)}, u32[]{:S(2)}, u32[]{:S(2)}) collective-permute-start(bf16[432,128]{1,0:T(8,128)(2,1)S(1)} %get-tuple-element.43), channel_id=1, source_target_pairs={{0,28},{4,24},{8,20},{12,16},{16,12},{20,8},{24,4},{28,0},{1,29},{... | collective-permute-start | bytes 331784 | tf_op jit(solution)/shard_map/ppermute | solution.py:85
  50.3 1.2 %collective-permute-start.9 = (bf16[432,128]{1,0:T(8,128)(2,1)S(1)}, bf16[432,128]{1,0:T(8,128)(2,1)S(1)}, u32[]{:S(2)}, u32[]{:S(2)}) collective-permute-start(bf16[432,128]{1,0:T(8,128)(2,1)S(1)} %get-tuple-element.44), channel_id=1, source_target_pairs={{0,24},{4,28},{8,16},{12,20},{16,8},{20,12},{24,0},{28,4},{1,25},{... | collective-permute-start | bytes 331784 | tf_op jit(solution)/shard_map/ppermute | solution.py:85
  51.5 0.0 collective-permute-start.10
  51.5 3.2 %collective-permute-start.11 = (bf16[432,128]{1,0:T(8,128)(2,1)S(1)}, bf16[432,128]{1,0:T(8,128)(2,1)S(1)}, u32[]{:S(2)}, u32[]{:S(2)}) collective-permute-start(bf16[432,128]{1,0:T(8,128)(2,1)S(1)} %get-tuple-element.46), channel_id=1, source_target_pairs={{0,8},{4,12},{8,0},{12,4},{16,24},{20,28},{24,16},{28,20},{1,9},{5... | collective-permute-start | bytes 331784 | tf_op jit(solution)/shard_map/ppermute | solution.py:85
  54.6 0.8 %collective-permute-start.12 = (bf16[432,128]{1,0:T(8,128)(2,1)S(1)}, bf16[432,128]{1,0:T(8,128)(2,1)S(1)}, u32[]{:S(2)}, u32[]{:S(2)}) collective-permute-start(bf16[432,128]{1,0:T(8,128)(2,1)S(1)} %get-tuple-element.47), channel_id=1, source_target_pairs={{0,20},{4,16},{8,28},{12,24},{16,4},{20,0},{24,12},{28,8},{1,21},{... | collective-permute-start | bytes 331784 | tf_op jit(solution)/shard_map/ppermute | solution.py:85
  55.5 0.0 collective-permute-done.8.refs_1_
  55.5 5.5 %collective-permute-start.13 = (bf16[432,128]{1,0:T(8,128)(2,1)S(1)}, bf16[432,128]{1,0:T(8,128)(2,1)S(1)}, u32[]{:S(2)}, u32[]{:S(2)}) collective-permute-start(bf16[432,128]{1,0:T(8,128)(2,1)S(1)} %get-tuple-element.48), channel_id=1, source_target_pairs={{0,12},{4,8},{8,4},{12,0},{16,28},{20,24},{24,20},{28,16},{1,13},{... | collective-permute-start | bytes 331784 | tf_op jit(solution)/shard_map/ppermute | solution.py:85
  60.9 0.0 collective-permute-done.9.refs_2_
  60.9 0.0 collective-permute-start.14
  60.9 6.1 %collective-permute-done.10.refs_3_ = bf16[432,128]{1,0:T(8,128)(2,1)S(1)} collective-permute-done((bf16[432,128]{1,0:T(8,128)(2,1)S(1)}, bf16[432,128]{1,0:T(8,128)(2,1)S(1)}, u32[]{:S(2)}, u32[]{:S(2)}) %collective-permute-start.10) | collective-permute-done | bytes 110624 | tf_op jit(solution)/shard_map/ppermute | solution.py:85
  67.1 0.0 collective-permute-done.11.refs_4_
  67.1 2.1 %collective-permute-done.12.refs_5_ = bf16[432,128]{1,0:T(8,128)(2,1)S(1)} collective-permute-done((bf16[432,128]{1,0:T(8,128)(2,1)S(1)}, bf16[432,128]{1,0:T(8,128)(2,1)S(1)}, u32[]{:S(2)}, u32[]{:S(2)}) %collective-permute-start.12) | collective-permute-done | bytes 110624 | tf_op jit(solution)/shard_map/ppermute | solution.py:85
  69.1 0.0 collective-permute-done.13.refs_6_
  69.1 0.0 collective-permute-done.14.refs_7_
  69.1 0.0 copy-done
  69.1 0.0 copy-done.1
  69.1 0.0 copy-done.2
  69.2 0.0 copy-done.3
  69.2 3.0 %shard_map.146 = (bf16[256,512]{1,0:T(8,128)(2,1)}, bf16[256,512]{1,0:T(8,128)(2,1)}, bf16[256,512]{1,0:T(8,128)(2,1)}, bf16[256,512]{1,0:T(8,128)(2,1)}, f32[25...) custom-call(bf16[432,128]{1,0:T(8,128)(2,1)S(1)} %get-tuple-element.42.refs_0_, ...), custom_call_target="tpu_custom_call" | custom-call | tf_op jit(solution)/shard_map/pallas_call | solution.py:242
  (8 shorter events, 0.0 us)
Async XLA Ops:
  0.6 38.2 %copy-start.4 = (bf16[256,1536]{1,0:T(8,128)(2,1)S(1)}, bf16[256,1536]{1,0:T(8,128)(2,1)}, u32[]{:S(2)}) copy-start(bf16[256,1536]{1,0:T(8,128)(2,1)} %constant.10.clone.refs_9_) | copy-start | bytes 2359300
  0.6 38.1 %copy-start.5 = (bf16[512,768]{1,0:T(8,128)(2,1)S(1)}, bf16[512,768]{1,0:T(8,128)(2,1)}, u32[]{:S(2)}) copy-start(bf16[512,768]{1,0:T(8,128)(2,1)} %constant.3.clone.refs_8_) | copy-start | bytes 2359300
  3.8 11.3 %copy-start.7 = (f32[3,3,64]{2,1,0:T(4,128)S(1)}, f32[3,3,64]{2,1,0:T(4,128)}, u32[]{:S(2)}) copy-start(f32[3,3,64]{2,1,0:T(4,128)} %param.13) | copy-start | bytes 6916
  3.8 11.3 %collective-permute-start = (bf16[656,128]{1,0:T(8,128)(2,1)}, bf16[656,128]{1,0:T(8,128)(2,1)S(1)}, u32[]{:S(2)}, u32[]{:S(2)}) collective-permute-start(bf16[656,128]{1,0:T(8,128)(2,1)} %get-tuple-element.33), channel_id=1, source_target_pairs={{0,28},{4,24},{8,20},{12,16},{16,12},{20,8},{24,4},{28,0},{1,29},{... | collective-permute-start | bytes 503816 | tf_op jit(solution)/shard_map/ppermute | solution.py:85
  9.8 13.8 %collective-permute-start.1 = (bf16[656,128]{1,0:T(8,128)(2,1)}, bf16[656,128]{1,0:T(8,128)(2,1)S(1)}, u32[]{:S(2)}, u32[]{:S(2)}) collective-permute-start(bf16[656,128]{1,0:T(8,128)(2,1)} %get-tuple-element.35), channel_id=1, source_target_pairs={{0,24},{4,28},{8,16},{12,20},{16,8},{20,12},{24,0},{28,4},{1,25},{... | collective-permute-start | bytes 503816 | tf_op jit(solution)/shard_map/ppermute | solution.py:85
  10.0 15.8 %collective-permute-start.2 = (bf16[656,128]{1,0:T(8,128)(2,1)}, bf16[656,128]{1,0:T(8,128)(2,1)S(1)}, u32[]{:S(2)}, u32[]{:S(2)}) collective-permute-start(bf16[656,128]{1,0:T(8,128)(2,1)} %get-tuple-element.36), channel_id=1, source_target_pairs={{0,12},{4,8},{8,4},{12,0},{16,28},{20,24},{24,20},{28,16},{1,13},{... | collective-permute-start | bytes 503816 | tf_op jit(solution)/shard_map/ppermute | solution.py:85
  10.0 16.5 %collective-permute-start.3 = (bf16[656,128]{1,0:T(8,128)(2,1)}, bf16[656,128]{1,0:T(8,128)(2,1)S(1)}, u32[]{:S(2)}, u32[]{:S(2)}) collective-permute-start(bf16[656,128]{1,0:T(8,128)(2,1)} %get-tuple-element.37), channel_id=1, source_target_pairs={{0,8},{4,12},{8,0},{12,4},{16,24},{20,28},{24,16},{28,20},{1,9},{5... | collective-permute-start | bytes 503816 | tf_op jit(solution)/shard_map/ppermute | solution.py:85
  11.9 24.1 %collective-permute-start.4 = (bf16[656,128]{1,0:T(8,128)(2,1)}, bf16[656,128]{1,0:T(8,128)(2,1)S(1)}, u32[]{:S(2)}, u32[]{:S(2)}) collective-permute-start(bf16[656,128]{1,0:T(8,128)(2,1)} %get-tuple-element.38), channel_id=1, source_target_pairs={{0,20},{4,16},{8,28},{12,24},{16,4},{20,0},{24,12},{28,8},{1,21},{... | collective-permute-start | bytes 503816 | tf_op jit(solution)/shard_map/ppermute | solution.py:85
  15.2 23.6 %collective-permute-start.5 = (bf16[656,128]{1,0:T(8,128)(2,1)}, bf16[656,128]{1,0:T(8,128)(2,1)S(1)}, u32[]{:S(2)}, u32[]{:S(2)}) collective-permute-start(bf16[656,128]{1,0:T(8,128)(2,1)} %get-tuple-element.39), channel_id=1, source_target_pairs={{0,16},{4,20},{8,24},{12,28},{16,0},{20,4},{24,8},{28,12},{1,17},{... | collective-permute-start | bytes 503816 | tf_op jit(solution)/shard_map/ppermute | solution.py:85
  23.7 15.1 %collective-permute-start.6 = (bf16[656,128]{1,0:T(8,128)(2,1)}, bf16[656,128]{1,0:T(8,128)(2,1)S(1)}, u32[]{:S(2)}, u32[]{:S(2)}) collective-permute-start(bf16[656,128]{1,0:T(8,128)(2,1)} %get-tuple-element.40), channel_id=1, source_target_pairs={{0,4},{4,0},{8,12},{12,8},{16,20},{20,16},{24,28},{28,24},{1,5},{5... | collective-permute-start | bytes 503816 | tf_op jit(solution)/shard_map/ppermute | solution.py:85
  25.1 0.7 copy-start.8
  25.1 0.7 copy-start.9
  25.9 12.9 %collective-permute-start.7 = (f32[8,128]{1,0:T(8,128)S(1)}, f32[8,128]{1,0:T(8,128)S(1)}, u32[]{:S(2)}, u32[]{:S(2)}) collective-permute-start(f32[8,128]{1,0:T(8,128)S(1)} %maximum_maximum_fusion), channel_id=1, source_target_pairs={{0,0},{1,4},{2,8},{3,12},{4,16},{5,20},{6,24},{7,28},{8,1},{9,5},{... | collective-permute-start | bytes 12296 | tf_op jit(solution)/shard_map/ppermute | solution.py:570
  38.8 0.9 %copy-start.6 = (bf16[656,128]{1,0:T(8,128)(2,1)S(1)}, bf16[656,128]{1,0:T(8,128)(2,1)}, u32[]{:S(2)}) copy-start(bf16[656,128]{1,0:T(8,128)(2,1)} %get-tuple-element.32.refs_0_) | copy-start | bytes 503812
  39.7 29.4 %copy-start = (bf16[256,512]{1,0:T(8,128)(2,1)S(1)}, bf16[256,512]{1,0:T(8,128)(2,1)}, u32[]{:S(2)}) copy-start(bf16[256,512]{1,0:T(8,128)(2,1)} %refs_8_.2) | copy-start | bytes 786436
  39.7 29.4 %copy-start.1 = (bf16[256,512]{1,0:T(8,128)(2,1)S(1)}, bf16[256,512]{1,0:T(8,128)(2,1)}, u32[]{:S(2)}) copy-start(bf16[256,512]{1,0:T(8,128)(2,1)} %refs_9_.2) | copy-start | bytes 786436
  39.7 29.4 %copy-start.2 = (bf16[256,512]{1,0:T(8,128)(2,1)S(1)}, bf16[256,512]{1,0:T(8,128)(2,1)}, u32[]{:S(2)}) copy-start(bf16[256,512]{1,0:T(8,128)(2,1)} %refs_10_.1) | copy-start | bytes 786436
  39.7 29.4 %copy-start.3 = (bf16[256,512]{1,0:T(8,128)(2,1)S(1)}, bf16[256,512]{1,0:T(8,128)(2,1)}, u32[]{:S(2)}) copy-start(bf16[256,512]{1,0:T(8,128)(2,1)} %refs_11_.1) | copy-start | bytes 786436
  47.8 7.7 %collective-permute-start.8 = (bf16[432,128]{1,0:T(8,128)(2,1)S(1)}, bf16[432,128]{1,0:T(8,128)(2,1)S(1)}, u32[]{:S(2)}, u32[]{:S(2)}) collective-permute-start(bf16[432,128]{1,0:T(8,128)(2,1)S(1)} %get-tuple-element.43), channel_id=1, source_target_pairs={{0,28},{4,24},{8,20},{12,16},{16,12},{20,8},{24,4},{28,0},{1,29},{... | collective-permute-start | bytes 331784 | tf_op jit(solution)/shard_map/ppermute | solution.py:85
  50.3 10.7 %collective-permute-start.9 = (bf16[432,128]{1,0:T(8,128)(2,1)S(1)}, bf16[432,128]{1,0:T(8,128)(2,1)S(1)}, u32[]{:S(2)}, u32[]{:S(2)}) collective-permute-start(bf16[432,128]{1,0:T(8,128)(2,1)S(1)} %get-tuple-element.44), channel_id=1, source_target_pairs={{0,24},{4,28},{8,16},{12,20},{16,8},{20,12},{24,0},{28,4},{1,25},{... | collective-permute-start | bytes 331784 | tf_op jit(solution)/shard_map/ppermute | solution.py:85
  51.5 15.6 %collective-permute-start.10 = (bf16[432,128]{1,0:T(8,128)(2,1)S(1)}, bf16[432,128]{1,0:T(8,128)(2,1)S(1)}, u32[]{:S(2)}, u32[]{:S(2)}) collective-permute-start(bf16[432,128]{1,0:T(8,128)(2,1)S(1)} %get-tuple-element.45), channel_id=1, source_target_pairs={{0,16},{4,20},{8,24},{12,28},{16,0},{20,4},{24,8},{28,12},{1,17},{... | collective-permute-start | bytes 331784 | tf_op jit(solution)/shard_map/ppermute | solution.py:85
  51.5 15.6 %collective-permute-start.11 = (bf16[432,128]{1,0:T(8,128)(2,1)S(1)}, bf16[432,128]{1,0:T(8,128)(2,1)S(1)}, u32[]{:S(2)}, u32[]{:S(2)}) collective-permute-start(bf16[432,128]{1,0:T(8,128)(2,1)S(1)} %get-tuple-element.46), channel_id=1, source_target_pairs={{0,8},{4,12},{8,0},{12,4},{16,24},{20,28},{24,16},{28,20},{1,9},{5... | collective-permute-start | bytes 331784 | tf_op jit(solution)/shard_map/ppermute | solution.py:85
  54.6 14.5 %collective-permute-start.12 = (bf16[432,128]{1,0:T(8,128)(2,1)S(1)}, bf16[432,128]{1,0:T(8,128)(2,1)S(1)}, u32[]{:S(2)}, u32[]{:S(2)}) collective-permute-start(bf16[432,128]{1,0:T(8,128)(2,1)S(1)} %get-tuple-element.47), channel_id=1, source_target_pairs={{0,20},{4,16},{8,28},{12,24},{16,4},{20,0},{24,12},{28,8},{1,21},{... | collective-permute-start | bytes 331784 | tf_op jit(solution)/shard_map/ppermute | solution.py:85
  55.5 13.7 %collective-permute-start.13 = (bf16[432,128]{1,0:T(8,128)(2,1)S(1)}, bf16[432,128]{1,0:T(8,128)(2,1)S(1)}, u32[]{:S(2)}, u32[]{:S(2)}) collective-permute-start(bf16[432,128]{1,0:T(8,128)(2,1)S(1)} %get-tuple-element.48), channel_id=1, source_target_pairs={{0,12},{4,8},{8,4},{12,0},{16,28},{20,24},{24,20},{28,16},{1,13},{... | collective-permute-start | bytes 331784 | tf_op jit(solution)/shard_map/ppermute | solution.py:85
  60.9 8.2 %collective-permute-start.14 = (bf16[432,128]{1,0:T(8,128)(2,1)S(1)}, bf16[432,128]{1,0:T(8,128)(2,1)S(1)}, u32[]{:S(2)}, u32[]{:S(2)}) collective-permute-start(bf16[432,128]{1,0:T(8,128)(2,1)S(1)} %get-tuple-element.49), channel_id=1, source_target_pairs={{0,4},{4,0},{8,12},{12,8},{16,20},{20,16},{24,28},{28,24},{1,5},{5... | collective-permute-start | bytes 331784 | tf_op jit(solution)/shard_map/ppermute | solution.py:85

commit v6 on v5

--- a/solution.py
+++ b/solution.py
@@ -1,3 +1,4 @@
+import functools
 import math
 
 import jax
@@ -18,6 +19,7 @@
 VMEM_BYTES = 62 * MEBIBYTE
 LISTED = 8
 OUT_ORDER = (0, 7, 6, 3, 2, 5, 4, 1)
+PACK_STEPS = ((3,), (1, 2, 0))
 BACK_ORDER = (0, 7, 6, 4, 2, 5, 3, 1)
 
 
@@ -108,43 +110,88 @@
     return jnp.where(mask, pltpu.roll(one, side * HALF, 1), pltpu.roll(two, HALF - side * HALF, 1))
 
 
-def pack_kernel(query_ref, key_ref, value_ref, cot_ref, filter_ref, *out_refs):
-    rows, channels = query_ref.shape
+def pack_kernel(steps, *refs):
+    low_refs, filter_ref, refs = refs[:4], refs[4], refs[5:]
+    low, high, staged, in_sems, out_sems = refs[-5:]
+    out_refs = refs[:-5]
+    rows, channels = filter_ref.shape
     devices = channels // HALF
     half = rows // 2
     place = lax.axis_index("seq")
     left = left_lanes((rows, LANES))
     left_half = left_lanes((half, LANES))
-
-    def one_piece(index, _):
-        out_ref = piece(out_refs, index, place)
-        dest = index ^ place
-        side = lax.rem(dest, 2)
-        at = pl.ds(pl.multiple_of(dest // 2 * LANES, LANES), LANES)
-        for first, second, start in ((query_ref, key_ref, 0), (cot_ref, value_ref, rows)):
-            one = first[:, at].astype(jnp.float32)
-            two = second[:, at].astype(jnp.float32)
-            out_ref[pl.ds(start, rows), :] = join(left, one, two, side).astype(jnp.bfloat16)
-        upper = filter_ref[pl.ds(0, half), at]
-        lower = filter_ref[pl.ds(half, half), at]
-        pair = join(left_half, upper, lower, side)
-        scale = scale_of(pair)
-        out_ref[pl.ds(2 * rows, half), :] = encode(pair, scale).astype(jnp.bfloat16)
-        head, tail = head_tail(jnp.broadcast_to(scale, (8, LANES)))
-        both = jnp.concatenate([head.astype(jnp.float32), tail.astype(jnp.float32)], axis=0)
-        out_ref[pl.ds(2 * rows + half, 16), :] = both.astype(jnp.bfloat16)
-        return 0
-
-    loop(devices, one_piece, 0, len(out_refs) > 1)
+    copies = {}
+    for step in steps:
+        tile = step ^ (place // 2)
+        at = pl.ds(pl.multiple_of(tile * LANES, LANES), LANES)
+        pairs = [(ref.at[:, at], low.at[step, stream]) for stream, ref in enumerate(low_refs)]
+        pairs.append((filter_ref.at[:, at], high.at[step]))
+        copies[step] = [
+            pltpu.make_async_copy(source, target, in_sems.at[step, stream])
+            for stream, (source, target) in enumerate(pairs)
+        ]
+        for copy in copies[step]:
+            copy.start()
+    leaving = []
+    for step in steps:
+        for copy in copies[step]:
+            copy.wait()
+        for index in (2 * step + 1, 2 * step):
+            side = lax.rem(index ^ place, 2)
+            for first, second, start in ((0, 1, 0), (3, 2, rows)):
+                one = low[step, first].astype(jnp.float32)
+                two = low[step, second].astype(jnp.float32)
+                joined = join(left, one, two, side).astype(jnp.bfloat16)
+                staged[index, pl.ds(start, rows), :] = joined
+            pair = join(left_half, high[step, :half], high[step, half:], side)
+            scale = scale_of(pair)
+            staged[index, pl.ds(2 * rows, half), :] = encode(pair, scale).astype(jnp.bfloat16)
+            head, tail = head_tail(jnp.broadcast_to(scale, (8, LANES)))
+            both = jnp.concatenate([head.astype(jnp.float32), tail.astype(jnp.float32)], axis=0)
+            staged[index, pl.ds(2 * rows + half, 16), :] = both.astype(jnp.bfloat16)
+            if len(out_refs) == 1:
+                target = out_refs[0].at[index ^ place]
+            else:
+                target = out_refs[2 * steps.index(step) + index % 2]
+            leaving.append(pltpu.make_async_copy(staged.at[index], target, out_sems.at[index]))
+            leaving[-1].start()
+    for copy in leaving:
+        copy.wait()
+
+
+def pack_steps(arrays, devices, steps):
+    rows = arrays[-1].shape[0]
+    sent_rows = 2 * rows + rows // 2 + 16
+    shapes = piece_shapes(devices, sent_rows)
+    if len(shapes) > 1:
+        shapes = shapes[: 2 * len(steps)]
+    anywhere = pl.BlockSpec(memory_space=pl.ANY)
+    return pl.pallas_call(
+        functools.partial(pack_kernel, steps),
+        in_specs=[anywhere] * 5,
+        out_specs=[anywhere] * len(shapes),
+        out_shape=shapes,
+        scratch_shapes=[
+            pltpu.VMEM((devices // 2, 4, rows, LANES), jnp.bfloat16),
+            pltpu.VMEM((devices // 2, rows, LANES), jnp.float32),
+            pltpu.VMEM((devices, sent_rows, LANES), jnp.bfloat16),
+            pltpu.SemaphoreType.DMA((devices // 2, 5)),
+            pltpu.SemaphoreType.DMA((devices,)),
+        ],
+        compiler_params=pltpu.CompilerParams(vmem_limit_bytes=VMEM_BYTES),
+    )(*arrays)
 
 
 def pack(streams, cotangent, long_filter, devices):
-    rows = cotangent.shape[0]
-    return pl.pallas_call(
-        pack_kernel,
-        out_shape=piece_shapes(devices, 2 * rows + rows // 2 + 16),
-        compiler_params=pltpu.CompilerParams(vmem_limit_bytes=VMEM_BYTES),
-    )(*streams, cotangent, long_filter)
+    arrays = (*streams, cotangent, long_filter)
+    if devices != LISTED:
+        return pack_steps(arrays, devices, tuple(range(devices // 2)))
+    pieces = [None] * devices
+    for steps in PACK_STEPS:
+        made = pack_steps(arrays, devices, steps)
+        for at, step in enumerate(steps):
+            pieces[2 * step], pieces[2 * step + 1] = made[2 * at], made[2 * at + 1]
+    return pieces
 
 
 def finish_kernel(
@@ -470,7 +517,6 @@
                     earlier = edged[index, stream, pl.ds(8 - offset, rows), :]
                     total = totals[3 * stream + offset]
                     new_totals.append(total + fold(grads[stream] * earlier))
-            new_totals.append(totals[6] + fold(field * swap(field)))
             totals = tuple(new_totals)
 
             upper_half = block // half
@@ -483,13 +529,13 @@
         return totals
 
     starts[blocks] = nothing
-    totals = loop(half, outputs, (nothing,) * 7, unrolled)
+    totals = loop(half, outputs, (nothing,) * 6, unrolled)
     sums = [grad_scale * jnp.sum(total, axis=0, keepdims=True) for total in totals]
     shared[0:6, :] = taps[0:6]
     for row in range(6):
         value = sums[row]
         if row == 3:
-            value = jnp.where(left_lanes((1, LANES)), sums[6], value)
+            value = jnp.where(left_lanes((1, LANES)), filters[0, 0:1, :], value)
         shared[6 + row : 7 + row, :] = value
 
     def close(index, _):
@@ -566,7 +612,9 @@
         (flat, (flat % places) * columns + flat // places) for flat in range(places * columns)
     ]
     if len(received) > 1:
-        rows, received[-1] = lax.optimization_barrier((rows, received[-1]))
+        unit = jnp.ones((1, 1), jnp.bfloat16)
+        rows, unit, received[-1] = lax.optimization_barrier((rows, unit, received[-1]))
+        received[0] = received[0] * unit
     return lax.ppermute(rows, ("seq", "chan"), route), received
 
 

time: 72.3 us -> 70.5 us (0.975)
  starting transfers between devices: 35 us -> 31.3 us
  Pallas kernels: 14.2 us -> 16.2 us
  other arithmetic: 0.08 us -> 1.01 us
  local copies, waits for them, and re-layouts: 1.7 us -> 0.8 us
    ppermute x14, starting transfers between devices: 34.4 us -> 30.7 us  [exchange(): lax.ppermute(value, 'seq', [(one, one ^ index) for one in range(len(piece...]
    pallas_call x1 -> x2, Pallas kernels: 3.17 us -> 5.26 us  [pack_steps(): pl.pallas_call(functools.partial(pack_kernel, steps), in_specs=[anywhere]...]
    mul x0 -> x1, other arithmetic: none -> 0.93 us  [own_taps(): received[0] = received[0] * unit]
    unnamed x20 -> x18, local copies, waits for them, and re-layouts: 1.63 us -> 0.72 us
  transfers between devices with their start and end apart: 15 -> 15, of which waited for: 4 -> 4; matrix products, arithmetic and copies ran while one was open for 0% -> 2% of each run, Pallas kernels for 0% -> 4%
where the time goes in v6:
time: 70.5 us; the launch traced here: 70.3 us
  starting transfers between devices  31.3 us (44%)
  waiting for transfers between devices  20.2 us (29%)
  Pallas kernels  16.2 us (23%)
  other arithmetic  1.01 us (1%)
  local copies, waits for them, and re-layouts  0.8 us (1%)
  between operations  0.77 us (1%)
    ppermute x14, starting transfers between devices, exchange(): lax.ppermute(value, 'seq', [(one, one ^ index) for one in range(len(piece...  30.7 us
    ppermute x14, waiting for transfers between devices, exchange(): lax.ppermute(value, 'seq', [(one, one ^ index) for one in range(len(piece...  20.2 us
    pallas_call x1, Pallas kernels, operator(): pl.pallas_call(kernel, out_shape=piece_shapes(devices, rows + rows // 2 +...  7.91 us
    pallas_call x2, Pallas kernels, pack_steps(): pl.pallas_call(functools.partial(pack_kernel, steps), in_specs=[anywhere]...  5.26 us
    pallas_call x1, Pallas kernels, finish(): pl.pallas_call(kernel, out_shape=(low, low, low, low, jax.ShapeDtypeStruc...  3 us
  transfers between devices with their start and end apart: 15, of which 4 were waited for; matrix products, arithmetic and copies ran while one was open for 2% of the time, Pallas kernels for 4%

profile of v6, /device:TPU:0, one launch (start us, length us, event | category | flops | bytes accessed | tf_op | source)
XLA Modules:
  0.0 70.3 jit_solution(862273926531362237)
XLA Ops:
  0.6 2.3 %shard_map.145 = (bf16[656,128]{1,0:T(8,128)(2,1)}, bf16[656,128]{1,0:T(8,128)(2,1)}) custom-call(bf16[256,512]{1,0:T(8,128)(2,1)} %refs_8_.2, bf16[256,512]{1,0:T(8,128)(2,1)} %refs_9_.2, bf16[256,512]{1,0:T(8,128)(2,1)} %refs_10_.1, bf16[256,512]{1,0:T(8,128)(2,1)} %refs_11_.1, f32[256,512]{1,0:T(8,128)} %refs_4_.3), custom_call_target="tpu_custom_call" | custom-call | tf_op jit(solution)/shard_map/pallas_call | solution.py:169
  2.9 6.0 %collective-permute-start = (bf16[656,128]{1,0:T(8,128)(2,1)}, bf16[656,128]{1,0:T(8,128)(2,1)S(1)}, u32[]{:S(2)}, u32[]{:S(2)}) collective-permute-start(bf16[656,128]{1,0:T(8,128)(2,1)} %get-tuple-element.34), channel_id=1, source_target_pairs={{0,28},{4,24},{8,20},{12,16},{16,12},{20,8},{24,4},{28,0},{1,29},{... | collective-permute-start | bytes 503816 | tf_op jit(solution)/shard_map/ppermute | solution.py:87
  9.0 0.2 collective-permute-start.1
  9.2 3.0 %shard_map.144 = (bf16[656,128]{1,0:T(8,128)(2,1)}, bf16[656,128]{1,0:T(8,128)(2,1)}, bf16[656,128]{1,0:T(8,128)(2,1)}, bf16[656,128]{1,0:T(8,128)(2,1)}, bf16[6...) custom-call(bf16[256,512]{1,0:T(8,128)(2,1)} %refs_8_.2, bf16[256,512]{1,0:T(8,128)(2,1)} %refs_9_.2, ...), custom_call_target="tpu_custom_call" | custom-call | tf_op jit(solution)/shard_map/pallas_call | solution.py:169
  12.2 0.1 collective-permute-start.2
  12.3 1.9 %collective-permute-start.3 = (bf16[656,128]{1,0:T(8,128)(2,1)}, bf16[656,128]{1,0:T(8,128)(2,1)S(1)}, u32[]{:S(2)}, u32[]{:S(2)}) collective-permute-start(bf16[656,128]{1,0:T(8,128)(2,1)} %get-tuple-element.39), channel_id=1, source_target_pairs={{0,8},{4,12},{8,0},{12,4},{16,24},{20,28},{24,16},{28,20},{1,9},{5... | collective-permute-start | bytes 503816 | tf_op jit(solution)/shard_map/ppermute | solution.py:87
  14.1 3.1 %collective-permute-start.4 = (bf16[656,128]{1,0:T(8,128)(2,1)}, bf16[656,128]{1,0:T(8,128)(2,1)S(1)}, u32[]{:S(2)}, u32[]{:S(2)}) collective-permute-start(bf16[656,128]{1,0:T(8,128)(2,1)} %get-tuple-element.40), channel_id=1, source_target_pairs={{0,20},{4,16},{8,28},{12,24},{16,4},{20,0},{24,12},{28,8},{1,21},{... | collective-permute-start | bytes 503816 | tf_op jit(solution)/shard_map/ppermute | solution.py:87
  17.2 0.0 copy-done.6
  17.2 0.1 pad.6.clone
  17.3 0.7 copy-done.7
  18.0 0.0 copy-done.8
  18.0 0.1 maximum_maximum_fusion
  18.0 0.0 collective-permute-done.refs_1_
  18.0 4.8 %collective-permute-start.5 = (bf16[656,128]{1,0:T(8,128)(2,1)}, bf16[656,128]{1,0:T(8,128)(2,1)S(1)}, u32[]{:S(2)}, u32[]{:S(2)}) collective-permute-start(bf16[656,128]{1,0:T(8,128)(2,1)} %get-tuple-element.41), channel_id=1, source_target_pairs={{0,16},{4,20},{8,24},{12,28},{16,0},{20,4},{24,8},{28,12},{1,17},{... | collective-permute-start | bytes 503816 | tf_op jit(solution)/shard_map/ppermute | solution.py:87
  22.8 0.0 collective-permute-done.1.refs_2_
  22.8 1.4 %collective-permute-start.6 = (bf16[656,128]{1,0:T(8,128)(2,1)}, bf16[656,128]{1,0:T(8,128)(2,1)S(1)}, u32[]{:S(2)}, u32[]{:S(2)}) collective-permute-start(bf16[656,128]{1,0:T(8,128)(2,1)} %get-tuple-element.42), channel_id=1, source_target_pairs={{0,4},{4,0},{8,12},{12,8},{16,20},{20,16},{24,28},{28,24},{1,5},{5... | collective-permute-start | bytes 503816 | tf_op jit(solution)/shard_map/ppermute | solution.py:87
  24.2 0.0 collective-permute-done.2.refs_3_
  24.2 0.7 collective-permute-start.7
  24.9 0.9 %broadcast_multiply_fusion.refs_0_ = bf16[656,128]{1,0:T(8,128)(2,1)S(1)} fusion(bf16[656,128]{1,0:T(8,128)(2,1)} %get-tuple-element.33, bf16[]{:T(256)} %bitcast.4), kind=kLoop, calls=%fused_computation | loop fusion | flops 83968 | bytes 335874 | tf_op jit(solution)/shard_map/mul | solution.py:617
  25.8 0.0 copy-start
  25.8 0.0 copy-start.1
  25.9 0.0 copy-start.2
  25.9 0.0 copy-start.3
  25.9 0.0 collective-permute-done.3.refs_4_
  25.9 9.3 %collective-permute-done.4.refs_5_ = bf16[656,128]{1,0:T(8,128)(2,1)S(1)} collective-permute-done((bf16[656,128]{1,0:T(8,128)(2,1)}, bf16[656,128]{1,0:T(8,128)(2,1)S(1)}, u32[]{:S(2)}, u32[]{:S(2)}) %collective-permute-start.4) | collective-permute-done | bytes 167968 | tf_op jit(solution)/shard_map/ppermute | solution.py:87
  35.1 2.8 %collective-permute-done.5.refs_6_ = bf16[656,128]{1,0:T(8,128)(2,1)S(1)} collective-permute-done((bf16[656,128]{1,0:T(8,128)(2,1)}, bf16[656,128]{1,0:T(8,128)(2,1)S(1)}, u32[]{:S(2)}, u32[]{:S(2)}) %collective-permute-start.5) | collective-permute-done | bytes 167968 | tf_op jit(solution)/shard_map/ppermute | solution.py:87
  37.9 0.0 collective-permute-done.6.refs_7_
  37.9 0.0 collective-permute-done.7.refs_10_
  37.9 0.0 copy-done.4
  37.9 0.0 copy-done.5
  37.9 7.9 %shard_map.146 = (bf16[432,128]{1,0:T(8,128)(2,1)S(1)}, bf16[432,128]{1,0:T(8,128)(2,1)S(1)}, bf16[432,128]{1,0:T(8,128)(2,1)S(1)}, bf16[432,128]{1,0:T(8,128)(2...) custom-call(bf16[656,128]{1,0:T(8,128)(2,1)S(1)} %broadcast_multiply, ...), custom_call_target="tpu_custom_call" | custom-call | tf_op jit(solution)/shard_map/pallas_call | solution.py:570
  45.9 2.5 %collective-permute-start.8 = (bf16[432,128]{1,0:T(8,128)(2,1)S(1)}, bf16[432,128]{1,0:T(8,128)(2,1)S(1)}, u32[]{:S(2)}, u32[]{:S(2)}) collective-permute-start(bf16[432,128]{1,0:T(8,128)(2,1)S(1)} %get-tuple-element.45), channel_id=1, source_target_pairs={{0,28},{4,24},{8,20},{12,16},{16,12},{20,8},{24,4},{28,0},{1,29},{... | collective-permute-start | bytes 331784 | tf_op jit(solution)/shard_map/ppermute | solution.py:87
  48.4 1.2 %collective-permute-start.9 = (bf16[432,128]{1,0:T(8,128)(2,1)S(1)}, bf16[432,128]{1,0:T(8,128)(2,1)S(1)}, u32[]{:S(2)}, u32[]{:S(2)}) collective-permute-start(bf16[432,128]{1,0:T(8,128)(2,1)S(1)} %get-tuple-element.46), channel_id=1, source_target_pairs={{0,24},{4,28},{8,16},{12,20},{16,8},{20,12},{24,0},{28,4},{1,25},{... | collective-permute-start | bytes 331784 | tf_op jit(solution)/shard_map/ppermute | solution.py:87
  49.6 0.0 collective-permute-start.10
  49.6 3.2 %collective-permute-start.11 = (bf16[432,128]{1,0:T(8,128)(2,1)S(1)}, bf16[432,128]{1,0:T(8,128)(2,1)S(1)}, u32[]{:S(2)}, u32[]{:S(2)}) collective-permute-start(bf16[432,128]{1,0:T(8,128)(2,1)S(1)} %get-tuple-element.48), channel_id=1, source_target_pairs={{0,8},{4,12},{8,0},{12,4},{16,24},{20,28},{24,16},{28,20},{1,9},{5... | collective-permute-start | bytes 331784 | tf_op jit(solution)/shard_map/ppermute | solution.py:87
  52.8 0.8 %collective-permute-start.12 = (bf16[432,128]{1,0:T(8,128)(2,1)S(1)}, bf16[432,128]{1,0:T(8,128)(2,1)S(1)}, u32[]{:S(2)}, u32[]{:S(2)}) collective-permute-start(bf16[432,128]{1,0:T(8,128)(2,1)S(1)} %get-tuple-element.49), channel_id=1, source_target_pairs={{0,20},{4,16},{8,28},{12,24},{16,4},{20,0},{24,12},{28,8},{1,21},{... | collective-permute-start | bytes 331784 | tf_op jit(solution)/shard_map/ppermute | solution.py:87
  53.6 0.0 collective-permute-done.8.refs_1_
  53.6 5.5 %collective-permute-start.13 = (bf16[432,128]{1,0:T(8,128)(2,1)S(1)}, bf16[432,128]{1,0:T(8,128)(2,1)S(1)}, u32[]{:S(2)}, u32[]{:S(2)}) collective-permute-start(bf16[432,128]{1,0:T(8,128)(2,1)S(1)} %get-tuple-element.50), channel_id=1, source_target_pairs={{0,12},{4,8},{8,4},{12,0},{16,28},{20,24},{24,20},{28,16},{1,13},{... | collective-permute-start | bytes 331784 | tf_op jit(solution)/shard_map/ppermute | solution.py:87
  59.1 0.0 collective-permute-done.9.refs_2_
  59.1 0.0 collective-permute-start.14
  59.1 6.1 %collective-permute-done.10.refs_3_ = bf16[432,128]{1,0:T(8,128)(2,1)S(1)} collective-permute-done((bf16[432,128]{1,0:T(8,128)(2,1)S(1)}, bf16[432,128]{1,0:T(8,128)(2,1)S(1)}, u32[]{:S(2)}, u32[]{:S(2)}) %collective-permute-start.10) | collective-permute-done | bytes 110624 | tf_op jit(solution)/shard_map/ppermute | solution.py:87
  65.2 0.0 collective-permute-done.11.refs_4_
  65.2 2.0 %collective-permute-done.12.refs_5_ = bf16[432,128]{1,0:T(8,128)(2,1)S(1)} collective-permute-done((bf16[432,128]{1,0:T(8,128)(2,1)S(1)}, bf16[432,128]{1,0:T(8,128)(2,1)S(1)}, u32[]{:S(2)}, u32[]{:S(2)}) %collective-permute-start.12) | collective-permute-done | bytes 110624 | tf_op jit(solution)/shard_map/ppermute | solution.py:87
  67.2 0.0 collective-permute-done.13.refs_6_
  67.2 0.0 collective-permute-done.14.refs_7_
  67.2 0.0 copy-done
  67.2 0.0 copy-done.1
  67.3 3.0 %shard_map.147 = (bf16[256,512]{1,0:T(8,128)(2,1)}, bf16[256,512]{1,0:T(8,128)(2,1)}, bf16[256,512]{1,0:T(8,128)(2,1)}, bf16[256,512]{1,0:T(8,128)(2,1)}, f32[25...) custom-call(bf16[432,128]{1,0:T(8,128)(2,1)S(1)} %get-tuple-element.44.refs_0_, ...), custom_call_target="tpu_custom_call" | custom-call | tf_op jit(solution)/shard_map/pallas_call | solution.py:289
  (8 shorter events, 0.0 us)
Async XLA Ops:
  2.9 15.1 %collective-permute-start = (bf16[656,128]{1,0:T(8,128)(2,1)}, bf16[656,128]{1,0:T(8,128)(2,1)S(1)}, u32[]{:S(2)}, u32[]{:S(2)}) collective-permute-start(bf16[656,128]{1,0:T(8,128)(2,1)} %get-tuple-element.34), channel_id=1, source_target_pairs={{0,28},{4,24},{8,20},{12,16},{16,12},{20,8},{24,4},{28,0},{1,29},{... | collective-permute-start | bytes 503816 | tf_op jit(solution)/shard_map/ppermute | solution.py:87
  8.9 8.2 %copy-start.6 = (f32[3,3,64]{2,1,0:T(4,128)S(1)}, f32[3,3,64]{2,1,0:T(4,128)}, u32[]{:S(2)}) copy-start(f32[3,3,64]{2,1,0:T(4,128)} %param.13) | copy-start | bytes 6916
  8.9 29.0 %copy-start.4 = (bf16[256,1536]{1,0:T(8,128)(2,1)S(1)}, bf16[256,1536]{1,0:T(8,128)(2,1)}, u32[]{:S(2)}) copy-start(bf16[256,1536]{1,0:T(8,128)(2,1)} %constant.12.clone.refs_9_) | copy-start | bytes 2359300
  9.0 29.0 %copy-start.5 = (bf16[512,768]{1,0:T(8,128)(2,1)S(1)}, bf16[512,768]{1,0:T(8,128)(2,1)}, u32[]{:S(2)}) copy-start(bf16[512,768]{1,0:T(8,128)(2,1)} %constant.4.clone.refs_8_) | copy-start | bytes 2359300
  9.0 13.9 %collective-permute-start.1 = (bf16[656,128]{1,0:T(8,128)(2,1)}, bf16[656,128]{1,0:T(8,128)(2,1)S(1)}, u32[]{:S(2)}, u32[]{:S(2)}) collective-permute-start(bf16[656,128]{1,0:T(8,128)(2,1)} %get-tuple-element.37), channel_id=1, source_target_pairs={{0,24},{4,28},{8,16},{12,20},{16,8},{20,12},{24,0},{28,4},{1,25},{... | collective-permute-start | bytes 503816 | tf_op jit(solution)/shard_map/ppermute | solution.py:87
  12.2 12.1 %collective-permute-start.2 = (bf16[656,128]{1,0:T(8,128)(2,1)}, bf16[656,128]{1,0:T(8,128)(2,1)S(1)}, u32[]{:S(2)}, u32[]{:S(2)}) collective-permute-start(bf16[656,128]{1,0:T(8,128)(2,1)} %get-tuple-element.38), channel_id=1, source_target_pairs={{0,12},{4,8},{8,4},{12,0},{16,28},{20,24},{24,20},{28,16},{1,13},{... | collective-permute-start | bytes 503816 | tf_op jit(solution)/shard_map/ppermute | solution.py:87
  12.3 13.6 %collective-permute-start.3 = (bf16[656,128]{1,0:T(8,128)(2,1)}, bf16[656,128]{1,0:T(8,128)(2,1)S(1)}, u32[]{:S(2)}, u32[]{:S(2)}) collective-permute-start(bf16[656,128]{1,0:T(8,128)(2,1)} %get-tuple-element.39), channel_id=1, source_target_pairs={{0,8},{4,12},{8,0},{12,4},{16,24},{20,28},{24,16},{28,20},{1,9},{5... | collective-permute-start | bytes 503816 | tf_op jit(solution)/shard_map/ppermute | solution.py:87
  14.1 21.0 %collective-permute-start.4 = (bf16[656,128]{1,0:T(8,128)(2,1)}, bf16[656,128]{1,0:T(8,128)(2,1)S(1)}, u32[]{:S(2)}, u32[]{:S(2)}) collective-permute-start(bf16[656,128]{1,0:T(8,128)(2,1)} %get-tuple-element.40), channel_id=1, source_target_pairs={{0,20},{4,16},{8,28},{12,24},{16,4},{20,0},{24,12},{28,8},{1,21},{... | collective-permute-start | bytes 503816 | tf_op jit(solution)/shard_map/ppermute | solution.py:87
  17.3 0.7 copy-start.7
  17.3 0.7 copy-start.8
  18.0 19.9 %collective-permute-start.5 = (bf16[656,128]{1,0:T(8,128)(2,1)}, bf16[656,128]{1,0:T(8,128)(2,1)S(1)}, u32[]{:S(2)}, u32[]{:S(2)}) collective-permute-start(bf16[656,128]{1,0:T(8,128)(2,1)} %get-tuple-element.41), channel_id=1, source_target_pairs={{0,16},{4,20},{8,24},{12,28},{16,0},{20,4},{24,8},{28,12},{1,17},{... | collective-permute-start | bytes 503816 | tf_op jit(solution)/shard_map/ppermute | solution.py:87
  22.8 15.1 %collective-permute-start.6 = (bf16[656,128]{1,0:T(8,128)(2,1)}, bf16[656,128]{1,0:T(8,128)(2,1)S(1)}, u32[]{:S(2)}, u32[]{:S(2)}) collective-permute-start(bf16[656,128]{1,0:T(8,128)(2,1)} %get-tuple-element.42), channel_id=1, source_target_pairs={{0,4},{4,0},{8,12},{12,8},{16,20},{20,16},{24,28},{28,24},{1,5},{5... | collective-permute-start | bytes 503816 | tf_op jit(solution)/shard_map/ppermute | solution.py:87
  24.2 13.7 %collective-permute-start.7 = (f32[8,128]{1,0:T(8,128)S(1)}, f32[8,128]{1,0:T(8,128)S(1)}, u32[]{:S(2)}, u32[]{:S(2)}) collective-permute-start(f32[8,128]{1,0:T(8,128)S(1)} %maximum_maximum_fusion), channel_id=1, source_target_pairs={{0,0},{1,4},{2,8},{3,12},{4,16},{5,20},{6,24},{7,28},{8,1},{9,5},{... | collective-permute-start | bytes 12296 | tf_op jit(solution)/shard_map/ppermute | solution.py:618
  25.8 41.4 %copy-start = (bf16[256,512]{1,0:T(8,128)(2,1)S(1)}, bf16[256,512]{1,0:T(8,128)(2,1)}, u32[]{:S(2)}) copy-start(bf16[256,512]{1,0:T(8,128)(2,1)} %refs_8_.2) | copy-start | bytes 786436
  25.8 41.4 %copy-start.1 = (bf16[256,512]{1,0:T(8,128)(2,1)S(1)}, bf16[256,512]{1,0:T(8,128)(2,1)}, u32[]{:S(2)}) copy-start(bf16[256,512]{1,0:T(8,128)(2,1)} %refs_9_.2) | copy-start | bytes 786436
  25.9 41.4 %copy-start.2 = (bf16[256,512]{1,0:T(8,128)(2,1)S(1)}, bf16[256,512]{1,0:T(8,128)(2,1)}, u32[]{:S(2)}) copy-start(bf16[256,512]{1,0:T(8,128)(2,1)} %refs_10_.1) | copy-start | bytes 786436
  25.9 41.4 %copy-start.3 = (bf16[256,512]{1,0:T(8,128)(2,1)S(1)}, bf16[256,512]{1,0:T(8,128)(2,1)}, u32[]{:S(2)}) copy-start(bf16[256,512]{1,0:T(8,128)(2,1)} %refs_11_.1) | copy-start | bytes 786436
  45.9 7.7 %collective-permute-start.8 = (bf16[432,128]{1,0:T(8,128)(2,1)S(1)}, bf16[432,128]{1,0:T(8,128)(2,1)S(1)}, u32[]{:S(2)}, u32[]{:S(2)}) collective-permute-start(bf16[432,128]{1,0:T(8,128)(2,1)S(1)} %get-tuple-element.45), channel_id=1, source_target_pairs={{0,28},{4,24},{8,20},{12,16},{16,12},{20,8},{24,4},{28,0},{1,29},{... | collective-permute-start | bytes 331784 | tf_op jit(solution)/shard_map/ppermute | solution.py:87
  48.4 10.7 %collective-permute-start.9 = (bf16[432,128]{1,0:T(8,128)(2,1)S(1)}, bf16[432,128]{1,0:T(8,128)(2,1)S(1)}, u32[]{:S(2)}, u32[]{:S(2)}) collective-permute-start(bf16[432,128]{1,0:T(8,128)(2,1)S(1)} %get-tuple-element.46), channel_id=1, source_target_pairs={{0,24},{4,28},{8,16},{12,20},{16,8},{20,12},{24,0},{28,4},{1,25},{... | collective-permute-start | bytes 331784 | tf_op jit(solution)/shard_map/ppermute | solution.py:87
  49.6 15.6 %collective-permute-start.10 = (bf16[432,128]{1,0:T(8,128)(2,1)S(1)}, bf16[432,128]{1,0:T(8,128)(2,1)S(1)}, u32[]{:S(2)}, u32[]{:S(2)}) collective-permute-start(bf16[432,128]{1,0:T(8,128)(2,1)S(1)} %get-tuple-element.47), channel_id=1, source_target_pairs={{0,16},{4,20},{8,24},{12,28},{16,0},{20,4},{24,8},{28,12},{1,17},{... | collective-permute-start | bytes 331784 | tf_op jit(solution)/shard_map/ppermute | solution.py:87
  49.6 15.6 %collective-permute-start.11 = (bf16[432,128]{1,0:T(8,128)(2,1)S(1)}, bf16[432,128]{1,0:T(8,128)(2,1)S(1)}, u32[]{:S(2)}, u32[]{:S(2)}) collective-permute-start(bf16[432,128]{1,0:T(8,128)(2,1)S(1)} %get-tuple-element.48), channel_id=1, source_target_pairs={{0,8},{4,12},{8,0},{12,4},{16,24},{20,28},{24,16},{28,20},{1,9},{5... | collective-permute-start | bytes 331784 | tf_op jit(solution)/shard_map/ppermute | solution.py:87
  52.8 14.5 %collective-permute-start.12 = (bf16[432,128]{1,0:T(8,128)(2,1)S(1)}, bf16[432,128]{1,0:T(8,128)(2,1)S(1)}, u32[]{:S(2)}, u32[]{:S(2)}) collective-permute-start(bf16[432,128]{1,0:T(8,128)(2,1)S(1)} %get-tuple-element.49), channel_id=1, source_target_pairs={{0,20},{4,16},{8,28},{12,24},{16,4},{20,0},{24,12},{28,8},{1,21},{... | collective-permute-start | bytes 331784 | tf_op jit(solution)/shard_map/ppermute | solution.py:87
  53.6 13.7 %collective-permute-start.13 = (bf16[432,128]{1,0:T(8,128)(2,1)S(1)}, bf16[432,128]{1,0:T(8,128)(2,1)S(1)}, u32[]{:S(2)}, u32[]{:S(2)}) collective-permute-start(bf16[432,128]{1,0:T(8,128)(2,1)S(1)} %get-tuple-element.50), channel_id=1, source_target_pairs={{0,12},{4,8},{8,4},{12,0},{16,28},{20,24},{24,20},{28,16},{1,13},{... | collective-permute-start | bytes 331784 | tf_op jit(solution)/shard_map/ppermute | solution.py:87
  59.1 8.2 %collective-permute-start.14 = (bf16[432,128]{1,0:T(8,128)(2,1)S(1)}, bf16[432,128]{1,0:T(8,128)(2,1)S(1)}, u32[]{:S(2)}, u32[]{:S(2)}) collective-permute-start(bf16[432,128]{1,0:T(8,128)(2,1)S(1)} %get-tuple-element.51), channel_id=1, source_target_pairs={{0,4},{4,0},{8,12},{12,8},{16,20},{20,16},{24,28},{28,24},{1,5},{5... | collective-permute-start | bytes 331784 | tf_op jit(solution)/shard_map/ppermute | solution.py:87

commit v7 on v6

--- a/solution.py
+++ b/solution.py
@@ -20,7 +20,7 @@
 LISTED = 8
 OUT_ORDER = (0, 7, 6, 3, 2, 5, 4, 1)
 PACK_STEPS = ((3,), (1, 2, 0))
-BACK_ORDER = (0, 7, 6, 4, 2, 5, 3, 1)
+BACK_ORDER = (0, 7, 2, 5, 4, 6, 3, 1)
 
 
 def swap(value):

time: 70.5 us -> 68.7 us (0.974)
  starting transfers between devices: 31.3 us -> 27.4 us
  waiting for transfers between devices: 20.2 us -> 22.4 us
    ppermute x14, starting transfers between devices: 30.7 us -> 26.8 us  [exchange(): lax.ppermute(value, 'seq', [(one, one ^ index) for one in range(len(piece...]
    ppermute x14, waiting for transfers between devices: 20.2 us -> 22.4 us  [exchange(): lax.ppermute(value, 'seq', [(one, one ^ index) for one in range(len(piece...]
  transfers between devices with their start and end apart: 15 -> 15, of which waited for: 4 -> 6; matrix products, arithmetic and copies ran while one was open for 2% -> 2% of each run, Pallas kernels for 4% -> 4%
where the time goes in v7:
time: 68.7 us; the launch traced here: 68.5 us
  starting transfers between devices  27.4 us (40%)
  waiting for transfers between devices  22.4 us (33%)
  Pallas kernels  16.2 us (24%)
  other arithmetic  1.01 us (1%)
  local copies, waits for them, and re-layouts  0.8 us (1%)
  between operations  0.78 us (1%)
    ppermute x14, starting transfers between devices, exchange(): lax.ppermute(value, 'seq', [(one, one ^ index) for one in range(len(piece...  26.8 us
    ppermute x14, waiting for transfers between devices, exchange(): lax.ppermute(value, 'seq', [(one, one ^ index) for one in range(len(piece...  22.4 us
    pallas_call x1, Pallas kernels, operator(): pl.pallas_call(kernel, out_shape=piece_shapes(devices, rows + rows // 2 +...  7.91 us
    pallas_call x2, Pallas kernels, pack_steps(): pl.pallas_call(functools.partial(pack_kernel, steps), in_specs=[anywhere]...  5.26 us
    pallas_call x1, Pallas kernels, finish(): pl.pallas_call(kernel, out_shape=(low, low, low, low, jax.ShapeDtypeStruc...  3 us
  transfers between devices with their start and end apart: 15, of which 6 were waited for; matrix products, arithmetic and copies ran while one was open for 2% of the time, Pallas kernels for 4%

profile of v7, /device:TPU:0, one launch (start us, length us, event | category | flops | bytes accessed | tf_op | source)
XLA Modules:
  0.0 68.5 jit_solution(11960489932945834586)
XLA Ops:
  0.6 2.3 %shard_map.145 = (bf16[656,128]{1,0:T(8,128)(2,1)}, bf16[656,128]{1,0:T(8,128)(2,1)}) custom-call(bf16[256,512]{1,0:T(8,128)(2,1)} %refs_8_.2, bf16[256,512]{1,0:T(8,128)(2,1)} %refs_9_.2, bf16[256,512]{1,0:T(8,128)(2,1)} %refs_10_.1, bf16[256,512]{1,0:T(8,128)(2,1)} %refs_11_.1, f32[256,512]{1,0:T(8,128)} %refs_4_.3), custom_call_target="tpu_custom_call" | custom-call | tf_op jit(solution)/shard_map/pallas_call | solution.py:169
  2.9 6.0 %collective-permute-start = (bf16[656,128]{1,0:T(8,128)(2,1)}, bf16[656,128]{1,0:T(8,128)(2,1)S(1)}, u32[]{:S(2)}, u32[]{:S(2)}) collective-permute-start(bf16[656,128]{1,0:T(8,128)(2,1)} %get-tuple-element.34), channel_id=1, source_target_pairs={{0,28},{4,24},{8,20},{12,16},{16,12},{20,8},{24,4},{28,0},{1,29},{... | collective-permute-start | bytes 503816 | tf_op jit(solution)/shard_map/ppermute | solution.py:87
  9.0 0.2 collective-permute-start.1
  9.2 3.0 %shard_map.144 = (bf16[656,128]{1,0:T(8,128)(2,1)}, bf16[656,128]{1,0:T(8,128)(2,1)}, bf16[656,128]{1,0:T(8,128)(2,1)}, bf16[656,128]{1,0:T(8,128)(2,1)}, bf16[6...) custom-call(bf16[256,512]{1,0:T(8,128)(2,1)} %refs_8_.2, bf16[256,512]{1,0:T(8,128)(2,1)} %refs_9_.2, ...), custom_call_target="tpu_custom_call" | custom-call | tf_op jit(solution)/shard_map/pallas_call | solution.py:169
  12.2 0.1 collective-permute-start.2
  12.3 1.9 %collective-permute-start.3 = (bf16[656,128]{1,0:T(8,128)(2,1)}, bf16[656,128]{1,0:T(8,128)(2,1)S(1)}, u32[]{:S(2)}, u32[]{:S(2)}) collective-permute-start(bf16[656,128]{1,0:T(8,128)(2,1)} %get-tuple-element.39), channel_id=1, source_target_pairs={{0,8},{4,12},{8,0},{12,4},{16,24},{20,28},{24,16},{28,20},{1,9},{5... | collective-permute-start | bytes 503816 | tf_op jit(solution)/shard_map/ppermute | solution.py:87
  14.1 3.1 %collective-permute-start.4 = (bf16[656,128]{1,0:T(8,128)(2,1)}, bf16[656,128]{1,0:T(8,128)(2,1)S(1)}, u32[]{:S(2)}, u32[]{:S(2)}) collective-permute-start(bf16[656,128]{1,0:T(8,128)(2,1)} %get-tuple-element.40), channel_id=1, source_target_pairs={{0,20},{4,16},{8,28},{12,24},{16,4},{20,0},{24,12},{28,8},{1,21},{... | collective-permute-start | bytes 503816 | tf_op jit(solution)/shard_map/ppermute | solution.py:87
  17.2 0.0 copy-done.6
  17.2 0.1 pad.6.clone
  17.3 0.7 copy-done.7
  18.0 0.0 copy-done.8
  18.0 0.1 maximum_maximum_fusion
  18.0 0.0 collective-permute-done.refs_1_
  18.0 4.8 %collective-permute-start.5 = (bf16[656,128]{1,0:T(8,128)(2,1)}, bf16[656,128]{1,0:T(8,128)(2,1)S(1)}, u32[]{:S(2)}, u32[]{:S(2)}) collective-permute-start(bf16[656,128]{1,0:T(8,128)(2,1)} %get-tuple-element.41), channel_id=1, source_target_pairs={{0,16},{4,20},{8,24},{12,28},{16,0},{20,4},{24,8},{28,12},{1,17},{... | collective-permute-start | bytes 503816 | tf_op jit(solution)/shard_map/ppermute | solution.py:87
  22.8 0.0 collective-permute-done.1.refs_2_
  22.8 1.4 %collective-permute-start.6 = (bf16[656,128]{1,0:T(8,128)(2,1)}, bf16[656,128]{1,0:T(8,128)(2,1)S(1)}, u32[]{:S(2)}, u32[]{:S(2)}) collective-permute-start(bf16[656,128]{1,0:T(8,128)(2,1)} %get-tuple-element.42), channel_id=1, source_target_pairs={{0,4},{4,0},{8,12},{12,8},{16,20},{20,16},{24,28},{28,24},{1,5},{5... | collective-permute-start | bytes 503816 | tf_op jit(solution)/shard_map/ppermute | solution.py:87
  24.2 0.0 collective-permute-done.2.refs_3_
  24.2 0.7 collective-permute-start.7
  24.9 0.9 %broadcast_multiply_fusion.refs_0_ = bf16[656,128]{1,0:T(8,128)(2,1)S(1)} fusion(bf16[656,128]{1,0:T(8,128)(2,1)} %get-tuple-element.33, bf16[]{:T(256)} %bitcast.4), kind=kLoop, calls=%fused_computation | loop fusion | flops 83968 | bytes 335874 | tf_op jit(solution)/shard_map/mul | solution.py:617
  25.8 0.0 copy-start
  25.8 0.0 copy-start.1
  25.9 0.0 copy-start.2
  25.9 0.0 copy-start.3
  25.9 0.0 collective-permute-done.3.refs_4_
  25.9 9.3 %collective-permute-done.4.refs_5_ = bf16[656,128]{1,0:T(8,128)(2,1)S(1)} collective-permute-done((bf16[656,128]{1,0:T(8,128)(2,1)}, bf16[656,128]{1,0:T(8,128)(2,1)S(1)}, u32[]{:S(2)}, u32[]{:S(2)}) %collective-permute-start.4) | collective-permute-done | bytes 167968 | tf_op jit(solution)/shard_map/ppermute | solution.py:87
  35.1 2.8 %collective-permute-done.5.refs_6_ = bf16[656,128]{1,0:T(8,128)(2,1)S(1)} collective-permute-done((bf16[656,128]{1,0:T(8,128)(2,1)}, bf16[656,128]{1,0:T(8,128)(2,1)S(1)}, u32[]{:S(2)}, u32[]{:S(2)}) %collective-permute-start.5) | collective-permute-done | bytes 167968 | tf_op jit(solution)/shard_map/ppermute | solution.py:87
  37.9 0.0 collective-permute-done.6.refs_7_
  37.9 0.0 collective-permute-done.7.refs_10_
  37.9 0.0 copy-done.4
  37.9 0.0 copy-done.5
  37.9 7.9 %shard_map.146 = (bf16[432,128]{1,0:T(8,128)(2,1)S(1)}, bf16[432,128]{1,0:T(8,128)(2,1)S(1)}, bf16[432,128]{1,0:T(8,128)(2,1)S(1)}, bf16[432,128]{1,0:T(8,128)(2...) custom-call(bf16[656,128]{1,0:T(8,128)(2,1)S(1)} %broadcast_multiply, ...), custom_call_target="tpu_custom_call" | custom-call | tf_op jit(solution)/shard_map/pallas_call | solution.py:570
  45.9 2.5 %collective-permute-start.8 = (bf16[432,128]{1,0:T(8,128)(2,1)S(1)}, bf16[432,128]{1,0:T(8,128)(2,1)S(1)}, u32[]{:S(2)}, u32[]{:S(2)}) collective-permute-start(bf16[432,128]{1,0:T(8,128)(2,1)S(1)} %get-tuple-element.45), channel_id=1, source_target_pairs={{0,28},{4,24},{8,20},{12,16},{16,12},{20,8},{24,4},{28,0},{1,29},{... | collective-permute-start | bytes 331784 | tf_op jit(solution)/shard_map/ppermute | solution.py:87
  48.4 0.0 collective-permute-start.9
  48.4 2.8 %collective-permute-start.10 = (bf16[432,128]{1,0:T(8,128)(2,1)S(1)}, bf16[432,128]{1,0:T(8,128)(2,1)S(1)}, u32[]{:S(2)}, u32[]{:S(2)}) collective-permute-start(bf16[432,128]{1,0:T(8,128)(2,1)S(1)} %get-tuple-element.47), channel_id=1, source_target_pairs={{0,20},{4,16},{8,28},{12,24},{16,4},{20,0},{24,12},{28,8},{1,21},{... | collective-permute-start | bytes 331784 | tf_op jit(solution)/shard_map/ppermute | solution.py:87
  51.2 0.9 %collective-permute-start.11 = (bf16[432,128]{1,0:T(8,128)(2,1)S(1)}, bf16[432,128]{1,0:T(8,128)(2,1)S(1)}, u32[]{:S(2)}, u32[]{:S(2)}) collective-permute-start(bf16[432,128]{1,0:T(8,128)(2,1)S(1)} %get-tuple-element.48), channel_id=1, source_target_pairs={{0,16},{4,20},{8,24},{12,28},{16,0},{20,4},{24,8},{28,12},{1,17},{... | collective-permute-start | bytes 331784 | tf_op jit(solution)/shard_map/ppermute | solution.py:87
  52.1 1.5 %collective-permute-start.12 = (bf16[432,128]{1,0:T(8,128)(2,1)S(1)}, bf16[432,128]{1,0:T(8,128)(2,1)S(1)}, u32[]{:S(2)}, u32[]{:S(2)}) collective-permute-start(bf16[432,128]{1,0:T(8,128)(2,1)S(1)} %get-tuple-element.49), channel_id=1, source_target_pairs={{0,24},{4,28},{8,16},{12,20},{16,8},{20,12},{24,0},{28,4},{1,25},{... | collective-permute-start | bytes 331784 | tf_op jit(solution)/shard_map/ppermute | solution.py:87
  53.6 1.1 %collective-permute-done.8.refs_1_ = bf16[432,128]{1,0:T(8,128)(2,1)S(1)} collective-permute-done((bf16[432,128]{1,0:T(8,128)(2,1)S(1)}, bf16[432,128]{1,0:T(8,128)(2,1)S(1)}, u32[]{:S(2)}, u32[]{:S(2)}) %collective-permute-start.8) | collective-permute-done | bytes 110624 | tf_op jit(solution)/shard_map/ppermute | solution.py:87
  54.7 0.0 collective-permute-start.13
  54.7 1.9 %collective-permute-done.9.refs_2_ = bf16[432,128]{1,0:T(8,128)(2,1)S(1)} collective-permute-done((bf16[432,128]{1,0:T(8,128)(2,1)S(1)}, bf16[432,128]{1,0:T(8,128)(2,1)S(1)}, u32[]{:S(2)}, u32[]{:S(2)}) %collective-permute-start.9) | collective-permute-done | bytes 110624 | tf_op jit(solution)/shard_map/ppermute | solution.py:87
  56.6 1.6 %collective-permute-start.14 = (bf16[432,128]{1,0:T(8,128)(2,1)S(1)}, bf16[432,128]{1,0:T(8,128)(2,1)S(1)}, u32[]{:S(2)}, u32[]{:S(2)}) collective-permute-start(bf16[432,128]{1,0:T(8,128)(2,1)S(1)} %get-tuple-element.51), channel_id=1, source_target_pairs={{0,4},{4,0},{8,12},{12,8},{16,20},{20,16},{24,28},{28,24},{1,5},{5... | collective-permute-start | bytes 331784 | tf_op jit(solution)/shard_map/ppermute | solution.py:87
  58.2 5.4 %collective-permute-done.10.refs_3_ = bf16[432,128]{1,0:T(8,128)(2,1)S(1)} collective-permute-done((bf16[432,128]{1,0:T(8,128)(2,1)S(1)}, bf16[432,128]{1,0:T(8,128)(2,1)S(1)}, u32[]{:S(2)}, u32[]{:S(2)}) %collective-permute-start.10) | collective-permute-done | bytes 110624 | tf_op jit(solution)/shard_map/ppermute | solution.py:87
  63.6 1.9 %collective-permute-done.11.refs_4_ = bf16[432,128]{1,0:T(8,128)(2,1)S(1)} collective-permute-done((bf16[432,128]{1,0:T(8,128)(2,1)S(1)}, bf16[432,128]{1,0:T(8,128)(2,1)S(1)}, u32[]{:S(2)}, u32[]{:S(2)}) %collective-permute-start.11) | collective-permute-done | bytes 110624 | tf_op jit(solution)/shard_map/ppermute | solution.py:87
  65.5 0.0 collective-permute-done.12.refs_5_
  65.5 0.0 collective-permute-done.13.refs_6_
  65.5 0.0 collective-permute-done.14.refs_7_
  65.5 0.0 copy-done
  65.5 0.0 copy-done.1
  65.5 3.0 %shard_map.147 = (bf16[256,512]{1,0:T(8,128)(2,1)}, bf16[256,512]{1,0:T(8,128)(2,1)}, bf16[256,512]{1,0:T(8,128)(2,1)}, bf16[256,512]{1,0:T(8,128)(2,1)}, f32[25...) custom-call(bf16[432,128]{1,0:T(8,128)(2,1)S(1)} %get-tuple-element.44.refs_0_, ...), custom_call_target="tpu_custom_call" | custom-call | tf_op jit(solution)/shard_map/pallas_call | solution.py:289
  (8 shorter events, 0.0 us)
Async XLA Ops:
  2.9 15.1 %collective-permute-start = (bf16[656,128]{1,0:T(8,128)(2,1)}, bf16[656,128]{1,0:T(8,128)(2,1)S(1)}, u32[]{:S(2)}, u32[]{:S(2)}) collective-permute-start(bf16[656,128]{1,0:T(8,128)(2,1)} %get-tuple-element.34), channel_id=1, source_target_pairs={{0,28},{4,24},{8,20},{12,16},{16,12},{20,8},{24,4},{28,0},{1,29},{... | collective-permute-start | bytes 503816 | tf_op jit(solution)/shard_map/ppermute | solution.py:87
  8.9 8.2 %copy-start.6 = (f32[3,3,64]{2,1,0:T(4,128)S(1)}, f32[3,3,64]{2,1,0:T(4,128)}, u32[]{:S(2)}) copy-start(f32[3,3,64]{2,1,0:T(4,128)} %param.13) | copy-start | bytes 6916
  8.9 29.0 %copy-start.4 = (bf16[256,1536]{1,0:T(8,128)(2,1)S(1)}, bf16[256,1536]{1,0:T(8,128)(2,1)}, u32[]{:S(2)}) copy-start(bf16[256,1536]{1,0:T(8,128)(2,1)} %constant.12.clone.refs_9_) | copy-start | bytes 2359300
  9.0 29.0 %copy-start.5 = (bf16[512,768]{1,0:T(8,128)(2,1)S(1)}, bf16[512,768]{1,0:T(8,128)(2,1)}, u32[]{:S(2)}) copy-start(bf16[512,768]{1,0:T(8,128)(2,1)} %constant.4.clone.refs_8_) | copy-start | bytes 2359300
  9.0 13.9 %collective-permute-start.1 = (bf16[656,128]{1,0:T(8,128)(2,1)}, bf16[656,128]{1,0:T(8,128)(2,1)S(1)}, u32[]{:S(2)}, u32[]{:S(2)}) collective-permute-start(bf16[656,128]{1,0:T(8,128)(2,1)} %get-tuple-element.37), channel_id=1, source_target_pairs={{0,24},{4,28},{8,16},{12,20},{16,8},{20,12},{24,0},{28,4},{1,25},{... | collective-permute-start | bytes 503816 | tf_op jit(solution)/shard_map/ppermute | solution.py:87
  12.2 12.1 %collective-permute-start.2 = (bf16[656,128]{1,0:T(8,128)(2,1)}, bf16[656,128]{1,0:T(8,128)(2,1)S(1)}, u32[]{:S(2)}, u32[]{:S(2)}) collective-permute-start(bf16[656,128]{1,0:T(8,128)(2,1)} %get-tuple-element.38), channel_id=1, source_target_pairs={{0,12},{4,8},{8,4},{12,0},{16,28},{20,24},{24,20},{28,16},{1,13},{... | collective-permute-start | bytes 503816 | tf_op jit(solution)/shard_map/ppermute | solution.py:87
  12.3 13.6 %collective-permute-start.3 = (bf16[656,128]{1,0:T(8,128)(2,1)}, bf16[656,128]{1,0:T(8,128)(2,1)S(1)}, u32[]{:S(2)}, u32[]{:S(2)}) collective-permute-start(bf16[656,128]{1,0:T(8,128)(2,1)} %get-tuple-element.39), channel_id=1, source_target_pairs={{0,8},{4,12},{8,0},{12,4},{16,24},{20,28},{24,16},{28,20},{1,9},{5... | collective-permute-start | bytes 503816 | tf_op jit(solution)/shard_map/ppermute | solution.py:87
  14.1 21.0 %collective-permute-start.4 = (bf16[656,128]{1,0:T(8,128)(2,1)}, bf16[656,128]{1,0:T(8,128)(2,1)S(1)}, u32[]{:S(2)}, u32[]{:S(2)}) collective-permute-start(bf16[656,128]{1,0:T(8,128)(2,1)} %get-tuple-element.40), channel_id=1, source_target_pairs={{0,20},{4,16},{8,28},{12,24},{16,4},{20,0},{24,12},{28,8},{1,21},{... | collective-permute-start | bytes 503816 | tf_op jit(solution)/shard_map/ppermute | solution.py:87
  17.3 0.7 copy-start.7
  17.3 0.7 copy-start.8
  18.0 19.9 %collective-permute-start.5 = (bf16[656,128]{1,0:T(8,128)(2,1)}, bf16[656,128]{1,0:T(8,128)(2,1)S(1)}, u32[]{:S(2)}, u32[]{:S(2)}) collective-permute-start(bf16[656,128]{1,0:T(8,128)(2,1)} %get-tuple-element.41), channel_id=1, source_target_pairs={{0,16},{4,20},{8,24},{12,28},{16,0},{20,4},{24,8},{28,12},{1,17},{... | collective-permute-start | bytes 503816 | tf_op jit(solution)/shard_map/ppermute | solution.py:87
  22.8 15.1 %collective-permute-start.6 = (bf16[656,128]{1,0:T(8,128)(2,1)}, bf16[656,128]{1,0:T(8,128)(2,1)S(1)}, u32[]{:S(2)}, u32[]{:S(2)}) collective-permute-start(bf16[656,128]{1,0:T(8,128)(2,1)} %get-tuple-element.42), channel_id=1, source_target_pairs={{0,4},{4,0},{8,12},{12,8},{16,20},{20,16},{24,28},{28,24},{1,5},{5... | collective-permute-start | bytes 503816 | tf_op jit(solution)/shard_map/ppermute | solution.py:87
  24.2 13.7 %collective-permute-start.7 = (f32[8,128]{1,0:T(8,128)S(1)}, f32[8,128]{1,0:T(8,128)S(1)}, u32[]{:S(2)}, u32[]{:S(2)}) collective-permute-start(f32[8,128]{1,0:T(8,128)S(1)} %maximum_maximum_fusion), channel_id=1, source_target_pairs={{0,0},{1,4},{2,8},{3,12},{4,16},{5,20},{6,24},{7,28},{8,1},{9,5},{... | collective-permute-start | bytes 12296 | tf_op jit(solution)/shard_map/ppermute | solution.py:618
  25.8 39.7 %copy-start = (bf16[256,512]{1,0:T(8,128)(2,1)S(1)}, bf16[256,512]{1,0:T(8,128)(2,1)}, u32[]{:S(2)}) copy-start(bf16[256,512]{1,0:T(8,128)(2,1)} %refs_8_.2) | copy-start | bytes 786436
  25.8 39.7 %copy-start.1 = (bf16[256,512]{1,0:T(8,128)(2,1)S(1)}, bf16[256,512]{1,0:T(8,128)(2,1)}, u32[]{:S(2)}) copy-start(bf16[256,512]{1,0:T(8,128)(2,1)} %refs_9_.2) | copy-start | bytes 786436
  25.9 39.7 %copy-start.2 = (bf16[256,512]{1,0:T(8,128)(2,1)S(1)}, bf16[256,512]{1,0:T(8,128)(2,1)}, u32[]{:S(2)}) copy-start(bf16[256,512]{1,0:T(8,128)(2,1)} %refs_10_.1) | copy-start | bytes 786436
  25.9 39.7 %copy-start.3 = (bf16[256,512]{1,0:T(8,128)(2,1)S(1)}, bf16[256,512]{1,0:T(8,128)(2,1)}, u32[]{:S(2)}) copy-start(bf16[256,512]{1,0:T(8,128)(2,1)} %refs_11_.1) | copy-start | bytes 786436
  45.9 8.9 %collective-permute-start.8 = (bf16[432,128]{1,0:T(8,128)(2,1)S(1)}, bf16[432,128]{1,0:T(8,128)(2,1)S(1)}, u32[]{:S(2)}, u32[]{:S(2)}) collective-permute-start(bf16[432,128]{1,0:T(8,128)(2,1)S(1)} %get-tuple-element.45), channel_id=1, source_target_pairs={{0,28},{4,24},{8,20},{12,16},{16,12},{20,8},{24,4},{28,0},{1,29},{... | collective-permute-start | bytes 331784 | tf_op jit(solution)/shard_map/ppermute | solution.py:87
  48.4 8.2 %collective-permute-start.9 = (bf16[432,128]{1,0:T(8,128)(2,1)S(1)}, bf16[432,128]{1,0:T(8,128)(2,1)S(1)}, u32[]{:S(2)}, u32[]{:S(2)}) collective-permute-start(bf16[432,128]{1,0:T(8,128)(2,1)S(1)} %get-tuple-element.46), channel_id=1, source_target_pairs={{0,8},{4,12},{8,0},{12,4},{16,24},{20,28},{24,16},{28,20},{1,9},{5... | collective-permute-start | bytes 331784 | tf_op jit(solution)/shard_map/ppermute | solution.py:87
  48.4 15.2 %collective-permute-start.10 = (bf16[432,128]{1,0:T(8,128)(2,1)S(1)}, bf16[432,128]{1,0:T(8,128)(2,1)S(1)}, u32[]{:S(2)}, u32[]{:S(2)}) collective-permute-start(bf16[432,128]{1,0:T(8,128)(2,1)S(1)} %get-tuple-element.47), channel_id=1, source_target_pairs={{0,20},{4,16},{8,28},{12,24},{16,4},{20,0},{24,12},{28,8},{1,21},{... | collective-permute-start | bytes 331784 | tf_op jit(solution)/shard_map/ppermute | solution.py:87
  51.2 14.3 %collective-permute-start.11 = (bf16[432,128]{1,0:T(8,128)(2,1)S(1)}, bf16[432,128]{1,0:T(8,128)(2,1)S(1)}, u32[]{:S(2)}, u32[]{:S(2)}) collective-permute-start(bf16[432,128]{1,0:T(8,128)(2,1)S(1)} %get-tuple-element.48), channel_id=1, source_target_pairs={{0,16},{4,20},{8,24},{12,28},{16,0},{20,4},{24,8},{28,12},{1,17},{... | collective-permute-start | bytes 331784 | tf_op jit(solution)/shard_map/ppermute | solution.py:87
  52.1 13.4 %collective-permute-start.12 = (bf16[432,128]{1,0:T(8,128)(2,1)S(1)}, bf16[432,128]{1,0:T(8,128)(2,1)S(1)}, u32[]{:S(2)}, u32[]{:S(2)}) collective-permute-start(bf16[432,128]{1,0:T(8,128)(2,1)S(1)} %get-tuple-element.49), channel_id=1, source_target_pairs={{0,24},{4,28},{8,16},{12,20},{16,8},{20,12},{24,0},{28,4},{1,25},{... | collective-permute-start | bytes 331784 | tf_op jit(solution)/shard_map/ppermute | solution.py:87
  54.7 10.8 %collective-permute-start.13 = (bf16[432,128]{1,0:T(8,128)(2,1)S(1)}, bf16[432,128]{1,0:T(8,128)(2,1)S(1)}, u32[]{:S(2)}, u32[]{:S(2)}) collective-permute-start(bf16[432,128]{1,0:T(8,128)(2,1)S(1)} %get-tuple-element.50), channel_id=1, source_target_pairs={{0,12},{4,8},{8,4},{12,0},{16,28},{20,24},{24,20},{28,16},{1,13},{... | collective-permute-start | bytes 331784 | tf_op jit(solution)/shard_map/ppermute | solution.py:87
  56.6 8.9 %collective-permute-start.14 = (bf16[432,128]{1,0:T(8,128)(2,1)S(1)}, bf16[432,128]{1,0:T(8,128)(2,1)S(1)}, u32[]{:S(2)}, u32[]{:S(2)}) collective-permute-start(bf16[432,128]{1,0:T(8,128)(2,1)S(1)} %get-tuple-element.51), channel_id=1, source_target_pairs={{0,4},{4,0},{8,12},{12,8},{16,20},{20,16},{24,28},{28,24},{1,5},{5... | collective-permute-start | bytes 331784 | tf_op jit(solution)/shard_map/ppermute | solution.py:87

commit v8 on v7

--- a/solution.py
+++ b/solution.py
@@ -11,8 +11,7 @@
 
 HALF = 64
 LANES = 2 * HALF
-ENDS = 16
-MISC = 16
+MISC = 32
 SPAN = 252.0
 FLOOR = 125.0
 MEBIBYTE = 1024 * 1024
@@ -205,7 +204,6 @@
     odd = lax.rem(place, 2) == 1
     left = left_lanes((rows, LANES))
     left_half = left_lanes((half, LANES))
-    left_misc = left_lanes((MISC, LANES))
 
     def one_tile(step, _):
         refs = piece(in_refs, 2 * step, place), piece(in_refs, 2 * step + 1, place)
@@ -219,27 +217,33 @@
             one, two = values
             return jnp.where(mask, one, swap(two)), jnp.where(mask, swap(one), two)
 
-        miscs = [
-            head + tail
-            for head, tail in zip(both(rows + half, MISC), both(rows + half + MISC, MISC))
-        ]
+        miscs = both(rows + half, MISC)
+        scales = [misc[0:5] + misc[5:10] for misc in miscs]
+
+        def small(start, stop, scale):
+            return [
+                decode(misc[start:stop], row[scale : scale + 1])
+                for misc, row in zip(miscs, scales)
+            ]
+
         codes = both(0, rows)
-        back, mixed = sides(left, [decode(code, misc[0:1]) for code, misc in zip(codes, miscs)])
+        back, mixed = sides(left, [decode(code, row[0:1]) for code, row in zip(codes, scales)])
         codes = both(rows, half)
         upper, lower = sides(
-            left_half, [decode(code, misc[1:2]) for code, misc in zip(codes, miscs)]
+            left_half, [decode(code, row[1:2]) for code, row in zip(codes, scales)]
         )
         filter_out[pl.ds(0, half), at] = upper
         filter_out[pl.ds(half, half), at] = lower
-        ends = sides(left_misc, both(rows + half + 2 * MISC, ENDS))
-        lefts, rights = sides(left_misc, miscs)
-        taps = (lefts[4:7], rights[4:7], rights[7:10])
+        ends = sides(left_lanes((8, LANES)), [misc[24:32] for misc in miscs])
+        lefts, rights = sides(left_lanes((6, LANES)), small(12, 18, 3))
+        taps = (lefts[0:3], rights[0:3], rights[3:6])
+        lefts, rights = sides(left_lanes((6, LANES)), small(18, 24, 4))
         for offset in range(3):
-            taps_out[0, offset : offset + 1, at] = lefts[10 + offset : 11 + offset]
-            taps_out[1, offset : offset + 1, at] = rights[10 + offset : 11 + offset]
-            taps_out[2, offset : offset + 1, at] = rights[13 + offset : 14 + offset]
-        skip_out[0:1, at] = lefts[13:14]
-        back_edge, mixed_edge = lefts[2:4], rights[2:4]
+            taps_out[0, offset : offset + 1, at] = lefts[offset : offset + 1]
+            taps_out[1, offset : offset + 1, at] = rights[offset : offset + 1]
+            taps_out[2, offset : offset + 1, at] = rights[3 + offset : 4 + offset]
+        skip_out[0:1, at] = lefts[3:4]
+        back_edge, mixed_edge = sides(left_lanes((2, LANES)), small(10, 12, 2))
         convs, edges = [], []
         for stream, (source, end, row) in enumerate(
             ((query_ref, ends[0], 0), (key_ref, ends[1], 0), (value_ref, ends[1], 2))
@@ -537,18 +541,26 @@
         if row == 3:
             value = jnp.where(left_lanes((1, LANES)), filters[0, 0:1, :], value)
         shared[6 + row : 7 + row, :] = value
+    tap_rows, sum_rows = shared[0:6, :], shared[6:12, :]
+    tap_scale, sum_scale = scale_of(tap_rows), scale_of(sum_rows)
+    tap_codes, sum_codes = encode(tap_rows, tap_scale), encode(sum_rows, sum_scale)
 
     def close(index, _):
         out_ref = piece(out_refs, index, place)
         block = index ^ place
-        misc[index, 2:4, :] = starts[block + 1, 0:2, :]
-        misc[index, 4:16, :] = shared[0:12, :]
-        head, tail = head_tail(misc[index])
-        here = rows + half_rows
-        out_ref[pl.ds(here, MISC), :] = head
-        out_ref[pl.ds(here + MISC, MISC), :] = tail
-        near = jnp.concatenate([ends[block, 0:4, :], ends[block + 2, 4:8, :], nothing], axis=0)
-        out_ref[pl.ds(here + 2 * MISC, ENDS), :] = near.astype(jnp.bfloat16)
+        edge = starts[block + 1, 0:2, :]
+        scale = scale_of(edge)
+        misc[index, 2:3, :] = scale
+        misc[index, 3:4, :] = tap_scale
+        misc[index, 4:5, :] = sum_scale
+        scales = misc[index, 0:5, :]
+        misc[index, 5:10, :] = scales - scales.astype(jnp.bfloat16).astype(jnp.float32)
+        misc[index, 10:12, :] = encode(edge, scale)
+        misc[index, 12:18, :] = tap_codes
+        misc[index, 18:24, :] = sum_codes
+        misc[index, 24:28, :] = ends[block, 0:4, :]
+        misc[index, 28:32, :] = ends[block + 2, 4:8, :]
+        out_ref[pl.ds(rows + half_rows, MISC), :] = misc[index].astype(jnp.bfloat16)
         return 0
 
     loop(blocks, close, 0, unrolled)
@@ -569,7 +581,7 @@
 
     return pl.pallas_call(
         kernel,
-        out_shape=piece_shapes(devices, rows + rows // 2 + 2 * MISC + ENDS),
+        out_shape=piece_shapes(devices, rows + rows // 2 + MISC),
         scratch_shapes=[
             pltpu.VMEM((blocks + 2, 8, LANES), jnp.float32),
             pltpu.VMEM((blocks + 1, 8, LANES), jnp.float32),

time: 68.7 us -> 68.3 us (level)
  waiting for transfers between devices: 22.4 us -> 21.7 us
    ppermute x14, waiting for transfers between devices: 22.4 us -> 21.7 us  [exchange(): lax.ppermute(value, 'seq', [(one, one ^ index) for one in range(len(piece...]
where the time goes in v8:
time: 68.3 us; the launch traced here: 68.1 us
  starting transfers between devices  27.7 us (41%)
  waiting for transfers between devices  21.7 us (32%)
  Pallas kernels  16.2 us (24%)
  other arithmetic  1.01 us (1%)
  local copies, waits for them, and re-layouts  0.8 us (1%)
  between operations  0.78 us (1%)
    ppermute x14, starting transfers between devices, exchange(): lax.ppermute(value, 'seq', [(one, one ^ index) for one in range(len(piece...  27 us
    ppermute x14, waiting for transfers between devices, exchange(): lax.ppermute(value, 'seq', [(one, one ^ index) for one in range(len(piece...  21.7 us
    pallas_call x1, Pallas kernels, operator(): pl.pallas_call(kernel, out_shape=piece_shapes(devices, rows + rows // 2 +...  7.89 us
    pallas_call x2, Pallas kernels, pack_steps(): pl.pallas_call(functools.partial(pack_kernel, steps), in_specs=[anywhere]...  5.26 us
    pallas_call x1, Pallas kernels, finish(): pl.pallas_call(kernel, out_shape=(low, low, low, low, jax.ShapeDtypeStruc...  3.06 us
  transfers between devices with their start and end apart: 15, of which 6 were waited for; matrix products, arithmetic and copies ran while one was open for 2% of the time, Pallas kernels for 4%

profile of v8, /device:TPU:0, one launch (start us, length us, event | category | flops | bytes accessed | tf_op | source)
XLA Modules:
  0.0 68.1 jit_solution(11896441903674601372)
XLA Ops:
  0.6 2.3 %shard_map.145 = (bf16[656,128]{1,0:T(8,128)(2,1)}, bf16[656,128]{1,0:T(8,128)(2,1)}) custom-call(bf16[256,512]{1,0:T(8,128)(2,1)} %refs_8_.2, bf16[256,512]{1,0:T(8,128)(2,1)} %refs_9_.2, bf16[256,512]{1,0:T(8,128)(2,1)} %refs_10_.1, bf16[256,512]{1,0:T(8,128)(2,1)} %refs_11_.1, f32[256,512]{1,0:T(8,128)} %refs_4_.3), custom_call_target="tpu_custom_call" | custom-call | tf_op jit(solution)/shard_map/pallas_call | solution.py:168
  2.9 6.0 %collective-permute-start = (bf16[656,128]{1,0:T(8,128)(2,1)}, bf16[656,128]{1,0:T(8,128)(2,1)S(1)}, u32[]{:S(2)}, u32[]{:S(2)}) collective-permute-start(bf16[656,128]{1,0:T(8,128)(2,1)} %get-tuple-element.34), channel_id=1, source_target_pairs={{0,28},{4,24},{8,20},{12,16},{16,12},{20,8},{24,4},{28,0},{1,29},{... | collective-permute-start | bytes 503816 | tf_op jit(solution)/shard_map/ppermute | solution.py:86
  9.0 0.2 collective-permute-start.1
  9.2 3.0 %shard_map.144 = (bf16[656,128]{1,0:T(8,128)(2,1)}, bf16[656,128]{1,0:T(8,128)(2,1)}, bf16[656,128]{1,0:T(8,128)(2,1)}, bf16[656,128]{1,0:T(8,128)(2,1)}, bf16[6...) custom-call(bf16[256,512]{1,0:T(8,128)(2,1)} %refs_8_.2, bf16[256,512]{1,0:T(8,128)(2,1)} %refs_9_.2, ...), custom_call_target="tpu_custom_call" | custom-call | tf_op jit(solution)/shard_map/pallas_call | solution.py:168
  12.2 0.1 collective-permute-start.2
  12.3 1.9 %collective-permute-start.3 = (bf16[656,128]{1,0:T(8,128)(2,1)}, bf16[656,128]{1,0:T(8,128)(2,1)S(1)}, u32[]{:S(2)}, u32[]{:S(2)}) collective-permute-start(bf16[656,128]{1,0:T(8,128)(2,1)} %get-tuple-element.39), channel_id=1, source_target_pairs={{0,8},{4,12},{8,0},{12,4},{16,24},{20,28},{24,16},{28,20},{1,9},{5... | collective-permute-start | bytes 503816 | tf_op jit(solution)/shard_map/ppermute | solution.py:86
  14.1 3.1 %collective-permute-start.4 = (bf16[656,128]{1,0:T(8,128)(2,1)}, bf16[656,128]{1,0:T(8,128)(2,1)S(1)}, u32[]{:S(2)}, u32[]{:S(2)}) collective-permute-start(bf16[656,128]{1,0:T(8,128)(2,1)} %get-tuple-element.40), channel_id=1, source_target_pairs={{0,20},{4,16},{8,28},{12,24},{16,4},{20,0},{24,12},{28,8},{1,21},{... | collective-permute-start | bytes 503816 | tf_op jit(solution)/shard_map/ppermute | solution.py:86
  17.2 0.0 copy-done.6
  17.2 0.1 pad.6.clone
  17.3 0.7 copy-done.7
  18.0 0.0 copy-done.8
  18.0 0.1 maximum_maximum_fusion
  18.0 0.0 collective-permute-done.refs_1_
  18.0 4.8 %collective-permute-start.5 = (bf16[656,128]{1,0:T(8,128)(2,1)}, bf16[656,128]{1,0:T(8,128)(2,1)S(1)}, u32[]{:S(2)}, u32[]{:S(2)}) collective-permute-start(bf16[656,128]{1,0:T(8,128)(2,1)} %get-tuple-element.41), channel_id=1, source_target_pairs={{0,16},{4,20},{8,24},{12,28},{16,0},{20,4},{24,8},{28,12},{1,17},{... | collective-permute-start | bytes 503816 | tf_op jit(solution)/shard_map/ppermute | solution.py:86
  22.8 0.0 collective-permute-done.1.refs_2_
  22.8 1.4 %collective-permute-start.6 = (bf16[656,128]{1,0:T(8,128)(2,1)}, bf16[656,128]{1,0:T(8,128)(2,1)S(1)}, u32[]{:S(2)}, u32[]{:S(2)}) collective-permute-start(bf16[656,128]{1,0:T(8,128)(2,1)} %get-tuple-element.42), channel_id=1, source_target_pairs={{0,4},{4,0},{8,12},{12,8},{16,20},{20,16},{24,28},{28,24},{1,5},{5... | collective-permute-start | bytes 503816 | tf_op jit(solution)/shard_map/ppermute | solution.py:86
  24.2 0.0 collective-permute-done.2.refs_3_
  24.2 0.7 collective-permute-start.7
  24.9 0.9 %broadcast_multiply_fusion.refs_0_ = bf16[656,128]{1,0:T(8,128)(2,1)S(1)} fusion(bf16[656,128]{1,0:T(8,128)(2,1)} %get-tuple-element.33, bf16[]{:T(256)} %bitcast.4), kind=kLoop, calls=%fused_computation | loop fusion | flops 83968 | bytes 335874 | tf_op jit(solution)/shard_map/mul | solution.py:629
  25.8 0.0 copy-start
  25.8 0.0 copy-start.1
  25.9 0.0 copy-start.2
  25.9 0.0 copy-start.3
  25.9 0.0 collective-permute-done.3.refs_4_
  25.9 9.3 %collective-permute-done.4.refs_5_ = bf16[656,128]{1,0:T(8,128)(2,1)S(1)} collective-permute-done((bf16[656,128]{1,0:T(8,128)(2,1)}, bf16[656,128]{1,0:T(8,128)(2,1)S(1)}, u32[]{:S(2)}, u32[]{:S(2)}) %collective-permute-start.4) | collective-permute-done | bytes 167968 | tf_op jit(solution)/shard_map/ppermute | solution.py:86
  35.1 2.8 %collective-permute-done.5.refs_6_ = bf16[656,128]{1,0:T(8,128)(2,1)S(1)} collective-permute-done((bf16[656,128]{1,0:T(8,128)(2,1)}, bf16[656,128]{1,0:T(8,128)(2,1)S(1)}, u32[]{:S(2)}, u32[]{:S(2)}) %collective-permute-start.5) | collective-permute-done | bytes 167968 | tf_op jit(solution)/shard_map/ppermute | solution.py:86
  37.9 0.0 collective-permute-done.6.refs_7_
  37.9 0.0 collective-permute-done.7.refs_10_
  37.9 7.9 %shard_map.146 = (bf16[416,128]{1,0:T(8,128)(2,1)S(1)}, bf16[416,128]{1,0:T(8,128)(2,1)S(1)}, bf16[416,128]{1,0:T(8,128)(2,1)S(1)}, bf16[416,128]{1,0:T(8,128)(2...) custom-call(bf16[656,128]{1,0:T(8,128)(2,1)S(1)} %broadcast_multiply, ...), custom_call_target="tpu_custom_call" | custom-call | tf_op jit(solution)/shard_map/pallas_call | solution.py:582
  45.8 2.5 %collective-permute-start.8 = (bf16[416,128]{1,0:T(8,128)(2,1)S(1)}, bf16[416,128]{1,0:T(8,128)(2,1)S(1)}, u32[]{:S(2)}, u32[]{:S(2)}) collective-permute-start(bf16[416,128]{1,0:T(8,128)(2,1)S(1)} %get-tuple-element.45), channel_id=1, source_target_pairs={{0,28},{4,24},{8,20},{12,16},{16,12},{20,8},{24,4},{28,0},{1,29},{... | collective-permute-start | bytes 319496 | tf_op jit(solution)/shard_map/ppermute | solution.py:86
  48.4 0.0 collective-permute-start.9
  48.4 2.8 %collective-permute-start.10 = (bf16[416,128]{1,0:T(8,128)(2,1)S(1)}, bf16[416,128]{1,0:T(8,128)(2,1)S(1)}, u32[]{:S(2)}, u32[]{:S(2)}) collective-permute-start(bf16[416,128]{1,0:T(8,128)(2,1)S(1)} %get-tuple-element.47), channel_id=1, source_target_pairs={{0,20},{4,16},{8,28},{12,24},{16,4},{20,0},{24,12},{28,8},{1,21},{... | collective-permute-start | bytes 319496 | tf_op jit(solution)/shard_map/ppermute | solution.py:86
  51.2 0.9 %collective-permute-start.11 = (bf16[416,128]{1,0:T(8,128)(2,1)S(1)}, bf16[416,128]{1,0:T(8,128)(2,1)S(1)}, u32[]{:S(2)}, u32[]{:S(2)}) collective-permute-start(bf16[416,128]{1,0:T(8,128)(2,1)S(1)} %get-tuple-element.48), channel_id=1, source_target_pairs={{0,16},{4,20},{8,24},{12,28},{16,0},{20,4},{24,8},{28,12},{1,17},{... | collective-permute-start | bytes 319496 | tf_op jit(solution)/shard_map/ppermute | solution.py:86
  52.1 1.5 %collective-permute-start.12 = (bf16[416,128]{1,0:T(8,128)(2,1)S(1)}, bf16[416,128]{1,0:T(8,128)(2,1)S(1)}, u32[]{:S(2)}, u32[]{:S(2)}) collective-permute-start(bf16[416,128]{1,0:T(8,128)(2,1)S(1)} %get-tuple-element.49), channel_id=1, source_target_pairs={{0,24},{4,28},{8,16},{12,20},{16,8},{20,12},{24,0},{28,4},{1,25},{... | collective-permute-start | bytes 319496 | tf_op jit(solution)/shard_map/ppermute | solution.py:86
  53.6 0.9 %collective-permute-done.8.refs_1_ = bf16[416,128]{1,0:T(8,128)(2,1)S(1)} collective-permute-done((bf16[416,128]{1,0:T(8,128)(2,1)S(1)}, bf16[416,128]{1,0:T(8,128)(2,1)S(1)}, u32[]{:S(2)}, u32[]{:S(2)}) %collective-permute-start.8) | collective-permute-done | bytes 106528 | tf_op jit(solution)/shard_map/ppermute | solution.py:86
  54.5 0.1 collective-permute-start.13
  54.5 1.6 %collective-permute-done.9.refs_2_ = bf16[416,128]{1,0:T(8,128)(2,1)S(1)} collective-permute-done((bf16[416,128]{1,0:T(8,128)(2,1)S(1)}, bf16[416,128]{1,0:T(8,128)(2,1)S(1)}, u32[]{:S(2)}, u32[]{:S(2)}) %collective-permute-start.9) | collective-permute-done | bytes 106528 | tf_op jit(solution)/shard_map/ppermute | solution.py:86
  56.1 1.8 %collective-permute-start.14 = (bf16[416,128]{1,0:T(8,128)(2,1)S(1)}, bf16[416,128]{1,0:T(8,128)(2,1)S(1)}, u32[]{:S(2)}, u32[]{:S(2)}) collective-permute-start(bf16[416,128]{1,0:T(8,128)(2,1)S(1)} %get-tuple-element.51), channel_id=1, source_target_pairs={{0,4},{4,0},{8,12},{12,8},{16,20},{20,16},{24,28},{28,24},{1,5},{5... | collective-permute-start | bytes 319496 | tf_op jit(solution)/shard_map/ppermute | solution.py:86
  57.9 5.2 %collective-permute-done.10.refs_3_ = bf16[416,128]{1,0:T(8,128)(2,1)S(1)} collective-permute-done((bf16[416,128]{1,0:T(8,128)(2,1)S(1)}, bf16[416,128]{1,0:T(8,128)(2,1)S(1)}, u32[]{:S(2)}, u32[]{:S(2)}) %collective-permute-start.10) | collective-permute-done | bytes 106528 | tf_op jit(solution)/shard_map/ppermute | solution.py:86
  63.1 1.9 %collective-permute-done.11.refs_4_ = bf16[416,128]{1,0:T(8,128)(2,1)S(1)} collective-permute-done((bf16[416,128]{1,0:T(8,128)(2,1)S(1)}, bf16[416,128]{1,0:T(8,128)(2,1)S(1)}, u32[]{:S(2)}, u32[]{:S(2)}) %collective-permute-start.11) | collective-permute-done | bytes 106528 | tf_op jit(solution)/shard_map/ppermute | solution.py:86
  65.0 0.0 collective-permute-done.12.refs_5_
  65.0 0.0 collective-permute-done.13.refs_6_
  65.0 0.0 collective-permute-done.14.refs_7_
  65.0 0.0 copy-done
  65.0 0.0 copy-done.1
  65.1 0.0 copy-done.2
  65.1 0.0 copy-done.3
  65.1 3.1 %shard_map.147 = (bf16[256,512]{1,0:T(8,128)(2,1)}, bf16[256,512]{1,0:T(8,128)(2,1)}, bf16[256,512]{1,0:T(8,128)(2,1)}, bf16[256,512]{1,0:T(8,128)(2,1)}, f32[25...) custom-call(bf16[416,128]{1,0:T(8,128)(2,1)S(1)} %get-tuple-element.44.refs_0_, ...), custom_call_target="tpu_custom_call" | custom-call | tf_op jit(solution)/shard_map/pallas_call | solution.py:293
  (8 shorter events, 0.0 us)
Async XLA Ops:
  2.9 15.1 %collective-permute-start = (bf16[656,128]{1,0:T(8,128)(2,1)}, bf16[656,128]{1,0:T(8,128)(2,1)S(1)}, u32[]{:S(2)}, u32[]{:S(2)}) collective-permute-start(bf16[656,128]{1,0:T(8,128)(2,1)} %get-tuple-element.34), channel_id=1, source_target_pairs={{0,28},{4,24},{8,20},{12,16},{16,12},{20,8},{24,4},{28,0},{1,29},{... | collective-permute-start | bytes 503816 | tf_op jit(solution)/shard_map/ppermute | solution.py:86
  8.9 8.2 %copy-start.6 = (f32[3,3,64]{2,1,0:T(4,128)S(1)}, f32[3,3,64]{2,1,0:T(4,128)}, u32[]{:S(2)}) copy-start(f32[3,3,64]{2,1,0:T(4,128)} %param.13) | copy-start | bytes 6916
  8.9 29.0 %copy-start.4 = (bf16[256,1536]{1,0:T(8,128)(2,1)S(1)}, bf16[256,1536]{1,0:T(8,128)(2,1)}, u32[]{:S(2)}) copy-start(bf16[256,1536]{1,0:T(8,128)(2,1)} %constant.12.clone.refs_9_) | copy-start | bytes 2359300
  9.0 29.0 %copy-start.5 = (bf16[512,768]{1,0:T(8,128)(2,1)S(1)}, bf16[512,768]{1,0:T(8,128)(2,1)}, u32[]{:S(2)}) copy-start(bf16[512,768]{1,0:T(8,128)(2,1)} %constant.4.clone.refs_8_) | copy-start | bytes 2359300
  9.0 13.9 %collective-permute-start.1 = (bf16[656,128]{1,0:T(8,128)(2,1)}, bf16[656,128]{1,0:T(8,128)(2,1)S(1)}, u32[]{:S(2)}, u32[]{:S(2)}) collective-permute-start(bf16[656,128]{1,0:T(8,128)(2,1)} %get-tuple-element.37), channel_id=1, source_target_pairs={{0,24},{4,28},{8,16},{12,20},{16,8},{20,12},{24,0},{28,4},{1,25},{... | collective-permute-start | bytes 503816 | tf_op jit(solution)/shard_map/ppermute | solution.py:86
  12.2 12.1 %collective-permute-start.2 = (bf16[656,128]{1,0:T(8,128)(2,1)}, bf16[656,128]{1,0:T(8,128)(2,1)S(1)}, u32[]{:S(2)}, u32[]{:S(2)}) collective-permute-start(bf16[656,128]{1,0:T(8,128)(2,1)} %get-tuple-element.38), channel_id=1, source_target_pairs={{0,12},{4,8},{8,4},{12,0},{16,28},{20,24},{24,20},{28,16},{1,13},{... | collective-permute-start | bytes 503816 | tf_op jit(solution)/shard_map/ppermute | solution.py:86
  12.3 13.6 %collective-permute-start.3 = (bf16[656,128]{1,0:T(8,128)(2,1)}, bf16[656,128]{1,0:T(8,128)(2,1)S(1)}, u32[]{:S(2)}, u32[]{:S(2)}) collective-permute-start(bf16[656,128]{1,0:T(8,128)(2,1)} %get-tuple-element.39), channel_id=1, source_target_pairs={{0,8},{4,12},{8,0},{12,4},{16,24},{20,28},{24,16},{28,20},{1,9},{5... | collective-permute-start | bytes 503816 | tf_op jit(solution)/shard_map/ppermute | solution.py:86
  14.1 21.0 %collective-permute-start.4 = (bf16[656,128]{1,0:T(8,128)(2,1)}, bf16[656,128]{1,0:T(8,128)(2,1)S(1)}, u32[]{:S(2)}, u32[]{:S(2)}) collective-permute-start(bf16[656,128]{1,0:T(8,128)(2,1)} %get-tuple-element.40), channel_id=1, source_target_pairs={{0,20},{4,16},{8,28},{12,24},{16,4},{20,0},{24,12},{28,8},{1,21},{... | collective-permute-start | bytes 503816 | tf_op jit(solution)/shard_map/ppermute | solution.py:86
  17.3 0.7 %copy-start.7 = (f32[3,64]{1,0:T(4,128)S(1)}, f32[3,64]{1,0:T(4,128)}, u32[]{:S(2)}) copy-start(f32[3,64]{1,0:T(4,128)} %constant.5.clone.1) | copy-start | bytes 2308
  17.3 0.7 %copy-start.8 = (f32[64]{0:T(128)S(1)}, f32[64]{0:T(128)}, u32[]{:S(2)}) copy-start(f32[64]{0:T(128)} %param.14) | copy-start | bytes 772
  18.0 19.9 %collective-permute-start.5 = (bf16[656,128]{1,0:T(8,128)(2,1)}, bf16[656,128]{1,0:T(8,128)(2,1)S(1)}, u32[]{:S(2)}, u32[]{:S(2)}) collective-permute-start(bf16[656,128]{1,0:T(8,128)(2,1)} %get-tuple-element.41), channel_id=1, source_target_pairs={{0,16},{4,20},{8,24},{12,28},{16,0},{20,4},{24,8},{28,12},{1,17},{... | collective-permute-start | bytes 503816 | tf_op jit(solution)/shard_map/ppermute | solution.py:86
  22.8 15.1 %collective-permute-start.6 = (bf16[656,128]{1,0:T(8,128)(2,1)}, bf16[656,128]{1,0:T(8,128)(2,1)S(1)}, u32[]{:S(2)}, u32[]{:S(2)}) collective-permute-start(bf16[656,128]{1,0:T(8,128)(2,1)} %get-tuple-element.42), channel_id=1, source_target_pairs={{0,4},{4,0},{8,12},{12,8},{16,20},{20,16},{24,28},{28,24},{1,5},{5... | collective-permute-start | bytes 503816 | tf_op jit(solution)/shard_map/ppermute | solution.py:86
  24.2 13.7 %collective-permute-start.7 = (f32[8,128]{1,0:T(8,128)S(1)}, f32[8,128]{1,0:T(8,128)S(1)}, u32[]{:S(2)}, u32[]{:S(2)}) collective-permute-start(f32[8,128]{1,0:T(8,128)S(1)} %maximum_maximum_fusion), channel_id=1, source_target_pairs={{0,0},{1,4},{2,8},{3,12},{4,16},{5,20},{6,24},{7,28},{8,1},{9,5},{... | collective-permute-start | bytes 12296 | tf_op jit(solution)/shard_map/ppermute | solution.py:630
  25.8 39.2 %copy-start = (bf16[256,512]{1,0:T(8,128)(2,1)S(1)}, bf16[256,512]{1,0:T(8,128)(2,1)}, u32[]{:S(2)}) copy-start(bf16[256,512]{1,0:T(8,128)(2,1)} %refs_8_.2) | copy-start | bytes 786436
  25.8 39.2 %copy-start.1 = (bf16[256,512]{1,0:T(8,128)(2,1)S(1)}, bf16[256,512]{1,0:T(8,128)(2,1)}, u32[]{:S(2)}) copy-start(bf16[256,512]{1,0:T(8,128)(2,1)} %refs_9_.2) | copy-start | bytes 786436
  25.9 39.2 %copy-start.2 = (bf16[256,512]{1,0:T(8,128)(2,1)S(1)}, bf16[256,512]{1,0:T(8,128)(2,1)}, u32[]{:S(2)}) copy-start(bf16[256,512]{1,0:T(8,128)(2,1)} %refs_10_.1) | copy-start | bytes 786436
  25.9 39.2 %copy-start.3 = (bf16[256,512]{1,0:T(8,128)(2,1)S(1)}, bf16[256,512]{1,0:T(8,128)(2,1)}, u32[]{:S(2)}) copy-start(bf16[256,512]{1,0:T(8,128)(2,1)} %refs_11_.1) | copy-start | bytes 786436
  45.8 8.6 %collective-permute-start.8 = (bf16[416,128]{1,0:T(8,128)(2,1)S(1)}, bf16[416,128]{1,0:T(8,128)(2,1)S(1)}, u32[]{:S(2)}, u32[]{:S(2)}) collective-permute-start(bf16[416,128]{1,0:T(8,128)(2,1)S(1)} %get-tuple-element.45), channel_id=1, source_target_pairs={{0,28},{4,24},{8,20},{12,16},{16,12},{20,8},{24,4},{28,0},{1,29},{... | collective-permute-start | bytes 319496 | tf_op jit(solution)/shard_map/ppermute | solution.py:86
  48.4 7.8 %collective-permute-start.9 = (bf16[416,128]{1,0:T(8,128)(2,1)S(1)}, bf16[416,128]{1,0:T(8,128)(2,1)S(1)}, u32[]{:S(2)}, u32[]{:S(2)}) collective-permute-start(bf16[416,128]{1,0:T(8,128)(2,1)S(1)} %get-tuple-element.46), channel_id=1, source_target_pairs={{0,8},{4,12},{8,0},{12,4},{16,24},{20,28},{24,16},{28,20},{1,9},{5... | collective-permute-start | bytes 319496 | tf_op jit(solution)/shard_map/ppermute | solution.py:86
  48.4 14.8 %collective-permute-start.10 = (bf16[416,128]{1,0:T(8,128)(2,1)S(1)}, bf16[416,128]{1,0:T(8,128)(2,1)S(1)}, u32[]{:S(2)}, u32[]{:S(2)}) collective-permute-start(bf16[416,128]{1,0:T(8,128)(2,1)S(1)} %get-tuple-element.47), channel_id=1, source_target_pairs={{0,20},{4,16},{8,28},{12,24},{16,4},{20,0},{24,12},{28,8},{1,21},{... | collective-permute-start | bytes 319496 | tf_op jit(solution)/shard_map/ppermute | solution.py:86
  51.2 13.8 %collective-permute-start.11 = (bf16[416,128]{1,0:T(8,128)(2,1)S(1)}, bf16[416,128]{1,0:T(8,128)(2,1)S(1)}, u32[]{:S(2)}, u32[]{:S(2)}) collective-permute-start(bf16[416,128]{1,0:T(8,128)(2,1)S(1)} %get-tuple-element.48), channel_id=1, source_target_pairs={{0,16},{4,20},{8,24},{12,28},{16,0},{20,4},{24,8},{28,12},{1,17},{... | collective-permute-start | bytes 319496 | tf_op jit(solution)/shard_map/ppermute | solution.py:86
  52.1 12.9 %collective-permute-start.12 = (bf16[416,128]{1,0:T(8,128)(2,1)S(1)}, bf16[416,128]{1,0:T(8,128)(2,1)S(1)}, u32[]{:S(2)}, u32[]{:S(2)}) collective-permute-start(bf16[416,128]{1,0:T(8,128)(2,1)S(1)} %get-tuple-element.49), channel_id=1, source_target_pairs={{0,24},{4,28},{8,16},{12,20},{16,8},{20,12},{24,0},{28,4},{1,25},{... | collective-permute-start | bytes 319496 | tf_op jit(solution)/shard_map/ppermute | solution.py:86
  54.5 10.6 %collective-permute-start.13 = (bf16[416,128]{1,0:T(8,128)(2,1)S(1)}, bf16[416,128]{1,0:T(8,128)(2,1)S(1)}, u32[]{:S(2)}, u32[]{:S(2)}) collective-permute-start(bf16[416,128]{1,0:T(8,128)(2,1)S(1)} %get-tuple-element.50), channel_id=1, source_target_pairs={{0,12},{4,8},{8,4},{12,0},{16,28},{20,24},{24,20},{28,16},{1,13},{... | collective-permute-start | bytes 319496 | tf_op jit(solution)/shard_map/ppermute | solution.py:86
  56.1 8.9 %collective-permute-start.14 = (bf16[416,128]{1,0:T(8,128)(2,1)S(1)}, bf16[416,128]{1,0:T(8,128)(2,1)S(1)}, u32[]{:S(2)}, u32[]{:S(2)}) collective-permute-start(bf16[416,128]{1,0:T(8,128)(2,1)S(1)} %get-tuple-element.51), channel_id=1, source_target_pairs={{0,4},{4,0},{8,12},{12,8},{16,20},{20,16},{24,28},{28,24},{1,5},{5... | collective-permute-start | bytes 319496 | tf_op jit(solution)/shard_map/ppermute | solution.py:86

commit v9 on v8

--- a/solution.py
+++ b/solution.py
@@ -64,7 +64,7 @@
 
 def scale_of(value):
     peak = jnp.max(jnp.abs(value), axis=0, keepdims=True)
-    return jnp.maximum(peak * 1.0001, 1e-30)
+    return jnp.maximum(peak * 1.0001, 1e-34)
 
 
 def loop(count, body, carry, unrolled):

time: 68.3 us -> 68.3 us (level)
  no operation moved by 1% of the time
where the time goes in v9:
time: 68.3 us; the launch traced here: 68.1 us
  starting transfers between devices  27.7 us (41%)
  waiting for transfers between devices  21.7 us (32%)
  Pallas kernels  16.2 us (24%)
  other arithmetic  1.01 us (1%)
  local copies, waits for them, and re-layouts  0.8 us (1%)
  between operations  0.78 us (1%)
    ppermute x14, starting transfers between devices, exchange(): lax.ppermute(value, 'seq', [(one, one ^ index) for one in range(len(piece...  27 us
    ppermute x14, waiting for transfers between devices, exchange(): lax.ppermute(value, 'seq', [(one, one ^ index) for one in range(len(piece...  21.7 us
    pallas_call x1, Pallas kernels, operator(): pl.pallas_call(kernel, out_shape=piece_shapes(devices, rows + rows // 2 +...  7.89 us
    pallas_call x2, Pallas kernels, pack_steps(): pl.pallas_call(functools.partial(pack_kernel, steps), in_specs=[anywhere]...  5.26 us
    pallas_call x1, Pallas kernels, finish(): pl.pallas_call(kernel, out_shape=(low, low, low, low, jax.ShapeDtypeStruc...  3.06 us
  transfers between devices with their start and end apart: 15, of which 6 were waited for; matrix products, arithmetic and copies ran while one was open for 2% of the time, Pallas kernels for 4%

profile of v9, /device:TPU:0, one launch (start us, length us, event | category | flops | bytes accessed | tf_op | source)
XLA Modules:
  0.0 68.1 jit_solution(18205157672012307683)
XLA Ops:
  0.6 2.3 %shard_map.145 = (bf16[656,128]{1,0:T(8,128)(2,1)}, bf16[656,128]{1,0:T(8,128)(2,1)}) custom-call(bf16[256,512]{1,0:T(8,128)(2,1)} %refs_8_.2, bf16[256,512]{1,0:T(8,128)(2,1)} %refs_9_.2, bf16[256,512]{1,0:T(8,128)(2,1)} %refs_10_.1, bf16[256,512]{1,0:T(8,128)(2,1)} %refs_11_.1, f32[256,512]{1,0:T(8,128)} %refs_4_.3), custom_call_target="tpu_custom_call" | custom-call | tf_op jit(solution)/shard_map/pallas_call | solution.py:168
  2.9 6.0 %collective-permute-start = (bf16[656,128]{1,0:T(8,128)(2,1)}, bf16[656,128]{1,0:T(8,128)(2,1)S(1)}, u32[]{:S(2)}, u32[]{:S(2)}) collective-permute-start(bf16[656,128]{1,0:T(8,128)(2,1)} %get-tuple-element.34), channel_id=1, source_target_pairs={{0,28},{4,24},{8,20},{12,16},{16,12},{20,8},{24,4},{28,0},{1,29},{... | collective-permute-start | bytes 503816 | tf_op jit(solution)/shard_map/ppermute | solution.py:86
  9.0 0.2 collective-permute-start.1
  9.2 3.0 %shard_map.144 = (bf16[656,128]{1,0:T(8,128)(2,1)}, bf16[656,128]{1,0:T(8,128)(2,1)}, bf16[656,128]{1,0:T(8,128)(2,1)}, bf16[656,128]{1,0:T(8,128)(2,1)}, bf16[6...) custom-call(bf16[256,512]{1,0:T(8,128)(2,1)} %refs_8_.2, bf16[256,512]{1,0:T(8,128)(2,1)} %refs_9_.2, ...), custom_call_target="tpu_custom_call" | custom-call | tf_op jit(solution)/shard_map/pallas_call | solution.py:168
  12.2 0.1 collective-permute-start.2
  12.3 1.9 %collective-permute-start.3 = (bf16[656,128]{1,0:T(8,128)(2,1)}, bf16[656,128]{1,0:T(8,128)(2,1)S(1)}, u32[]{:S(2)}, u32[]{:S(2)}) collective-permute-start(bf16[656,128]{1,0:T(8,128)(2,1)} %get-tuple-element.39), channel_id=1, source_target_pairs={{0,8},{4,12},{8,0},{12,4},{16,24},{20,28},{24,16},{28,20},{1,9},{5... | collective-permute-start | bytes 503816 | tf_op jit(solution)/shard_map/ppermute | solution.py:86
  14.1 3.1 %collective-permute-start.4 = (bf16[656,128]{1,0:T(8,128)(2,1)}, bf16[656,128]{1,0:T(8,128)(2,1)S(1)}, u32[]{:S(2)}, u32[]{:S(2)}) collective-permute-start(bf16[656,128]{1,0:T(8,128)(2,1)} %get-tuple-element.40), channel_id=1, source_target_pairs={{0,20},{4,16},{8,28},{12,24},{16,4},{20,0},{24,12},{28,8},{1,21},{... | collective-permute-start | bytes 503816 | tf_op jit(solution)/shard_map/ppermute | solution.py:86
  17.2 0.0 copy-done.6
  17.2 0.1 pad.6.clone
  17.3 0.7 copy-done.7
  18.0 0.0 copy-done.8
  18.0 0.1 maximum_maximum_fusion
  18.0 0.0 collective-permute-done.refs_1_
  18.0 4.8 %collective-permute-start.5 = (bf16[656,128]{1,0:T(8,128)(2,1)}, bf16[656,128]{1,0:T(8,128)(2,1)S(1)}, u32[]{:S(2)}, u32[]{:S(2)}) collective-permute-start(bf16[656,128]{1,0:T(8,128)(2,1)} %get-tuple-element.41), channel_id=1, source_target_pairs={{0,16},{4,20},{8,24},{12,28},{16,0},{20,4},{24,8},{28,12},{1,17},{... | collective-permute-start | bytes 503816 | tf_op jit(solution)/shard_map/ppermute | solution.py:86
  22.8 0.0 collective-permute-done.1.refs_2_
  22.8 1.4 %collective-permute-start.6 = (bf16[656,128]{1,0:T(8,128)(2,1)}, bf16[656,128]{1,0:T(8,128)(2,1)S(1)}, u32[]{:S(2)}, u32[]{:S(2)}) collective-permute-start(bf16[656,128]{1,0:T(8,128)(2,1)} %get-tuple-element.42), channel_id=1, source_target_pairs={{0,4},{4,0},{8,12},{12,8},{16,20},{20,16},{24,28},{28,24},{1,5},{5... | collective-permute-start | bytes 503816 | tf_op jit(solution)/shard_map/ppermute | solution.py:86
  24.2 0.0 collective-permute-done.2.refs_3_
  24.2 0.7 collective-permute-start.7
  24.9 0.9 %broadcast_multiply_fusion.refs_0_ = bf16[656,128]{1,0:T(8,128)(2,1)S(1)} fusion(bf16[656,128]{1,0:T(8,128)(2,1)} %get-tuple-element.33, bf16[]{:T(256)} %bitcast.4), kind=kLoop, calls=%fused_computation | loop fusion | flops 83968 | bytes 335874 | tf_op jit(solution)/shard_map/mul | solution.py:629
  25.8 0.0 copy-start
  25.8 0.0 copy-start.1
  25.9 0.0 copy-start.2
  25.9 0.0 copy-start.3
  25.9 0.0 collective-permute-done.3.refs_4_
  25.9 9.3 %collective-permute-done.4.refs_5_ = bf16[656,128]{1,0:T(8,128)(2,1)S(1)} collective-permute-done((bf16[656,128]{1,0:T(8,128)(2,1)}, bf16[656,128]{1,0:T(8,128)(2,1)S(1)}, u32[]{:S(2)}, u32[]{:S(2)}) %collective-permute-start.4) | collective-permute-done | bytes 167968 | tf_op jit(solution)/shard_map/ppermute | solution.py:86
  35.1 2.8 %collective-permute-done.5.refs_6_ = bf16[656,128]{1,0:T(8,128)(2,1)S(1)} collective-permute-done((bf16[656,128]{1,0:T(8,128)(2,1)}, bf16[656,128]{1,0:T(8,128)(2,1)S(1)}, u32[]{:S(2)}, u32[]{:S(2)}) %collective-permute-start.5) | collective-permute-done | bytes 167968 | tf_op jit(solution)/shard_map/ppermute | solution.py:86
  37.9 0.0 collective-permute-done.6.refs_7_
  37.9 0.0 collective-permute-done.7.refs_10_
  37.9 7.9 %shard_map.146 = (bf16[416,128]{1,0:T(8,128)(2,1)S(1)}, bf16[416,128]{1,0:T(8,128)(2,1)S(1)}, bf16[416,128]{1,0:T(8,128)(2,1)S(1)}, bf16[416,128]{1,0:T(8,128)(2...) custom-call(bf16[656,128]{1,0:T(8,128)(2,1)S(1)} %broadcast_multiply, ...), custom_call_target="tpu_custom_call" | custom-call | tf_op jit(solution)/shard_map/pallas_call | solution.py:582
  45.8 2.5 %collective-permute-start.8 = (bf16[416,128]{1,0:T(8,128)(2,1)S(1)}, bf16[416,128]{1,0:T(8,128)(2,1)S(1)}, u32[]{:S(2)}, u32[]{:S(2)}) collective-permute-start(bf16[416,128]{1,0:T(8,128)(2,1)S(1)} %get-tuple-element.45), channel_id=1, source_target_pairs={{0,28},{4,24},{8,20},{12,16},{16,12},{20,8},{24,4},{28,0},{1,29},{... | collective-permute-start | bytes 319496 | tf_op jit(solution)/shard_map/ppermute | solution.py:86
  48.4 0.0 collective-permute-start.9
  48.4 2.8 %collective-permute-start.10 = (bf16[416,128]{1,0:T(8,128)(2,1)S(1)}, bf16[416,128]{1,0:T(8,128)(2,1)S(1)}, u32[]{:S(2)}, u32[]{:S(2)}) collective-permute-start(bf16[416,128]{1,0:T(8,128)(2,1)S(1)} %get-tuple-element.47), channel_id=1, source_target_pairs={{0,20},{4,16},{8,28},{12,24},{16,4},{20,0},{24,12},{28,8},{1,21},{... | collective-permute-start | bytes 319496 | tf_op jit(solution)/shard_map/ppermute | solution.py:86
  51.2 0.9 %collective-permute-start.11 = (bf16[416,128]{1,0:T(8,128)(2,1)S(1)}, bf16[416,128]{1,0:T(8,128)(2,1)S(1)}, u32[]{:S(2)}, u32[]{:S(2)}) collective-permute-start(bf16[416,128]{1,0:T(8,128)(2,1)S(1)} %get-tuple-element.48), channel_id=1, source_target_pairs={{0,16},{4,20},{8,24},{12,28},{16,0},{20,4},{24,8},{28,12},{1,17},{... | collective-permute-start | bytes 319496 | tf_op jit(solution)/shard_map/ppermute | solution.py:86
  52.1 1.5 %collective-permute-start.12 = (bf16[416,128]{1,0:T(8,128)(2,1)S(1)}, bf16[416,128]{1,0:T(8,128)(2,1)S(1)}, u32[]{:S(2)}, u32[]{:S(2)}) collective-permute-start(bf16[416,128]{1,0:T(8,128)(2,1)S(1)} %get-tuple-element.49), channel_id=1, source_target_pairs={{0,24},{4,28},{8,16},{12,20},{16,8},{20,12},{24,0},{28,4},{1,25},{... | collective-permute-start | bytes 319496 | tf_op jit(solution)/shard_map/ppermute | solution.py:86
  53.6 0.9 %collective-permute-done.8.refs_1_ = bf16[416,128]{1,0:T(8,128)(2,1)S(1)} collective-permute-done((bf16[416,128]{1,0:T(8,128)(2,1)S(1)}, bf16[416,128]{1,0:T(8,128)(2,1)S(1)}, u32[]{:S(2)}, u32[]{:S(2)}) %collective-permute-start.8) | collective-permute-done | bytes 106528 | tf_op jit(solution)/shard_map/ppermute | solution.py:86
  54.5 0.1 collective-permute-start.13
  54.5 1.6 %collective-permute-done.9.refs_2_ = bf16[416,128]{1,0:T(8,128)(2,1)S(1)} collective-permute-done((bf16[416,128]{1,0:T(8,128)(2,1)S(1)}, bf16[416,128]{1,0:T(8,128)(2,1)S(1)}, u32[]{:S(2)}, u32[]{:S(2)}) %collective-permute-start.9) | collective-permute-done | bytes 106528 | tf_op jit(solution)/shard_map/ppermute | solution.py:86
  56.1 1.8 %collective-permute-start.14 = (bf16[416,128]{1,0:T(8,128)(2,1)S(1)}, bf16[416,128]{1,0:T(8,128)(2,1)S(1)}, u32[]{:S(2)}, u32[]{:S(2)}) collective-permute-start(bf16[416,128]{1,0:T(8,128)(2,1)S(1)} %get-tuple-element.51), channel_id=1, source_target_pairs={{0,4},{4,0},{8,12},{12,8},{16,20},{20,16},{24,28},{28,24},{1,5},{5... | collective-permute-start | bytes 319496 | tf_op jit(solution)/shard_map/ppermute | solution.py:86
  57.9 5.2 %collective-permute-done.10.refs_3_ = bf16[416,128]{1,0:T(8,128)(2,1)S(1)} collective-permute-done((bf16[416,128]{1,0:T(8,128)(2,1)S(1)}, bf16[416,128]{1,0:T(8,128)(2,1)S(1)}, u32[]{:S(2)}, u32[]{:S(2)}) %collective-permute-start.10) | collective-permute-done | bytes 106528 | tf_op jit(solution)/shard_map/ppermute | solution.py:86
  63.1 1.9 %collective-permute-done.11.refs_4_ = bf16[416,128]{1,0:T(8,128)(2,1)S(1)} collective-permute-done((bf16[416,128]{1,0:T(8,128)(2,1)S(1)}, bf16[416,128]{1,0:T(8,128)(2,1)S(1)}, u32[]{:S(2)}, u32[]{:S(2)}) %collective-permute-start.11) | collective-permute-done | bytes 106528 | tf_op jit(solution)/shard_map/ppermute | solution.py:86
  65.0 0.0 collective-permute-done.12.refs_5_
  65.0 0.0 collective-permute-done.13.refs_6_
  65.0 0.0 collective-permute-done.14.refs_7_
  65.0 0.0 copy-done
  65.0 0.0 copy-done.1
  65.1 0.0 copy-done.2
  65.1 0.0 copy-done.3
  65.1 3.1 %shard_map.147 = (bf16[256,512]{1,0:T(8,128)(2,1)}, bf16[256,512]{1,0:T(8,128)(2,1)}, bf16[256,512]{1,0:T(8,128)(2,1)}, bf16[256,512]{1,0:T(8,128)(2,1)}, f32[25...) custom-call(bf16[416,128]{1,0:T(8,128)(2,1)S(1)} %get-tuple-element.44.refs_0_, ...), custom_call_target="tpu_custom_call" | custom-call | tf_op jit(solution)/shard_map/pallas_call | solution.py:293
  (8 shorter events, 0.0 us)
Async XLA Ops:
  2.9 15.1 %collective-permute-start = (bf16[656,128]{1,0:T(8,128)(2,1)}, bf16[656,128]{1,0:T(8,128)(2,1)S(1)}, u32[]{:S(2)}, u32[]{:S(2)}) collective-permute-start(bf16[656,128]{1,0:T(8,128)(2,1)} %get-tuple-element.34), channel_id=1, source_target_pairs={{0,28},{4,24},{8,20},{12,16},{16,12},{20,8},{24,4},{28,0},{1,29},{... | collective-permute-start | bytes 503816 | tf_op jit(solution)/shard_map/ppermute | solution.py:86
  8.9 8.2 %copy-start.6 = (f32[3,3,64]{2,1,0:T(4,128)S(1)}, f32[3,3,64]{2,1,0:T(4,128)}, u32[]{:S(2)}) copy-start(f32[3,3,64]{2,1,0:T(4,128)} %param.13) | copy-start | bytes 6916
  8.9 29.0 %copy-start.4 = (bf16[256,1536]{1,0:T(8,128)(2,1)S(1)}, bf16[256,1536]{1,0:T(8,128)(2,1)}, u32[]{:S(2)}) copy-start(bf16[256,1536]{1,0:T(8,128)(2,1)} %constant.12.clone.refs_9_) | copy-start | bytes 2359300
  9.0 29.0 %copy-start.5 = (bf16[512,768]{1,0:T(8,128)(2,1)S(1)}, bf16[512,768]{1,0:T(8,128)(2,1)}, u32[]{:S(2)}) copy-start(bf16[512,768]{1,0:T(8,128)(2,1)} %constant.4.clone.refs_8_) | copy-start | bytes 2359300
  9.0 13.9 %collective-permute-start.1 = (bf16[656,128]{1,0:T(8,128)(2,1)}, bf16[656,128]{1,0:T(8,128)(2,1)S(1)}, u32[]{:S(2)}, u32[]{:S(2)}) collective-permute-start(bf16[656,128]{1,0:T(8,128)(2,1)} %get-tuple-element.37), channel_id=1, source_target_pairs={{0,24},{4,28},{8,16},{12,20},{16,8},{20,12},{24,0},{28,4},{1,25},{... | collective-permute-start | bytes 503816 | tf_op jit(solution)/shard_map/ppermute | solution.py:86
  12.2 12.1 %collective-permute-start.2 = (bf16[656,128]{1,0:T(8,128)(2,1)}, bf16[656,128]{1,0:T(8,128)(2,1)S(1)}, u32[]{:S(2)}, u32[]{:S(2)}) collective-permute-start(bf16[656,128]{1,0:T(8,128)(2,1)} %get-tuple-element.38), channel_id=1, source_target_pairs={{0,12},{4,8},{8,4},{12,0},{16,28},{20,24},{24,20},{28,16},{1,13},{... | collective-permute-start | bytes 503816 | tf_op jit(solution)/shard_map/ppermute | solution.py:86
  12.3 13.6 %collective-permute-start.3 = (bf16[656,128]{1,0:T(8,128)(2,1)}, bf16[656,128]{1,0:T(8,128)(2,1)S(1)}, u32[]{:S(2)}, u32[]{:S(2)}) collective-permute-start(bf16[656,128]{1,0:T(8,128)(2,1)} %get-tuple-element.39), channel_id=1, source_target_pairs={{0,8},{4,12},{8,0},{12,4},{16,24},{20,28},{24,16},{28,20},{1,9},{5... | collective-permute-start | bytes 503816 | tf_op jit(solution)/shard_map/ppermute | solution.py:86
  14.1 21.0 %collective-permute-start.4 = (bf16[656,128]{1,0:T(8,128)(2,1)}, bf16[656,128]{1,0:T(8,128)(2,1)S(1)}, u32[]{:S(2)}, u32[]{:S(2)}) collective-permute-start(bf16[656,128]{1,0:T(8,128)(2,1)} %get-tuple-element.40), channel_id=1, source_target_pairs={{0,20},{4,16},{8,28},{12,24},{16,4},{20,0},{24,12},{28,8},{1,21},{... | collective-permute-start | bytes 503816 | tf_op jit(solution)/shard_map/ppermute | solution.py:86
  17.3 0.7 %copy-start.7 = (f32[3,64]{1,0:T(4,128)S(1)}, f32[3,64]{1,0:T(4,128)}, u32[]{:S(2)}) copy-start(f32[3,64]{1,0:T(4,128)} %constant.5.clone.1) | copy-start | bytes 2308
  17.3 0.7 %copy-start.8 = (f32[64]{0:T(128)S(1)}, f32[64]{0:T(128)}, u32[]{:S(2)}) copy-start(f32[64]{0:T(128)} %param.14) | copy-start | bytes 772
  18.0 19.9 %collective-permute-start.5 = (bf16[656,128]{1,0:T(8,128)(2,1)}, bf16[656,128]{1,0:T(8,128)(2,1)S(1)}, u32[]{:S(2)}, u32[]{:S(2)}) collective-permute-start(bf16[656,128]{1,0:T(8,128)(2,1)} %get-tuple-element.41), channel_id=1, source_target_pairs={{0,16},{4,20},{8,24},{12,28},{16,0},{20,4},{24,8},{28,12},{1,17},{... | collective-permute-start | bytes 503816 | tf_op jit(solution)/shard_map/ppermute | solution.py:86
  22.8 15.1 %collective-permute-start.6 = (bf16[656,128]{1,0:T(8,128)(2,1)}, bf16[656,128]{1,0:T(8,128)(2,1)S(1)}, u32[]{:S(2)}, u32[]{:S(2)}) collective-permute-start(bf16[656,128]{1,0:T(8,128)(2,1)} %get-tuple-element.42), channel_id=1, source_target_pairs={{0,4},{4,0},{8,12},{12,8},{16,20},{20,16},{24,28},{28,24},{1,5},{5... | collective-permute-start | bytes 503816 | tf_op jit(solution)/shard_map/ppermute | solution.py:86
  24.2 13.7 %collective-permute-start.7 = (f32[8,128]{1,0:T(8,128)S(1)}, f32[8,128]{1,0:T(8,128)S(1)}, u32[]{:S(2)}, u32[]{:S(2)}) collective-permute-start(f32[8,128]{1,0:T(8,128)S(1)} %maximum_maximum_fusion), channel_id=1, source_target_pairs={{0,0},{1,4},{2,8},{3,12},{4,16},{5,20},{6,24},{7,28},{8,1},{9,5},{... | collective-permute-start | bytes 12296 | tf_op jit(solution)/shard_map/ppermute | solution.py:630
  25.8 39.2 %copy-start = (bf16[256,512]{1,0:T(8,128)(2,1)S(1)}, bf16[256,512]{1,0:T(8,128)(2,1)}, u32[]{:S(2)}) copy-start(bf16[256,512]{1,0:T(8,128)(2,1)} %refs_8_.2) | copy-start | bytes 786436
  25.8 39.2 %copy-start.1 = (bf16[256,512]{1,0:T(8,128)(2,1)S(1)}, bf16[256,512]{1,0:T(8,128)(2,1)}, u32[]{:S(2)}) copy-start(bf16[256,512]{1,0:T(8,128)(2,1)} %refs_9_.2) | copy-start | bytes 786436
  25.9 39.2 %copy-start.2 = (bf16[256,512]{1,0:T(8,128)(2,1)S(1)}, bf16[256,512]{1,0:T(8,128)(2,1)}, u32[]{:S(2)}) copy-start(bf16[256,512]{1,0:T(8,128)(2,1)} %refs_10_.1) | copy-start | bytes 786436
  25.9 39.2 %copy-start.3 = (bf16[256,512]{1,0:T(8,128)(2,1)S(1)}, bf16[256,512]{1,0:T(8,128)(2,1)}, u32[]{:S(2)}) copy-start(bf16[256,512]{1,0:T(8,128)(2,1)} %refs_11_.1) | copy-start | bytes 786436
  45.8 8.6 %collective-permute-start.8 = (bf16[416,128]{1,0:T(8,128)(2,1)S(1)}, bf16[416,128]{1,0:T(8,128)(2,1)S(1)}, u32[]{:S(2)}, u32[]{:S(2)}) collective-permute-start(bf16[416,128]{1,0:T(8,128)(2,1)S(1)} %get-tuple-element.45), channel_id=1, source_target_pairs={{0,28},{4,24},{8,20},{12,16},{16,12},{20,8},{24,4},{28,0},{1,29},{... | collective-permute-start | bytes 319496 | tf_op jit(solution)/shard_map/ppermute | solution.py:86
  48.4 7.8 %collective-permute-start.9 = (bf16[416,128]{1,0:T(8,128)(2,1)S(1)}, bf16[416,128]{1,0:T(8,128)(2,1)S(1)}, u32[]{:S(2)}, u32[]{:S(2)}) collective-permute-start(bf16[416,128]{1,0:T(8,128)(2,1)S(1)} %get-tuple-element.46), channel_id=1, source_target_pairs={{0,8},{4,12},{8,0},{12,4},{16,24},{20,28},{24,16},{28,20},{1,9},{5... | collective-permute-start | bytes 319496 | tf_op jit(solution)/shard_map/ppermute | solution.py:86
  48.4 14.8 %collective-permute-start.10 = (bf16[416,128]{1,0:T(8,128)(2,1)S(1)}, bf16[416,128]{1,0:T(8,128)(2,1)S(1)}, u32[]{:S(2)}, u32[]{:S(2)}) collective-permute-start(bf16[416,128]{1,0:T(8,128)(2,1)S(1)} %get-tuple-element.47), channel_id=1, source_target_pairs={{0,20},{4,16},{8,28},{12,24},{16,4},{20,0},{24,12},{28,8},{1,21},{... | collective-permute-start | bytes 319496 | tf_op jit(solution)/shard_map/ppermute | solution.py:86
  51.2 13.8 %collective-permute-start.11 = (bf16[416,128]{1,0:T(8,128)(2,1)S(1)}, bf16[416,128]{1,0:T(8,128)(2,1)S(1)}, u32[]{:S(2)}, u32[]{:S(2)}) collective-permute-start(bf16[416,128]{1,0:T(8,128)(2,1)S(1)} %get-tuple-element.48), channel_id=1, source_target_pairs={{0,16},{4,20},{8,24},{12,28},{16,0},{20,4},{24,8},{28,12},{1,17},{... | collective-permute-start | bytes 319496 | tf_op jit(solution)/shard_map/ppermute | solution.py:86
  52.1 12.9 %collective-permute-start.12 = (bf16[416,128]{1,0:T(8,128)(2,1)S(1)}, bf16[416,128]{1,0:T(8,128)(2,1)S(1)}, u32[]{:S(2)}, u32[]{:S(2)}) collective-permute-start(bf16[416,128]{1,0:T(8,128)(2,1)S(1)} %get-tuple-element.49), channel_id=1, source_target_pairs={{0,24},{4,28},{8,16},{12,20},{16,8},{20,12},{24,0},{28,4},{1,25},{... | collective-permute-start | bytes 319496 | tf_op jit(solution)/shard_map/ppermute | solution.py:86
  54.5 10.6 %collective-permute-start.13 = (bf16[416,128]{1,0:T(8,128)(2,1)S(1)}, bf16[416,128]{1,0:T(8,128)(2,1)S(1)}, u32[]{:S(2)}, u32[]{:S(2)}) collective-permute-start(bf16[416,128]{1,0:T(8,128)(2,1)S(1)} %get-tuple-element.50), channel_id=1, source_target_pairs={{0,12},{4,8},{8,4},{12,0},{16,28},{20,24},{24,20},{28,16},{1,13},{... | collective-permute-start | bytes 319496 | tf_op jit(solution)/shard_map/ppermute | solution.py:86
  56.1 8.9 %collective-permute-start.14 = (bf16[416,128]{1,0:T(8,128)(2,1)S(1)}, bf16[416,128]{1,0:T(8,128)(2,1)S(1)}, u32[]{:S(2)}, u32[]{:S(2)}) collective-permute-start(bf16[416,128]{1,0:T(8,128)(2,1)S(1)} %get-tuple-element.51), channel_id=1, source_target_pairs={{0,4},{4,0},{8,12},{12,8},{16,20},{20,16},{24,28},{28,24},{1,5},{5... | collective-permute-start | bytes 319496 | tf_op jit(solution)/shard_map/ppermute | solution.py:86

commit v10 on v9

--- a/solution.py
+++ b/solution.py
@@ -19,7 +19,7 @@
 LISTED = 8
 OUT_ORDER = (0, 7, 6, 3, 2, 5, 4, 1)
 PACK_STEPS = ((3,), (1, 2, 0))
-BACK_ORDER = (0, 7, 2, 5, 4, 6, 3, 1)
+BACK_ORDER = (0, 7, 2, 5, 4, 3, 6, 1)
 
 
 def swap(value):

time: 68.3 us -> 68.3 us (level)
  waiting for transfers between devices: 21.7 us -> 19.4 us
  starting transfers between devices: 27.7 us -> 29.9 us
    ppermute x14, waiting for transfers between devices: 21.7 us -> 19.4 us  [exchange(): lax.ppermute(value, 'seq', [(one, one ^ index) for one in range(len(piece...]
    ppermute x14, starting transfers between devices: 27 us -> 29.3 us  [exchange(): lax.ppermute(value, 'seq', [(one, one ^ index) for one in range(len(piece...]
  transfers between devices with their start and end apart: 15 -> 15, of which waited for: 6 -> 5; matrix products, arithmetic and copies ran while one was open for 2% -> 2% of each run, Pallas kernels for 4% -> 4%
where the time goes in v10:
time: 68.3 us; the launch traced here: 68.1 us
  starting transfers between devices  29.9 us (44%)
  waiting for transfers between devices  19.4 us (28%)
  Pallas kernels  16.2 us (24%)
  other arithmetic  1.01 us (1%)
  local copies, waits for them, and re-layouts  0.8 us (1%)
  between operations  0.78 us (1%)
    ppermute x14, starting transfers between devices, exchange(): lax.ppermute(value, 'seq', [(one, one ^ index) for one in range(len(piece...  29.3 us
    ppermute x14, waiting for transfers between devices, exchange(): lax.ppermute(value, 'seq', [(one, one ^ index) for one in range(len(piece...  19.4 us
    pallas_call x1, Pallas kernels, operator(): pl.pallas_call(kernel, out_shape=piece_shapes(devices, rows + rows // 2 +...  7.89 us
    pallas_call x2, Pallas kernels, pack_steps(): pl.pallas_call(functools.partial(pack_kernel, steps), in_specs=[anywhere]...  5.26 us
    pallas_call x1, Pallas kernels, finish(): pl.pallas_call(kernel, out_shape=(low, low, low, low, jax.ShapeDtypeStruc...  3.05 us
  transfers between devices with their start and end apart: 15, of which 5 were waited for; matrix products, arithmetic and copies ran while one was open for 2% of the time, Pallas kernels for 4%

profile of v10, /device:TPU:0, one launch (start us, length us, event | category | flops | bytes accessed | tf_op | source)
XLA Modules:
  0.0 68.1 jit_solution(7248470098279220134)
XLA Ops:
  0.6 2.3 %shard_map.145 = (bf16[656,128]{1,0:T(8,128)(2,1)}, bf16[656,128]{1,0:T(8,128)(2,1)}) custom-call(bf16[256,512]{1,0:T(8,128)(2,1)} %refs_8_.2, bf16[256,512]{1,0:T(8,128)(2,1)} %refs_9_.2, bf16[256,512]{1,0:T(8,128)(2,1)} %refs_10_.1, bf16[256,512]{1,0:T(8,128)(2,1)} %refs_11_.1, f32[256,512]{1,0:T(8,128)} %refs_4_.3), custom_call_target="tpu_custom_call" | custom-call | tf_op jit(solution)/shard_map/pallas_call | solution.py:168
  2.9 6.0 %collective-permute-start = (bf16[656,128]{1,0:T(8,128)(2,1)}, bf16[656,128]{1,0:T(8,128)(2,1)S(1)}, u32[]{:S(2)}, u32[]{:S(2)}) collective-permute-start(bf16[656,128]{1,0:T(8,128)(2,1)} %get-tuple-element.34), channel_id=1, source_target_pairs={{0,28},{4,24},{8,20},{12,16},{16,12},{20,8},{24,4},{28,0},{1,29},{... | collective-permute-start | bytes 503816 | tf_op jit(solution)/shard_map/ppermute | solution.py:86
  9.0 0.2 collective-permute-start.1
  9.2 3.0 %shard_map.144 = (bf16[656,128]{1,0:T(8,128)(2,1)}, bf16[656,128]{1,0:T(8,128)(2,1)}, bf16[656,128]{1,0:T(8,128)(2,1)}, bf16[656,128]{1,0:T(8,128)(2,1)}, bf16[6...) custom-call(bf16[256,512]{1,0:T(8,128)(2,1)} %refs_8_.2, bf16[256,512]{1,0:T(8,128)(2,1)} %refs_9_.2, ...), custom_call_target="tpu_custom_call" | custom-call | tf_op jit(solution)/shard_map/pallas_call | solution.py:168
  12.2 0.1 collective-permute-start.2
  12.3 1.9 %collective-permute-start.3 = (bf16[656,128]{1,0:T(8,128)(2,1)}, bf16[656,128]{1,0:T(8,128)(2,1)S(1)}, u32[]{:S(2)}, u32[]{:S(2)}) collective-permute-start(bf16[656,128]{1,0:T(8,128)(2,1)} %get-tuple-element.39), channel_id=1, source_target_pairs={{0,8},{4,12},{8,0},{12,4},{16,24},{20,28},{24,16},{28,20},{1,9},{5... | collective-permute-start | bytes 503816 | tf_op jit(solution)/shard_map/ppermute | solution.py:86
  14.1 3.1 %collective-permute-start.4 = (bf16[656,128]{1,0:T(8,128)(2,1)}, bf16[656,128]{1,0:T(8,128)(2,1)S(1)}, u32[]{:S(2)}, u32[]{:S(2)}) collective-permute-start(bf16[656,128]{1,0:T(8,128)(2,1)} %get-tuple-element.40), channel_id=1, source_target_pairs={{0,20},{4,16},{8,28},{12,24},{16,4},{20,0},{24,12},{28,8},{1,21},{... | collective-permute-start | bytes 503816 | tf_op jit(solution)/shard_map/ppermute | solution.py:86
  17.2 0.0 copy-done.6
  17.2 0.1 pad.6.clone
  17.3 0.7 copy-done.7
  18.0 0.0 copy-done.8
  18.0 0.1 maximum_maximum_fusion
  18.0 0.0 collective-permute-done.refs_1_
  18.0 4.8 %collective-permute-start.5 = (bf16[656,128]{1,0:T(8,128)(2,1)}, bf16[656,128]{1,0:T(8,128)(2,1)S(1)}, u32[]{:S(2)}, u32[]{:S(2)}) collective-permute-start(bf16[656,128]{1,0:T(8,128)(2,1)} %get-tuple-element.41), channel_id=1, source_target_pairs={{0,16},{4,20},{8,24},{12,28},{16,0},{20,4},{24,8},{28,12},{1,17},{... | collective-permute-start | bytes 503816 | tf_op jit(solution)/shard_map/ppermute | solution.py:86
  22.8 0.0 collective-permute-done.1.refs_2_
  22.8 1.4 %collective-permute-start.6 = (bf16[656,128]{1,0:T(8,128)(2,1)}, bf16[656,128]{1,0:T(8,128)(2,1)S(1)}, u32[]{:S(2)}, u32[]{:S(2)}) collective-permute-start(bf16[656,128]{1,0:T(8,128)(2,1)} %get-tuple-element.42), channel_id=1, source_target_pairs={{0,4},{4,0},{8,12},{12,8},{16,20},{20,16},{24,28},{28,24},{1,5},{5... | collective-permute-start | bytes 503816 | tf_op jit(solution)/shard_map/ppermute | solution.py:86
  24.2 0.0 collective-permute-done.2.refs_3_
  24.2 0.7 collective-permute-start.7
  24.9 0.9 %broadcast_multiply_fusion.refs_0_ = bf16[656,128]{1,0:T(8,128)(2,1)S(1)} fusion(bf16[656,128]{1,0:T(8,128)(2,1)} %get-tuple-element.33, bf16[]{:T(256)} %bitcast.4), kind=kLoop, calls=%fused_computation | loop fusion | flops 83968 | bytes 335874 | tf_op jit(solution)/shard_map/mul | solution.py:629
  25.8 0.0 copy-start
  25.8 0.0 copy-start.1
  25.9 0.0 copy-start.2
  25.9 0.0 copy-start.3
  25.9 0.0 collective-permute-done.3.refs_4_
  25.9 9.3 %collective-permute-done.4.refs_5_ = bf16[656,128]{1,0:T(8,128)(2,1)S(1)} collective-permute-done((bf16[656,128]{1,0:T(8,128)(2,1)}, bf16[656,128]{1,0:T(8,128)(2,1)S(1)}, u32[]{:S(2)}, u32[]{:S(2)}) %collective-permute-start.4) | collective-permute-done | bytes 167968 | tf_op jit(solution)/shard_map/ppermute | solution.py:86
  35.1 2.8 %collective-permute-done.5.refs_6_ = bf16[656,128]{1,0:T(8,128)(2,1)S(1)} collective-permute-done((bf16[656,128]{1,0:T(8,128)(2,1)}, bf16[656,128]{1,0:T(8,128)(2,1)S(1)}, u32[]{:S(2)}, u32[]{:S(2)}) %collective-permute-start.5) | collective-permute-done | bytes 167968 | tf_op jit(solution)/shard_map/ppermute | solution.py:86
  37.9 0.0 collective-permute-done.6.refs_7_
  37.9 0.0 collective-permute-done.7.refs_10_
  37.9 0.0 copy-done.4
  37.9 0.0 copy-done.5
  37.9 7.9 %shard_map.146 = (bf16[416,128]{1,0:T(8,128)(2,1)S(1)}, bf16[416,128]{1,0:T(8,128)(2,1)S(1)}, bf16[416,128]{1,0:T(8,128)(2,1)S(1)}, bf16[416,128]{1,0:T(8,128)(2...) custom-call(bf16[656,128]{1,0:T(8,128)(2,1)S(1)} %broadcast_multiply, ...), custom_call_target="tpu_custom_call" | custom-call | tf_op jit(solution)/shard_map/pallas_call | solution.py:582
  45.8 2.5 %collective-permute-start.8 = (bf16[416,128]{1,0:T(8,128)(2,1)S(1)}, bf16[416,128]{1,0:T(8,128)(2,1)S(1)}, u32[]{:S(2)}, u32[]{:S(2)}) collective-permute-start(bf16[416,128]{1,0:T(8,128)(2,1)S(1)} %get-tuple-element.45), channel_id=1, source_target_pairs={{0,28},{4,24},{8,20},{12,16},{16,12},{20,8},{24,4},{28,0},{1,29},{... | collective-permute-start | bytes 319496 | tf_op jit(solution)/shard_map/ppermute | solution.py:86
  48.4 0.0 collective-permute-start.9
  48.4 2.8 %collective-permute-start.10 = (bf16[416,128]{1,0:T(8,128)(2,1)S(1)}, bf16[416,128]{1,0:T(8,128)(2,1)S(1)}, u32[]{:S(2)}, u32[]{:S(2)}) collective-permute-start(bf16[416,128]{1,0:T(8,128)(2,1)S(1)} %get-tuple-element.47), channel_id=1, source_target_pairs={{0,20},{4,16},{8,28},{12,24},{16,4},{20,0},{24,12},{28,8},{1,21},{... | collective-permute-start | bytes 319496 | tf_op jit(solution)/shard_map/ppermute | solution.py:86
  51.2 0.9 %collective-permute-start.11 = (bf16[416,128]{1,0:T(8,128)(2,1)S(1)}, bf16[416,128]{1,0:T(8,128)(2,1)S(1)}, u32[]{:S(2)}, u32[]{:S(2)}) collective-permute-start(bf16[416,128]{1,0:T(8,128)(2,1)S(1)} %get-tuple-element.48), channel_id=1, source_target_pairs={{0,16},{4,20},{8,24},{12,28},{16,0},{20,4},{24,8},{28,12},{1,17},{... | collective-permute-start | bytes 319496 | tf_op jit(solution)/shard_map/ppermute | solution.py:86
  52.1 2.1 %collective-permute-start.12 = (bf16[416,128]{1,0:T(8,128)(2,1)S(1)}, bf16[416,128]{1,0:T(8,128)(2,1)S(1)}, u32[]{:S(2)}, u32[]{:S(2)}) collective-permute-start(bf16[416,128]{1,0:T(8,128)(2,1)S(1)} %get-tuple-element.49), channel_id=1, source_target_pairs={{0,12},{4,8},{8,4},{12,0},{16,28},{20,24},{24,20},{28,16},{1,13},{... | collective-permute-start | bytes 319496 | tf_op jit(solution)/shard_map/ppermute | solution.py:86
  54.2 0.2 collective-permute-done.8.refs_1_
  54.5 2.5 %collective-permute-start.13 = (bf16[416,128]{1,0:T(8,128)(2,1)S(1)}, bf16[416,128]{1,0:T(8,128)(2,1)S(1)}, u32[]{:S(2)}, u32[]{:S(2)}) collective-permute-start(bf16[416,128]{1,0:T(8,128)(2,1)S(1)} %get-tuple-element.50), channel_id=1, source_target_pairs={{0,24},{4,28},{8,16},{12,20},{16,8},{20,12},{24,0},{28,4},{1,25},{... | collective-permute-start | bytes 319496 | tf_op jit(solution)/shard_map/ppermute | solution.py:86
  56.9 0.0 collective-permute-done.9.refs_2_
  56.9 1.0 %collective-permute-start.14 = (bf16[416,128]{1,0:T(8,128)(2,1)S(1)}, bf16[416,128]{1,0:T(8,128)(2,1)S(1)}, u32[]{:S(2)}, u32[]{:S(2)}) collective-permute-start(bf16[416,128]{1,0:T(8,128)(2,1)S(1)} %get-tuple-element.51), channel_id=1, source_target_pairs={{0,4},{4,0},{8,12},{12,8},{16,20},{20,16},{24,28},{28,24},{1,5},{5... | collective-permute-start | bytes 319496 | tf_op jit(solution)/shard_map/ppermute | solution.py:86
  57.9 3.6 %collective-permute-done.10.refs_3_ = bf16[416,128]{1,0:T(8,128)(2,1)S(1)} collective-permute-done((bf16[416,128]{1,0:T(8,128)(2,1)S(1)}, bf16[416,128]{1,0:T(8,128)(2,1)S(1)}, u32[]{:S(2)}, u32[]{:S(2)}) %collective-permute-start.10) | collective-permute-done | bytes 106528 | tf_op jit(solution)/shard_map/ppermute | solution.py:86
  61.5 3.5 %collective-permute-done.11.refs_4_ = bf16[416,128]{1,0:T(8,128)(2,1)S(1)} collective-permute-done((bf16[416,128]{1,0:T(8,128)(2,1)S(1)}, bf16[416,128]{1,0:T(8,128)(2,1)S(1)}, u32[]{:S(2)}, u32[]{:S(2)}) %collective-permute-start.11) | collective-permute-done | bytes 106528 | tf_op jit(solution)/shard_map/ppermute | solution.py:86
  65.0 0.0 collective-permute-done.12.refs_5_
  65.0 0.0 collective-permute-done.13.refs_6_
  65.0 0.0 collective-permute-done.14.refs_7_
  65.0 0.0 copy-done
  65.0 0.0 copy-done.1
  65.1 3.1 %shard_map.147 = (bf16[256,512]{1,0:T(8,128)(2,1)}, bf16[256,512]{1,0:T(8,128)(2,1)}, bf16[256,512]{1,0:T(8,128)(2,1)}, bf16[256,512]{1,0:T(8,128)(2,1)}, f32[25...) custom-call(bf16[416,128]{1,0:T(8,128)(2,1)S(1)} %get-tuple-element.44.refs_0_, ...), custom_call_target="tpu_custom_call" | custom-call | tf_op jit(solution)/shard_map/pallas_call | solution.py:293
  (8 shorter events, 0.0 us)
Async XLA Ops:
  2.9 15.1 %collective-permute-start = (bf16[656,128]{1,0:T(8,128)(2,1)}, bf16[656,128]{1,0:T(8,128)(2,1)S(1)}, u32[]{:S(2)}, u32[]{:S(2)}) collective-permute-start(bf16[656,128]{1,0:T(8,128)(2,1)} %get-tuple-element.34), channel_id=1, source_target_pairs={{0,28},{4,24},{8,20},{12,16},{16,12},{20,8},{24,4},{28,0},{1,29},{... | collective-permute-start | bytes 503816 | tf_op jit(solution)/shard_map/ppermute | solution.py:86
  8.9 8.2 %copy-start.6 = (f32[3,3,64]{2,1,0:T(4,128)S(1)}, f32[3,3,64]{2,1,0:T(4,128)}, u32[]{:S(2)}) copy-start(f32[3,3,64]{2,1,0:T(4,128)} %param.13) | copy-start | bytes 6916
  8.9 29.0 %copy-start.4 = (bf16[256,1536]{1,0:T(8,128)(2,1)S(1)}, bf16[256,1536]{1,0:T(8,128)(2,1)}, u32[]{:S(2)}) copy-start(bf16[256,1536]{1,0:T(8,128)(2,1)} %constant.12.clone.refs_9_) | copy-start | bytes 2359300
  9.0 29.0 %copy-start.5 = (bf16[512,768]{1,0:T(8,128)(2,1)S(1)}, bf16[512,768]{1,0:T(8,128)(2,1)}, u32[]{:S(2)}) copy-start(bf16[512,768]{1,0:T(8,128)(2,1)} %constant.4.clone.refs_8_) | copy-start | bytes 2359300
  9.0 13.9 %collective-permute-start.1 = (bf16[656,128]{1,0:T(8,128)(2,1)}, bf16[656,128]{1,0:T(8,128)(2,1)S(1)}, u32[]{:S(2)}, u32[]{:S(2)}) collective-permute-start(bf16[656,128]{1,0:T(8,128)(2,1)} %get-tuple-element.37), channel_id=1, source_target_pairs={{0,24},{4,28},{8,16},{12,20},{16,8},{20,12},{24,0},{28,4},{1,25},{... | collective-permute-start | bytes 503816 | tf_op jit(solution)/shard_map/ppermute | solution.py:86
  12.2 12.1 %collective-permute-start.2 = (bf16[656,128]{1,0:T(8,128)(2,1)}, bf16[656,128]{1,0:T(8,128)(2,1)S(1)}, u32[]{:S(2)}, u32[]{:S(2)}) collective-permute-start(bf16[656,128]{1,0:T(8,128)(2,1)} %get-tuple-element.38), channel_id=1, source_target_pairs={{0,12},{4,8},{8,4},{12,0},{16,28},{20,24},{24,20},{28,16},{1,13},{... | collective-permute-start | bytes 503816 | tf_op jit(solution)/shard_map/ppermute | solution.py:86
  12.3 13.6 %collective-permute-start.3 = (bf16[656,128]{1,0:T(8,128)(2,1)}, bf16[656,128]{1,0:T(8,128)(2,1)S(1)}, u32[]{:S(2)}, u32[]{:S(2)}) collective-permute-start(bf16[656,128]{1,0:T(8,128)(2,1)} %get-tuple-element.39), channel_id=1, source_target_pairs={{0,8},{4,12},{8,0},{12,4},{16,24},{20,28},{24,16},{28,20},{1,9},{5... | collective-permute-start | bytes 503816 | tf_op jit(solution)/shard_map/ppermute | solution.py:86
  14.1 21.0 %collective-permute-start.4 = (bf16[656,128]{1,0:T(8,128)(2,1)}, bf16[656,128]{1,0:T(8,128)(2,1)S(1)}, u32[]{:S(2)}, u32[]{:S(2)}) collective-permute-start(bf16[656,128]{1,0:T(8,128)(2,1)} %get-tuple-element.40), channel_id=1, source_target_pairs={{0,20},{4,16},{8,28},{12,24},{16,4},{20,0},{24,12},{28,8},{1,21},{... | collective-permute-start | bytes 503816 | tf_op jit(solution)/shard_map/ppermute | solution.py:86
  17.3 0.7 %copy-start.7 = (f32[3,64]{1,0:T(4,128)S(1)}, f32[3,64]{1,0:T(4,128)}, u32[]{:S(2)}) copy-start(f32[3,64]{1,0:T(4,128)} %constant.5.clone.1) | copy-start | bytes 2308
  17.3 0.7 %copy-start.8 = (f32[64]{0:T(128)S(1)}, f32[64]{0:T(128)}, u32[]{:S(2)}) copy-start(f32[64]{0:T(128)} %param.14) | copy-start | bytes 772
  18.0 19.9 %collective-permute-start.5 = (bf16[656,128]{1,0:T(8,128)(2,1)}, bf16[656,128]{1,0:T(8,128)(2,1)S(1)}, u32[]{:S(2)}, u32[]{:S(2)}) collective-permute-start(bf16[656,128]{1,0:T(8,128)(2,1)} %get-tuple-element.41), channel_id=1, source_target_pairs={{0,16},{4,20},{8,24},{12,28},{16,0},{20,4},{24,8},{28,12},{1,17},{... | collective-permute-start | bytes 503816 | tf_op jit(solution)/shard_map/ppermute | solution.py:86
  22.8 15.1 %collective-permute-start.6 = (bf16[656,128]{1,0:T(8,128)(2,1)}, bf16[656,128]{1,0:T(8,128)(2,1)S(1)}, u32[]{:S(2)}, u32[]{:S(2)}) collective-permute-start(bf16[656,128]{1,0:T(8,128)(2,1)} %get-tuple-element.42), channel_id=1, source_target_pairs={{0,4},{4,0},{8,12},{12,8},{16,20},{20,16},{24,28},{28,24},{1,5},{5... | collective-permute-start | bytes 503816 | tf_op jit(solution)/shard_map/ppermute | solution.py:86
  24.2 13.7 %collective-permute-start.7 = (f32[8,128]{1,0:T(8,128)S(1)}, f32[8,128]{1,0:T(8,128)S(1)}, u32[]{:S(2)}, u32[]{:S(2)}) collective-permute-start(f32[8,128]{1,0:T(8,128)S(1)} %maximum_maximum_fusion), channel_id=1, source_target_pairs={{0,0},{1,4},{2,8},{3,12},{4,16},{5,20},{6,24},{7,28},{8,1},{9,5},{... | collective-permute-start | bytes 12296 | tf_op jit(solution)/shard_map/ppermute | solution.py:630
  25.8 39.2 %copy-start = (bf16[256,512]{1,0:T(8,128)(2,1)S(1)}, bf16[256,512]{1,0:T(8,128)(2,1)}, u32[]{:S(2)}) copy-start(bf16[256,512]{1,0:T(8,128)(2,1)} %refs_8_.2) | copy-start | bytes 786436
  25.8 39.2 %copy-start.1 = (bf16[256,512]{1,0:T(8,128)(2,1)S(1)}, bf16[256,512]{1,0:T(8,128)(2,1)}, u32[]{:S(2)}) copy-start(bf16[256,512]{1,0:T(8,128)(2,1)} %refs_9_.2) | copy-start | bytes 786436
  25.9 39.2 %copy-start.2 = (bf16[256,512]{1,0:T(8,128)(2,1)S(1)}, bf16[256,512]{1,0:T(8,128)(2,1)}, u32[]{:S(2)}) copy-start(bf16[256,512]{1,0:T(8,128)(2,1)} %refs_10_.1) | copy-start | bytes 786436
  25.9 39.2 %copy-start.3 = (bf16[256,512]{1,0:T(8,128)(2,1)S(1)}, bf16[256,512]{1,0:T(8,128)(2,1)}, u32[]{:S(2)}) copy-start(bf16[256,512]{1,0:T(8,128)(2,1)} %refs_11_.1) | copy-start | bytes 786436
  45.8 8.6 %collective-permute-start.8 = (bf16[416,128]{1,0:T(8,128)(2,1)S(1)}, bf16[416,128]{1,0:T(8,128)(2,1)S(1)}, u32[]{:S(2)}, u32[]{:S(2)}) collective-permute-start(bf16[416,128]{1,0:T(8,128)(2,1)S(1)} %get-tuple-element.45), channel_id=1, source_target_pairs={{0,28},{4,24},{8,20},{12,16},{16,12},{20,8},{24,4},{28,0},{1,29},{... | collective-permute-start | bytes 319496 | tf_op jit(solution)/shard_map/ppermute | solution.py:86
  48.4 8.6 %collective-permute-start.9 = (bf16[416,128]{1,0:T(8,128)(2,1)S(1)}, bf16[416,128]{1,0:T(8,128)(2,1)S(1)}, u32[]{:S(2)}, u32[]{:S(2)}) collective-permute-start(bf16[416,128]{1,0:T(8,128)(2,1)S(1)} %get-tuple-element.46), channel_id=1, source_target_pairs={{0,8},{4,12},{8,0},{12,4},{16,24},{20,28},{24,16},{28,20},{1,9},{5... | collective-permute-start | bytes 319496 | tf_op jit(solution)/shard_map/ppermute | solution.py:86
  48.4 13.1 %collective-permute-start.10 = (bf16[416,128]{1,0:T(8,128)(2,1)S(1)}, bf16[416,128]{1,0:T(8,128)(2,1)S(1)}, u32[]{:S(2)}, u32[]{:S(2)}) collective-permute-start(bf16[416,128]{1,0:T(8,128)(2,1)S(1)} %get-tuple-element.47), channel_id=1, source_target_pairs={{0,20},{4,16},{8,28},{12,24},{16,4},{20,0},{24,12},{28,8},{1,21},{... | collective-permute-start | bytes 319496 | tf_op jit(solution)/shard_map/ppermute | solution.py:86
  51.2 13.8 %collective-permute-start.11 = (bf16[416,128]{1,0:T(8,128)(2,1)S(1)}, bf16[416,128]{1,0:T(8,128)(2,1)S(1)}, u32[]{:S(2)}, u32[]{:S(2)}) collective-permute-start(bf16[416,128]{1,0:T(8,128)(2,1)S(1)} %get-tuple-element.48), channel_id=1, source_target_pairs={{0,16},{4,20},{8,24},{12,28},{16,0},{20,4},{24,8},{28,12},{1,17},{... | collective-permute-start | bytes 319496 | tf_op jit(solution)/shard_map/ppermute | solution.py:86
  52.1 12.9 %collective-permute-start.12 = (bf16[416,128]{1,0:T(8,128)(2,1)S(1)}, bf16[416,128]{1,0:T(8,128)(2,1)S(1)}, u32[]{:S(2)}, u32[]{:S(2)}) collective-permute-start(bf16[416,128]{1,0:T(8,128)(2,1)S(1)} %get-tuple-element.49), channel_id=1, source_target_pairs={{0,12},{4,8},{8,4},{12,0},{16,28},{20,24},{24,20},{28,16},{1,13},{... | collective-permute-start | bytes 319496 | tf_op jit(solution)/shard_map/ppermute | solution.py:86
  54.5 10.6 %collective-permute-start.13 = (bf16[416,128]{1,0:T(8,128)(2,1)S(1)}, bf16[416,128]{1,0:T(8,128)(2,1)S(1)}, u32[]{:S(2)}, u32[]{:S(2)}) collective-permute-start(bf16[416,128]{1,0:T(8,128)(2,1)S(1)} %get-tuple-element.50), channel_id=1, source_target_pairs={{0,24},{4,28},{8,16},{12,20},{16,8},{20,12},{24,0},{28,4},{1,25},{... | collective-permute-start | bytes 319496 | tf_op jit(solution)/shard_map/ppermute | solution.py:86
  56.9 8.1 %collective-permute-start.14 = (bf16[416,128]{1,0:T(8,128)(2,1)S(1)}, bf16[416,128]{1,0:T(8,128)(2,1)S(1)}, u32[]{:S(2)}, u32[]{:S(2)}) collective-permute-start(bf16[416,128]{1,0:T(8,128)(2,1)S(1)} %get-tuple-element.51), channel_id=1, source_target_pairs={{0,4},{4,0},{8,12},{12,8},{16,20},{20,16},{24,28},{28,24},{1,5},{5... | collective-permute-start | bytes 319496 | tf_op jit(solution)/shard_map/ppermute | solution.py:86
